TPU v7x, 32 devices: a whole 2x2x4 slice. The times are simulated.
32 devices in a mesh: gx: 8 (over y, x, core), gy: 4 (over z).
Axes of the slice: x: 2, y: 2, z: 4, core: 2. Of those that a mesh axis runs over, the one named last changes fastest.
Arguments:
- fractions: float32 [3, 16384], P(None, ('gx', 'gy')), may hold values from 0 to 1
- species: int32 [16384], P(('gx', 'gy')), may hold values from 0 to 5
- send_list: int32 [8, 512], P(None, ('gx', 'gy')), may hold values from 0 to 511
- tile_list: int32 [2, 192], P(None, ('gx', 'gy')), may hold values from 0 to 9, as said below
- counts: int32 [32], P(('gx', 'gy')), may hold values from 2 to 6, as said below
- embedding: float32 [6, 128], replicated, may hold values from -6 to 6
- radial: float32 [4, 8, 128], replicated, may hold values from -0.75 to 0.75
- mixing: float32 [5, 128, 128], replicated, may hold values from -0.5 to 0.5
- readout: float32 [128], replicated, may hold values from -0.5 to 0.5
Outputs:
- atom_energy: float32 [16384], P(('gx', 'gy'))
- forces: float32 [3, 16384], P(None, ('gx', 'gy'))
Inputs may be any that keep to these rules, and one draw needn't show every extreme that they name: `tile_list`: row 0 of each slot names one of the device's own 8 blocks, row 1 a block of its node list (8 own blocks, then 2 ghost blocks); slot k < 2 of every device names ghost block 8 + k. The first counts slots of a device are live, the rest are ignored.
All inputs are finite; a program needn't handle non-finite values.
Results may differ from a plain program's by a relative error of at most 0.0003.
Values sent between devices are 32-bit elements; how exact they have to be, the bound alone decides.
No kernel may reach another device: no remote copies, remote signals or barrier semaphores. Data moves between devices by JAX's collectives and lax.ppermute only.
A program may use at most 64 MiB of HBM per device.

v0:
```python
import functools

import jax
import jax.numpy as jnp
from jax import lax
from jax.experimental import pallas as pl
from jax.experimental.pallas import tpu as pltpu
from jax.sharding import PartitionSpec as P

F32 = jnp.float32
BF16 = jnp.bfloat16

BASIS = 8
BLOCK = 64
GHOSTS = 16
SPAN = 8
HIST = BASIS * 4 * SPAN
OFFSETS = ((-1, -1), (-1, 0), (-1, 1), (0, -1), (0, 1), (1, -1), (1, 0), (1, 1))
WIDTHS = (12.0, 12.0, 36.0)
CUT_INV = 1.0 / 25.0
ROOT = 1.6986436005760381
CENTERS = tuple(1.0 + 0.6 * n for n in range(BASIS))
ROWS = 32

VMEM = pl.BlockSpec(memory_space=pltpu.VMEM)
SMEM = pl.BlockSpec(memory_space=pltpu.SMEM)
PARAMS = pltpu.CompilerParams(vmem_limit_bytes=48 * 1024 * 1024)

ROWROW = (((1,), (1,)), ((), ()))
ROWCOL = (((1,), (0,)), ((), ()))


def split(value):
    high = value.astype(BF16)
    return high, (value - high.astype(F32)).astype(BF16)


def mm(left, right, dims=ROWCOL):
    return lax.dot_general(left, right, dims, preferred_element_type=F32)


def mm3(left, right, dims=ROWCOL):
    (lh, ll), (rh, rl) = left, right
    return mm(lh, rh, dims) + mm(ll, rh, dims) + mm(lh, rl, dims)


def sigmoid(value):
    return 1.0 / (1.0 + jnp.exp(-value))


def iota(shape, dim):
    return lax.broadcasted_iota(jnp.int32, shape, dim)


def low_half():
    return iota((1, 128), 1) < BLOCK


def pick_rows(even_x, even_y, mate, far, zmate, zfar):
    x_up, x_down = jnp.where(even_x, mate, far), jnp.where(even_x, far, mate)
    y_up = [jnp.where(even_y, zmate[i], zfar[i]) for i in range(3)]
    y_down = [jnp.where(even_y, zfar[i], zmate[i]) for i in range(3)]
    sources = {
        (1, 0): x_up,
        (-1, 0): x_down,
        (0, 1): y_up[0],
        (0, -1): y_down[0],
        (1, 1): jnp.where(even_x, y_up[1], y_up[2]),
        (-1, 1): jnp.where(even_x, y_up[2], y_up[1]),
        (1, -1): jnp.where(even_x, y_down[1], y_down[2]),
        (-1, -1): jnp.where(even_x, y_down[2], y_down[1]),
    }
    slot_of = iota((8, 128), 1) // GHOSTS
    total = jnp.zeros((8, 128), F32)
    for slot, offset in enumerate(OFFSETS):
        turned = pltpu.roll(sources[offset], ((2 * slot - 7) * GHOSTS) % 128, 1)
        total = jnp.where(slot_of == slot, turned, total)
    return total


def pick_slot(slot, even_x, even_y, mate, far, zmate, zfar):
    along_x, along_y = OFFSETS[slot]
    if along_y == 0:
        near = even_x if along_x == 1 else jnp.logical_not(even_x)
        return jnp.where(near, mate[1], far[1])
    near = even_y if along_y == 1 else jnp.logical_not(even_y)
    if along_x == 0:
        return jnp.where(near, zmate[2], zfar[2])
    first = even_x if along_x == 1 else jnp.logical_not(even_x)
    return jnp.where(
        near, jnp.where(first, zmate[0], zmate[1]), jnp.where(first, zfar[0], zfar[1])
    )


def pick_all(args):
    return jnp.concatenate([pick_slot(slot, *args) for slot in range(8)], axis=0)


def put_packets(even_x, piece, mate_ref, far_ref, side_ref):
    for part in range(3):
        down, up = piece(part), piece(5 + part)
        mate_ref[part] = jnp.where(even_x, up, down)
        far_ref[part] = jnp.where(even_x, down, up)
    side_ref[0] = piece(3)
    side_ref[1] = piece(4)


def send_columns(send):
    wide = jnp.concatenate([send] * 8, axis=1)
    own = iota((8, 128), 1) // GHOSTS == iota((8, 128), 0)
    return jnp.sum(jnp.where(own, wide, 0), axis=0, keepdims=True)


def chooser(send, atoms):
    return iota((atoms, 128), 0) == send_columns(send)


def separation(col_ref, row_ref, col_block, row_block, start, sign):
    base = pl.multiple_of(col_block * BLOCK, BLOCK)
    mine = col_ref[pl.ds(base + start, ROWS), :]
    other = row_ref[row_block]
    return [sign * (other[a : a + 1, :] - mine[:, a : a + 1]) for a in range(3)]


def envelope(parts, same, start):
    dist_sq = parts[0] * parts[0] + parts[1] * parts[1] + parts[2] * parts[2]
    soft = jnp.sqrt(dist_sq + 1.0)
    rows = iota((ROWS, 128), 0) + start
    columns = iota((ROWS, 128), 1) % BLOCK
    apart = jnp.where(jnp.logical_and(rows == columns, same), 0.0, 1.0)
    margin = jnp.maximum(1.0 - dist_sq * CUT_INV, 0.0) * apart
    return soft, margin


def angular(parts, inverse):
    u = [part * inverse for part in parts]
    low = low_half()
    return jnp.where(low, 1.0, u[0]), jnp.where(low, u[1], u[2])


def pair_forward(col_ref, row_ref, left, right, high_ref, low_ref):
    for start in range(0, BLOCK, ROWS):
        parts = separation(col_ref, row_ref, left, right, start, 1.0)
        soft, margin = envelope(parts, left == right, start)
        first, second = angular(parts, 1.0 / soft)
        weight = margin * margin
        first, second = first * weight, second * weight
        scaled = soft * ROOT
        for n in range(BASIS):
            shift = scaled - ROOT * CENTERS[n]
            bell = jnp.exp2(-(shift * shift))
            here = pl.ds(n * BLOCK + start, ROWS)
            for half, factor in enumerate((first, second)):
                high, low = split(bell * factor)
                high_ref[here, half * 128 : half * 128 + 128] = high
                low_ref[here, half * 128 : half * 128 + 128] = low


def pair_swapped(col_ref, row_ref, left, right, high_ref, low_ref):
    low_lanes = low_half()
    for start in range(0, BLOCK, ROWS):
        parts = separation(col_ref, row_ref, right, left, start, -1.0)
        soft, margin = envelope(parts, left == right, start)
        inverse = 1.0 / soft
        weight = margin * margin
        factors = [weight] + [weight * (part * inverse) for part in parts]
        scaled = soft * ROOT
        for pair in range(BASIS // 2):
            center = jnp.where(low_lanes, ROOT * CENTERS[2 * pair], ROOT * CENTERS[2 * pair + 1])
            shift = scaled - center
            bell = jnp.exp2(-(shift * shift))
            for order in range(4):
                high, low = split(bell * factors[order])
                here = pl.ds(order * BLOCK + start, ROWS)
                high_ref[here, pair * 128 : pair * 128 + 128] = high
                low_ref[here, pair * 128 : pair * 128 + 128] = low


def pair_backward(col_ref, row_ref, left, right, pull_ref, grad_row, grad_col):
    low_lanes = low_half()
    lane = iota((1, 128), 1)
    sums = [jnp.zeros((1, 128), F32) for _ in range(3)]
    for start in range(0, BLOCK, ROWS):
        parts = separation(col_ref, row_ref, left, right, start, 1.0)
        soft, margin = envelope(parts, left == right, start)
        inverse = 1.0 / soft
        first, second = angular(parts, inverse)
        scaled = soft * ROOT
        by_bell = jnp.zeros((ROWS, 128), F32)
        by_shift = jnp.zeros((ROWS, 128), F32)
        by_first = jnp.zeros((ROWS, 128), F32)
        by_second = jnp.zeros((ROWS, 128), F32)
        for n in range(BASIS):
            shift = scaled - ROOT * CENTERS[n]
            bell = jnp.exp2(-(shift * shift))
            here = pl.ds(n * BLOCK + start, ROWS)
            pull_first, pull_second = pull_ref[here, 0:128], pull_ref[here, 128:256]
            both = bell * (first * pull_first + second * pull_second)
            by_bell = by_bell + both
            by_shift = by_shift + shift * both
            by_first = by_first + bell * pull_first
            by_second = by_second + bell * pull_second
        weight = margin * margin
        by_bell = by_bell + pltpu.roll(by_bell, BLOCK, 1)
        by_shift = (by_shift + pltpu.roll(by_shift, BLOCK, 1)) * weight
        by_first, by_second = by_first * weight, by_second * weight
        turned = pltpu.roll(by_second, BLOCK, 1)
        by_u = [
            jnp.where(low_lanes, pltpu.roll(by_first, BLOCK, 1), by_first),
            jnp.where(low_lanes, by_second, turned),
            jnp.where(low_lanes, turned, by_second),
        ]
        along = (by_u[0] * parts[0] + by_u[1] * parts[1] + by_u[2] * parts[2]) * inverse
        by_soft = by_shift * (-4.0 / ROOT) - along * inverse
        radial_part = by_soft * inverse + by_bell * (margin * (-4.0 * CUT_INV))
        column = jnp.zeros((ROWS, 128), F32)
        for a in range(3):
            force = by_u[a] * inverse + parts[a] * radial_part
            sums[a] = sums[a] + jnp.sum(force, axis=0, keepdims=True)
            total = jnp.sum(jnp.where(low_lanes, force, 0.0), axis=1, keepdims=True)
            column = jnp.where(lane == a, total, column)
        base = pl.multiple_of(left * BLOCK, BLOCK)
        grad_col[pl.ds(base + start, ROWS), :] -= column
    grad_row[right] += jnp.concatenate(sums + [jnp.zeros((5, 128), F32)], axis=0)


def kind_table(col_ref, block):
    base = pl.multiple_of(block * BLOCK, BLOCK)
    kind = col_ref[pl.ds(base, BLOCK), 3:4].astype(jnp.int32)
    lane = iota((BLOCK, 128), 1)
    hit = kind == lane % SPAN
    return jnp.concatenate(
        [
            jnp.where(jnp.logical_and(hit, lane // SPAN % 4 == order), 1.0, 0.0)
            for order in range(4)
        ],
        axis=0,
    ).astype(BF16)


def pack_kernel(frac_ref, kind_ref, send_ref, site_ref, out_ref):
    atoms = frac_ref.shape[1]
    rows = jnp.concatenate(
        [frac_ref[...], kind_ref[...].astype(F32), jnp.zeros((4, atoms), F32)], axis=0
    )
    site_ref[...] = rows
    out_ref[...] = exact_pick(rows, chooser(send_ref[...], atoms), ROWCOL)


def exact_pick(rows, chosen, dims):
    high = rows.astype(BF16).astype(F32)
    rest = rows - high
    middle = rest.astype(BF16).astype(F32)
    stacked = jnp.concatenate(
        [high, middle, rest - middle, jnp.zeros_like(rows)], axis=0
    ).astype(BF16)
    picked = mm(stacked, chosen.astype(F32).astype(BF16), dims)
    return picked[0:8] + picked[8:16] + picked[16:24]


def doubled(rows, block):
    chunk = rows[:, block // 2 * 128 : block // 2 * 128 + 128]
    turned = pltpu.roll(chunk, BLOCK, 1)
    low = low_half()
    return jnp.where(low, chunk, turned) if block % 2 == 0 else jnp.where(low, turned, chunk)


def upright(rows):
    return jnp.concatenate([rows, jnp.zeros((120, rows.shape[1]), F32)], axis=0).T


def first_kernel(
    tile_ref,
    count_ref,
    even_ref,
    send_ref,
    site_ref,
    mate_in,
    far_in,
    zmate_in,
    zfar_in,
    embed_ref,
    radial_ref,
    mixing_ref,
    hist_ref,
    mate_ref,
    far_ref,
    side_ref,
    col_ref,
    row_ref,
    fold_high,
    fold_low,
    fold_ref,
    high_ref,
    low_ref,
):
    atoms = site_ref.shape[1]
    blocks = atoms // BLOCK
    even_x, even_y = even_ref[0] == 0, even_ref[1] == 0
    ghosts = pick_rows(even_x, even_y, mate_in[...], far_in[...], zmate_in[...], zfar_in[...])
    row = iota((8, 128), 0)
    slot = iota((8, 128), 1) // GHOSTS
    shift_x = jnp.where(slot < 3, -1.0, jnp.where(slot < 5, 0.0, 1.0))
    down = (slot == 0) | (slot == 3) | (slot == 5)
    level = (slot == 1) | (slot == 6)
    shift_y = jnp.where(down, -1.0, jnp.where(level, 0.0, 1.0))
    shift = jnp.where(row == 0, shift_x, jnp.where(row == 1, shift_y, 0.0))
    scale = jnp.where(row < 2, WIDTHS[0], jnp.where(row == 2, WIDTHS[2], 1.0))
    ghosts = (ghosts + shift) * scale
    own = site_ref[...] * scale[:, 0:1]
    col_ref[0:atoms, :] = upright(own)
    col_ref[atoms : atoms + 128, :] = upright(ghosts)
    for block in range(blocks):
        row_ref[block] = doubled(own, block)
    for block in range(2):
        row_ref[blocks + block] = doubled(ghosts, block)
    hist_ref[...] = jnp.zeros_like(hist_ref)

    embed = jnp.concatenate([embed_ref[...], jnp.zeros((SPAN - embed_ref.shape[0], 128), F32)], axis=0)
    scalar = jnp.concatenate([radial_ref[0, n : n + 1, :] * embed for n in range(BASIS)], axis=0)
    vector = jnp.concatenate([radial_ref[1, n : n + 1, :] * embed for n in range(BASIS)], axis=0)
    scalar, vector = split(scalar), split(vector)
    to_self = mm3(scalar, split(mixing_ref[0]))
    to_gate = mm3(scalar, split(mixing_ref[2]))
    to_vector = mm3(vector, split(mixing_ref[1]))
    fold_ref[...] = jnp.zeros_like(fold_ref)
    for n in range(BASIS):
        rows = slice(n * SPAN, n * SPAN + SPAN)
        base = n * 4 * SPAN
        fold_ref[base : base + SPAN, 0:128] = to_self[rows]
        fold_ref[base : base + SPAN, 128:256] = to_gate[rows]
        for a in range(3):
            here = base + (a + 1) * SPAN
            fold_ref[here : here + SPAN, (a + 2) * 128 : (a + 3) * 128] = to_vector[rows]
    fold = split(fold_ref[...])
    fold_high[...] = fold[0]
    fold_low[...] = fold[1]

    lane_basis = iota((1, 128), 1) // (4 * SPAN)

    def tile(slot_index, carried):
        left, right = tile_ref[0, slot_index], tile_ref[1, slot_index]
        pair_forward(col_ref, row_ref, left, right, high_ref, low_ref)
        table = kind_table(col_ref, right)
        found = mm(high_ref[...], table) + mm(low_ref[...], table)
        base = pl.multiple_of(left * BLOCK, BLOCK)
        for half in range(2):
            total = jnp.zeros((BLOCK, 128), F32)
            for n in range(4):
                begin = (half * 4 + n) * BLOCK
                total = jnp.where(lane_basis == n, found[begin : begin + BLOCK], total)
            hist_ref[pl.ds(base, BLOCK), half * 128 : half * 128 + 128] += total
        return carried

    lax.fori_loop(0, count_ref[0], tile, 0)

    def piece(slot):
        return jnp.concatenate(
            [hist_ref[pl.ds(send_ref[slot, entry], 1), :] for entry in range(GHOSTS)], axis=0
        )

    put_packets(even_x, piece, mate_ref, far_ref, side_ref)


def second_kernel(
    tile_ref,
    count_ref,
    even_ref,
    hist_ref,
    mate_in,
    far_in,
    zmate_in,
    zfar_in,
    col_ref,
    row_ref,
    fold_high,
    fold_low,
    embed_ref,
    radial_ref,
    mixing_ref,
    readout_ref,
    energy_ref,
    mate_ref,
    far_ref,
    side_ref,
    pull_hist_ref,
    grad_row,
    grad_col,
    pre_ref,
    feat_high,
    feat_low,
    scalar_ref,
    high_ref,
    low_ref,
    message_ref,
    direct_ref,
    pull_message,
    grad_feat,
    swap_high,
    swap_low,
    pull_ref,
):
    atoms = hist_ref.shape[0]
    nodes = atoms + 8 * GHOSTS
    blocks = nodes // BLOCK
    even_x, even_y = even_ref[0] == 0, even_ref[1] == 0
    fold = (fold_high[...], fold_low[...])
    ghost_hist = pick_all((even_x, even_y, mate_in, far_in, zmate_in, zfar_in))
    pre_ref[0:atoms, :] = mm3(split(hist_ref[...]), fold)
    pre_ref[atoms:nodes, :] = mm3(split(ghost_hist), fold)

    def gate_of(rows):
        return sigmoid(pre_ref[rows, 128:256])

    def make_features(block, carried):
        base = pl.multiple_of(block * BLOCK, BLOCK)
        rows = pl.ds(base, BLOCK)
        kind = col_ref[rows, 3:4].astype(jnp.int32)
        scalar = jnp.zeros((BLOCK, 128), F32)
        for species in range(embed_ref.shape[0]):
            scalar = jnp.where(kind == species, embed_ref[species : species + 1, :], scalar)
        pre = pre_ref[rows, 0:128]
        scalar = scalar + pre * sigmoid(pre)
        scalar_ref[rows, :] = scalar
        gate = gate_of(rows)
        parts = [scalar] + [
            pre_ref[rows, (a + 2) * 128 : (a + 3) * 128] * gate for a in range(3)
        ]
        empty = jnp.zeros((BLOCK, 128), BF16)
        for order, part in enumerate(parts):
            high, low = split(part)
            here = pl.ds(order * BLOCK, BLOCK)
            used = 0 if order == 0 else 128
            for ref, value in ((feat_high, high), (feat_low, low)):
                ref[block, here, used : used + 128] = value
                ref[block, here, 128 - used : 256 - used] = empty
        return carried

    lax.fori_loop(0, blocks, make_features, 0)

    message_ref[...] = jnp.zeros_like(message_ref)

    def forward(slot_index, carried):
        left, right = tile_ref[0, slot_index], tile_ref[1, slot_index]
        pair_forward(col_ref, row_ref, left, right, high_ref, low_ref)
        found = mm3((high_ref[...], low_ref[...]), (feat_high[right], feat_low[right]))
        total = jnp.zeros((BLOCK, 128), F32)
        for n in range(BASIS):
            rows = slice(n * BLOCK, n * BLOCK + BLOCK)
            total = total + found[rows, 0:128] * radial_ref[2, n : n + 1, :]
            total = total + found[rows, 128:256] * radial_ref[3, n : n + 1, :]
        message_ref[pl.ds(pl.multiple_of(left * BLOCK, BLOCK), BLOCK), :] += total
        return carried

    lax.fori_loop(0, count_ref[0], forward, 0)

    mix_message, mix_hidden = split(mixing_ref[3]), split(mixing_ref[4])
    mixed = mm3(split(message_ref[...]), mix_message)
    mixed_gate = sigmoid(mixed)
    final = scalar_ref[0:atoms, :] + mixed * mixed_gate
    hidden = mm3(split(final), mix_hidden)
    hidden_gate = sigmoid(hidden)
    readout = readout_ref[...]
    energy_ref[...] = mm3(split(jnp.broadcast_to(readout, (8, 128))), split(hidden * hidden_gate), ROWROW)[0:1]
    pull_hidden = readout * (hidden_gate * (1.0 + hidden * (1.0 - hidden_gate)))
    pull_final = mm3(split(pull_hidden), mix_hidden, ROWROW)
    direct_ref[...] = pull_final
    pull_mixed = pull_final * (mixed_gate * (1.0 + mixed * (1.0 - mixed_gate)))
    pull_message[...] = mm3(split(pull_mixed), mix_message, ROWROW)

    grad_feat[...] = jnp.zeros_like(grad_feat)
    grad_row[...] = jnp.zeros_like(grad_row)
    grad_col[...] = jnp.zeros_like(grad_col)

    def backward(slot_index, carried):
        left, right = tile_ref[0, slot_index], tile_ref[1, slot_index]
        cotangent = pull_message[pl.ds(pl.multiple_of(left * BLOCK, BLOCK), BLOCK), :]
        weighted = [
            split(
                jnp.concatenate(
                    [cotangent * radial_ref[path, n : n + 1, :] for n in range(BASIS)], axis=0
                )
            )
            for path in (2, 3)
        ]
        pair_swapped(col_ref, row_ref, left, right, swap_high, swap_low)
        to_scalar = mm3((swap_high[0:BLOCK, :], swap_low[0:BLOCK, :]), weighted[0])
        to_vector = mm3((swap_high[BLOCK:, :], swap_low[BLOCK:, :]), weighted[1])
        rows = pl.ds(pl.multiple_of(right * BLOCK, BLOCK), BLOCK)
        grad_feat[rows, 0:128] += to_scalar
        for a in range(3):
            grad_feat[rows, (a + 1) * 128 : (a + 2) * 128] += to_vector[a * BLOCK : (a + 1) * BLOCK]
        both = [
            jnp.concatenate([weighted[0][part], weighted[1][part]], axis=1) for part in range(2)
        ]
        pull_ref[...] = mm3(both, (feat_high[right], feat_low[right]), ROWROW)
        pair_backward(col_ref, row_ref, left, right, pull_ref, grad_row, grad_col)
        return carried

    lax.fori_loop(0, count_ref[0], backward, 0)

    def pull_features(rows, with_direct):
        by_scalar = grad_feat[rows, 0:128]
        if with_direct:
            by_scalar = by_scalar + direct_ref[rows, :]
        pre = pre_ref[rows, 0:128]
        own_gate = sigmoid(pre)
        gate = gate_of(rows)
        by_gate = jnp.zeros_like(gate)
        by_vector = []
        for a in range(3):
            pulled = grad_feat[rows, (a + 1) * 128 : (a + 2) * 128]
            by_gate = by_gate + pulled * pre_ref[rows, (a + 2) * 128 : (a + 3) * 128]
            by_vector.append(pulled * gate)
        by_pre = by_scalar * (own_gate * (1.0 + pre * (1.0 - own_gate)))
        return jnp.concatenate([by_pre, by_gate * gate * (1.0 - gate)] + by_vector, axis=1)

    ghost_pull = mm3(split(pull_features(slice(atoms, nodes), False)), fold, ROWROW)
    put_packets(
        even_x,
        lambda slot: ghost_pull[slot * GHOSTS : slot * GHOSTS + GHOSTS],
        mate_ref,
        far_ref,
        side_ref,
    )
    pull_hist_ref[...] = mm3(split(pull_features(slice(0, atoms), True)), fold, ROWROW)


def third_kernel(
    tile_ref,
    count_ref,
    even_ref,
    send_ref,
    pull_hist_ref,
    mate_in,
    far_in,
    zmate_in,
    zfar_in,
    col_ref,
    row_ref,
    grad_row_in,
    grad_col_in,
    own_ref,
    out_ref,
    total_ref,
    grad_row,
    grad_col,
    pull_ref,
):
    atoms = pull_hist_ref.shape[0]
    blocks = atoms // BLOCK
    even_x, even_y = even_ref[0] == 0, even_ref[1] == 0
    returned = split(pick_all((even_x, even_y, mate_in, far_in, zmate_in, zfar_in)))
    chosen = chooser(send_ref[...], atoms).astype(F32).astype(BF16)
    total_ref[...] = pull_hist_ref[...] + mm(chosen, returned[0]) + mm(chosen, returned[1])
    grad_row[...] = grad_row_in[...]
    grad_col[...] = grad_col_in[...]
    lane_basis = iota((1, 128), 1) // (4 * SPAN)

    def tile(slot_index, carried):
        left, right = tile_ref[0, slot_index], tile_ref[1, slot_index]
        rows = pl.ds(pl.multiple_of(left * BLOCK, BLOCK), BLOCK)
        parts = []
        for half in range(2):
            here = total_ref[rows, half * 128 : half * 128 + 128]
            parts += [jnp.where(lane_basis == n, here, 0.0) for n in range(4)]
        high, low = split(jnp.concatenate(parts, axis=0))
        table = kind_table(col_ref, right)
        pull_ref[...] = mm(high, table, ROWROW) + mm(low, table, ROWROW)
        pair_backward(col_ref, row_ref, left, right, pull_ref, grad_row, grad_col)
        return carried

    lax.fori_loop(0, count_ref[0], tile, 0)

    low = low_half()
    out_ref[...] = jnp.where(low, grad_row[blocks], grad_row[blocks + 1])
    by_sender = jnp.concatenate(
        [jnp.where(low, grad_row[2 * k], grad_row[2 * k + 1]) for k in range(blocks // 2)], axis=1
    )
    own_ref[...] = by_sender + grad_col[...].T[0:8]


def last_kernel(even_ref, send_ref, own_ref, mate_in, far_in, zmate_in, zfar_in, force_ref):
    atoms = own_ref.shape[1]
    even_x, even_y = even_ref[0] == 0, even_ref[1] == 0
    returned = pick_rows(even_x, even_y, mate_in[...], far_in[...], zmate_in[...], zfar_in[...])
    total = own_ref[...] + exact_pick(returned, chooser(send_ref[...], atoms), ROWROW)
    force_ref[...] = -total[0:3]


def partners(axis, far):
    count = lax.axis_size(axis)
    if far:
        return [(i, (i + (1 if i % 2 else -1)) % count) for i in range(count)]
    return [(i, i ^ 1) for i in range(count)]


def swap_both(axis, to_mate, to_far):
    to_mate, to_far = lax.optimization_barrier((to_mate, to_far))
    mate = lax.ppermute(to_mate, axis, partners(axis, False))
    far = lax.ppermute(to_far, axis, partners(axis, True))
    return lax.optimization_barrier((mate, far))


def exchange_rows(rows):
    mate, far = swap_both("gx", rows, rows)
    column = jnp.stack([rows, mate, far])
    zmate, zfar = swap_both("gy", column, column)
    return mate, far, zmate, zfar


def exchange_packets(even_y, to_mate, to_far, side):
    mate, far = swap_both("gx", to_mate, to_far)
    up = jnp.concatenate([mate[2:3], far[2:3], side[1:2]], axis=0)
    down = jnp.concatenate([mate[0:1], far[0:1], side[0:1]], axis=0)
    zmate, zfar = swap_both("gy", jnp.where(even_y, up, down), jnp.where(even_y, down, up))
    return mate, far, zmate, zfar


def struct(*shape, dtype=F32):
    return jax.ShapeDtypeStruct(shape, dtype)


def call(kernel, in_specs, outs, scratch=()):
    return pl.pallas_call(
        kernel,
        in_specs=in_specs,
        out_specs=jax.tree.map(lambda _: VMEM, outs),
        out_shape=outs,
        scratch_shapes=list(scratch),
        compiler_params=PARAMS,
    )


def shards(fractions, species, send_list, tile_list, counts, embedding, radial, mixing, readout):
    atoms = fractions.shape[1]
    nodes = atoms + 8 * GHOSTS
    blocks = nodes // BLOCK
    even = jnp.stack([lax.axis_index("gx") % 2, lax.axis_index("gy") % 2]).astype(jnp.int32)
    even_y = even[1] == 0
    packets = [struct(3, GHOSTS, HIST), struct(3, GHOSTS, HIST), struct(2, GHOSTS, HIST)]
    grads = [struct(blocks, 8, 128), struct(atoms, 128)]
    pair_half = pltpu.VMEM((BASIS * BLOCK, 256), BF16)
    swap_half = pltpu.VMEM((256, BASIS * BLOCK), BF16)
    feat_half = pltpu.VMEM((blocks, 256, 256), BF16)
    pull = pltpu.VMEM((BASIS * BLOCK, 256), F32)

    site, rows = call(pack_kernel, [VMEM] * 3, [struct(8, atoms), struct(8, 128)])(
        fractions, species[None], send_list
    )
    arrived = exchange_rows(rows)
    hist, to_mate, to_far, side, col, row, fold_high, fold_low = call(
        first_kernel,
        [SMEM] * 4 + [VMEM] * 8,
        [struct(atoms, HIST)]
        + packets
        + [
            struct(nodes, 128),
            struct(blocks, 8, 128),
            struct(HIST, 640, dtype=BF16),
            struct(HIST, 640, dtype=BF16),
        ],
        [pltpu.VMEM((HIST, 640), F32), pair_half, pair_half],
    )(tile_list, counts, even, send_list, site, *arrived, embedding, radial, mixing)
    arrived = exchange_packets(even_y, to_mate, to_far, side)
    energy, to_mate, to_far, side, pull_hist, grad_row, grad_col = call(
        second_kernel,
        [SMEM] * 3 + [VMEM] * 13,
        [struct(1, atoms)] + packets + [struct(atoms, HIST)] + grads,
        [
            pltpu.VMEM((nodes, 640), F32),
            feat_half,
            feat_half,
            pltpu.VMEM((nodes, 128), F32),
            pair_half,
            pair_half,
            pltpu.VMEM((atoms, 128), F32),
            pltpu.VMEM((atoms, 128), F32),
            pltpu.VMEM((atoms, 128), F32),
            pltpu.VMEM((nodes, 512), F32),
            swap_half,
            swap_half,
            pull,
        ],
    )(
        tile_list,
        counts,
        even,
        hist,
        *arrived,
        col,
        row,
        fold_high,
        fold_low,
        embedding,
        radial,
        mixing,
        readout[None],
    )
    arrived = exchange_packets(even_y, to_mate, to_far, side)
    own, rows = call(
        third_kernel,
        [SMEM] * 3 + [VMEM] * 10,
        [struct(8, atoms), struct(8, 128)],
        [pltpu.VMEM((atoms, HIST), F32), pltpu.VMEM((blocks, 8, 128), F32), pltpu.VMEM((atoms, 128), F32), pull],
    )(tile_list, counts, even, send_list, pull_hist, *arrived, col, row, grad_row, grad_col)
    arrived = exchange_rows(rows)
    forces = call(last_kernel, [SMEM] + [VMEM] * 6, struct(3, atoms))(even, send_list, own, *arrived)
    return energy[0], forces


def solution(mesh):
    placed = (
        P(None, ("gx", "gy")),
        P(("gx", "gy")),
        P(None, ("gx", "gy")),
        P(None, ("gx", "gy")),
        P(("gx", "gy")),
        P(),
        P(),
        P(),
        P(),
    )
    return jax.shard_map(
        shards,
        mesh=mesh,
        in_specs=placed,
        out_specs=(P(("gx", "gy")), P(None, ("gx", "gy"))),
        check_vma=False,
    )
```

profile of v0, /device:TPU:4, one launch (start us, length us, event | category | flops | bytes accessed | tf_op | source)
XLA Modules:
  0.0 70.8 jit_solution(17424527398986987145)
XLA Ops:
  0.6 0.0 copy-start.3
  0.6 0.7 copy-done.3
  1.3 0.7 copy-done.7
  2.0 0.7 copy-done.8
  2.7 0.2 shard_map.104
  2.9 0.0 collective-permute-start
  2.9 1.5 %collective-permute-start.1 = (f32[8,128]{1,0:T(8,128)S(1)}, f32[8,128]{1,0:T(8,128)S(1)}, u32[]{:S(2)}, u32[]{:S(2)}) collective-permute-start(f32[8,128]{1,0:T(8,128)S(1)} %get-tuple-element.56), channel_id=1, source_target_pairs={{0,28},{4,8},{8,4},{12,16},{16,12},{20,24},{24,20},{28,0},{1,29},{... | collective-permute-start | bytes 12296 | tf_op jit(solution)/shard_map/ppermute | solution.py:601
  4.5 0.0 collective-permute-done.mate_in
  4.5 2.5 %collective-permute-done.1.far_in = f32[8,128]{1,0:T(8,128)S(1)} collective-permute-done((f32[8,128]{1,0:T(8,128)S(1)}, f32[8,128]{1,0:T(8,128)S(1)}, u32[]{:S(2)}, u32[]{:S(2)}) %collective-permute-start.1) | collective-permute-done | bytes 4128 | tf_op jit(solution)/shard_map/ppermute | solution.py:601
  6.9 1.6 %collective-permute-start.2 = (f32[3,8,128]{2,1,0:T(8,128)S(1)}, f32[3,8,128]{2,1,0:T(8,128)S(1)}, u32[]{:S(2)}, u32[]{:S(2)}) collective-permute-start(f32[3,8,128]{2,1,0:T(8,128)S(1)} %pad_maximum_fusion.4), channel_id=1, source_target_pairs={{0,1},{1,0},{2,3},{3,2},{4,5},{5,4},{6,7},{7,6},{8,9},{9,8},{10,11... | collective-permute-start | bytes 36872 | tf_op jit(solution)/shard_map/ppermute | solution.py:600
  8.5 2.5 %collective-permute-start.3 = (f32[3,8,128]{2,1,0:T(8,128)S(1)}, f32[3,8,128]{2,1,0:T(8,128)S(1)}, u32[]{:S(2)}, u32[]{:S(2)}) collective-permute-start(f32[3,8,128]{2,1,0:T(8,128)S(1)} %pad_maximum_fusion.4), channel_id=1, source_target_pairs={{0,3},{1,2},{2,1},{3,0},{4,7},{5,6},{6,5},{7,4},{8,11},{9,10},{10,... | collective-permute-start | bytes 36872 | tf_op jit(solution)/shard_map/ppermute | solution.py:601
  11.0 0.1 pad_add_fusion.even_ref
  11.7 0.0 copy-start.6
  11.7 0.0 collective-permute-done.2.zmate_in
  11.7 2.3 %collective-permute-done.3.zfar_in = f32[3,8,128]{2,1,0:T(8,128)S(1)} collective-permute-done((f32[3,8,128]{2,1,0:T(8,128)S(1)}, f32[3,8,128]{2,1,0:T(8,128)S(1)}, u32[]{:S(2)}, u32[]{:S(2)}) %collective-permute-start.3) | collective-permute-done | bytes 12320 | tf_op jit(solution)/shard_map/ppermute | solution.py:601
  14.0 0.0 copy-done.2
  14.0 0.0 copy-done.5
  14.0 0.0 copy-start
  14.0 1.0 %copy-done = f32[5,128,128]{2,1,0:T(8,128)S(1)} copy-done((f32[5,128,128]{2,1,0:T(8,128)S(1)}, f32[5,128,128]{2,1,0:T(8,128)}, u32[]{:S(2)}) %copy-start) | copy-done | bytes 327704
  15.0 3.8 %shard_map.105 = (f32[512,256]{1,0:T(8,128)S(1)}, f32[3,16,256]{2,1,0:T(8,128)S(1)}, f32[3,16,256]{2,1,0:T(8,128)S(1)}, f32[2,16,256]{2,1,0:T(8,128)S(1)}, f32[6...) custom-call(s32[2,6]{1,0:T(2,128)S(1)} %copy-done.6, ...), custom_call_target="tpu_custom_call" | custom-call | tf_op jit(solution)/shard_map/pallas_call | solution.py:652
  18.8 0.1 collective-permute-start.4
  18.9 0.1 collective-permute-start.5
  19.0 1.1 %collective-permute-done.4.mate_in = f32[3,16,256]{2,1,0:T(8,128)S(1)} collective-permute-done((f32[3,16,256]{2,1,0:T(8,128)S(1)}, f32[3,16,256]{2,1,0:T(8,128)S(1)}, u32[]{:S(2)}, u32[]{:S(2)}) %collective-permute-start.4) | collective-permute-done | bytes 49184 | tf_op jit(solution)/shard_map/ppermute | solution.py:600
  20.1 3.3 %collective-permute-done.5.far_in = f32[3,16,256]{2,1,0:T(8,128)S(1)} collective-permute-done((f32[3,16,256]{2,1,0:T(8,128)S(1)}, f32[3,16,256]{2,1,0:T(8,128)S(1)}, u32[]{:S(2)}, u32[]{:S(2)}) %collective-permute-start.5) | collective-permute-done | bytes 49184 | tf_op jit(solution)/shard_map/ppermute | solution.py:601
  23.4 0.1 collective-permute-start.6
  23.5 2.4 %collective-permute-start.7 = (f32[3,16,256]{2,1,0:T(8,128)S(1)}, f32[3,16,256]{2,1,0:T(8,128)S(1)}, u32[]{:S(2)}, u32[]{:S(2)}) collective-permute-start(f32[3,16,256]{2,1,0:T(8,128)S(1)} %get-tuple-element.72), channel_id=1, source_target_pairs={{0,3},{1,2},{2,1},{3,0},{4,7},{5,6},{6,5},{7,4},{8,11},{9,10},{10,... | collective-permute-start | bytes 147464 | tf_op jit(solution)/shard_map/ppermute | solution.py:601
  25.9 1.7 %collective-permute-done.6.zmate_in = f32[3,16,256]{2,1,0:T(8,128)S(1)} collective-permute-done((f32[3,16,256]{2,1,0:T(8,128)S(1)}, f32[3,16,256]{2,1,0:T(8,128)S(1)}, u32[]{:S(2)}, u32[]{:S(2)}) %collective-permute-start.6) | collective-permute-done | bytes 49184 | tf_op jit(solution)/shard_map/ppermute | solution.py:600
  27.6 2.0 %collective-permute-done.7.zfar_in = f32[3,16,256]{2,1,0:T(8,128)S(1)} collective-permute-done((f32[3,16,256]{2,1,0:T(8,128)S(1)}, f32[3,16,256]{2,1,0:T(8,128)S(1)}, u32[]{:S(2)}, u32[]{:S(2)}) %collective-permute-start.7) | collective-permute-done | bytes 49184 | tf_op jit(solution)/shard_map/ppermute | solution.py:601
  29.6 0.7 copy-done.9
  30.2 14.4 %shard_map.106 = (f32[1,512]{1,0:T(1,128)}, f32[3,16,256]{2,1,0:T(8,128)S(1)}, f32[3,16,256]{2,1,0:T(8,128)S(1)}, f32[2,16,256]{2,1,0:T(8,128)S(1)}, f32[512,256...) custom-call(s32[2,6]{1,0:T(2,128)S(1)} %copy-done.6, s32[1]{0:T(128)S(6)} %copy.11.count_ref, ...), custom_call_target="tpu_custom_call" | custom-call | tf_op jit(solution)/shard_map/pallas_call | solution.py:666
  44.6 0.1 collective-permute-start.8
  44.7 0.1 collective-permute-start.9
  44.8 1.1 %collective-permute-done.8.mate_in = f32[3,16,256]{2,1,0:T(8,128)S(1)} collective-permute-done((f32[3,16,256]{2,1,0:T(8,128)S(1)}, f32[3,16,256]{2,1,0:T(8,128)S(1)}, u32[]{:S(2)}, u32[]{:S(2)}) %collective-permute-start.8) | collective-permute-done | bytes 49184 | tf_op jit(solution)/shard_map/ppermute | solution.py:600
  45.9 3.3 %collective-permute-done.9.far_in = f32[3,16,256]{2,1,0:T(8,128)S(1)} collective-permute-done((f32[3,16,256]{2,1,0:T(8,128)S(1)}, f32[3,16,256]{2,1,0:T(8,128)S(1)}, u32[]{:S(2)}, u32[]{:S(2)}) %collective-permute-start.9) | collective-permute-done | bytes 49184 | tf_op jit(solution)/shard_map/ppermute | solution.py:601
  49.2 0.1 collective-permute-start.10
  49.3 1.7 %collective-permute-start.11 = (f32[3,16,256]{2,1,0:T(8,128)S(1)}, f32[3,16,256]{2,1,0:T(8,128)S(1)}, u32[]{:S(2)}, u32[]{:S(2)}) collective-permute-start(f32[3,16,256]{2,1,0:T(8,128)S(1)} %get-tuple-element.89), channel_id=1, source_target_pairs={{0,3},{1,2},{2,1},{3,0},{4,7},{5,6},{6,5},{7,4},{8,11},{9,10},{10,... | collective-permute-start | bytes 147464 | tf_op jit(solution)/shard_map/ppermute | solution.py:601
  51.0 2.4 %collective-permute-done.10.zmate_in = f32[3,16,256]{2,1,0:T(8,128)S(1)} collective-permute-done((f32[3,16,256]{2,1,0:T(8,128)S(1)}, f32[3,16,256]{2,1,0:T(8,128)S(1)}, u32[]{:S(2)}, u32[]{:S(2)}) %collective-permute-start.10) | collective-permute-done | bytes 49184 | tf_op jit(solution)/shard_map/ppermute | solution.py:600
  53.4 2.0 %collective-permute-done.11.zfar_in = f32[3,16,256]{2,1,0:T(8,128)S(1)} collective-permute-done((f32[3,16,256]{2,1,0:T(8,128)S(1)}, f32[3,16,256]{2,1,0:T(8,128)S(1)}, u32[]{:S(2)}, u32[]{:S(2)}) %collective-permute-start.11) | collective-permute-done | bytes 49184 | tf_op jit(solution)/shard_map/ppermute | solution.py:601
  55.3 4.5 %shard_map.107 = (f32[8,512]{1,0:T(8,128)S(1)}, f32[8,128]{1,0:T(8,128)S(1)}) custom-call(s32[2,6]{1,0:T(2,128)S(1)} %copy-done.6, s32[1]{0:T(128)S(6)} %copy.11.count_ref, s32[2]{0:T(128)S(1)} %pad_add_fusion.even_ref, s32[8,16]{1,0:T(8,128)S(1)} %copy-done.4, f32[512,256]{1,0:T(8,128)S(1)} %get-tuple-element.80.pull_hist_ref, ...), custom_call_target="tpu_custom_call" | custom-call | tf_op jit(solution)/shard_map/pallas_call | solution.py:701
  59.8 0.1 collective-permute-start.12
  59.9 0.1 collective-permute-start.13
  60.0 1.1 %collective-permute-done.12.mate_in = f32[8,128]{1,0:T(8,128)S(1)} collective-permute-done((f32[8,128]{1,0:T(8,128)S(1)}, f32[8,128]{1,0:T(8,128)S(1)}, u32[]{:S(2)}, u32[]{:S(2)}) %collective-permute-start.12) | collective-permute-done | bytes 4128 | tf_op jit(solution)/shard_map/ppermute | solution.py:600
  61.0 2.8 %collective-permute-done.13.far_in = f32[8,128]{1,0:T(8,128)S(1)} collective-permute-done((f32[8,128]{1,0:T(8,128)S(1)}, f32[8,128]{1,0:T(8,128)S(1)}, u32[]{:S(2)}, u32[]{:S(2)}) %collective-permute-start.13) | collective-permute-done | bytes 4128 | tf_op jit(solution)/shard_map/ppermute | solution.py:601
  63.9 0.0 collective-permute-start.14
  63.9 1.3 %collective-permute-start.15 = (f32[3,8,128]{2,1,0:T(8,128)S(1)}, f32[3,8,128]{2,1,0:T(8,128)S(1)}, u32[]{:S(2)}, u32[]{:S(2)}) collective-permute-start(f32[3,8,128]{2,1,0:T(8,128)S(1)} %pad_maximum_fusion.5), channel_id=1, source_target_pairs={{0,3},{1,2},{2,1},{3,0},{4,7},{5,6},{6,5},{7,4},{8,11},{9,10},{10,... | collective-permute-start | bytes 36872 | tf_op jit(solution)/shard_map/ppermute | solution.py:601
  65.2 2.4 %collective-permute-done.14.zmate_in = f32[3,8,128]{2,1,0:T(8,128)S(1)} collective-permute-done((f32[3,8,128]{2,1,0:T(8,128)S(1)}, f32[3,8,128]{2,1,0:T(8,128)S(1)}, u32[]{:S(2)}, u32[]{:S(2)}) %collective-permute-start.14) | collective-permute-done | bytes 12320 | tf_op jit(solution)/shard_map/ppermute | solution.py:600
  67.6 1.8 %collective-permute-done.15.zfar_in = f32[3,8,128]{2,1,0:T(8,128)S(1)} collective-permute-done((f32[3,8,128]{2,1,0:T(8,128)S(1)}, f32[3,8,128]{2,1,0:T(8,128)S(1)}, u32[]{:S(2)}, u32[]{:S(2)}) %collective-permute-start.15) | collective-permute-done | bytes 12320 | tf_op jit(solution)/shard_map/ppermute | solution.py:601
  69.4 1.4 %shard_map.108 = f32[3,512]{1,0:T(4,128)} custom-call(s32[2]{0:T(128)S(1)} %pad_add_fusion.even_ref, s32[8,16]{1,0:T(8,128)S(1)} %copy-done.4, f32[8,512]{1,0:T(8,128)S(1)} %get-tuple-element.94.own_ref, f32[8,128]{1,0:T(8,128)S(1)} %collective-permute-done.12.mate_in, f32[8,128]{1,0:T(8,128)S(1)} %collective-permute-done.13.far_in, ...), custom_call_target="tpu_custom_call" | custom-call | tf_op jit(solution)/shard_map/pallas_call | solution.py:708
  (19 shorter events, 0.1 us)
Async XLA Ops:
  0.6 0.7 copy-start.3
  1.3 0.7 copy-start.7
  2.0 0.7 copy-start.8
  2.9 1.6 %collective-permute-start = (f32[8,128]{1,0:T(8,128)S(1)}, f32[8,128]{1,0:T(8,128)S(1)}, u32[]{:S(2)}, u32[]{:S(2)}) collective-permute-start(f32[8,128]{1,0:T(8,128)S(1)} %get-tuple-element.56), channel_id=1, source_target_pairs={{0,4},{4,0},{8,12},{12,8},{16,20},{20,16},{24,28},{28,24},{1,5},{5... | collective-permute-start | bytes 12296 | tf_op jit(solution)/shard_map/ppermute | solution.py:600
  2.9 4.0 %collective-permute-start.1 = (f32[8,128]{1,0:T(8,128)S(1)}, f32[8,128]{1,0:T(8,128)S(1)}, u32[]{:S(2)}, u32[]{:S(2)}) collective-permute-start(f32[8,128]{1,0:T(8,128)S(1)} %get-tuple-element.56), channel_id=1, source_target_pairs={{0,28},{4,8},{8,4},{12,16},{16,12},{20,24},{24,20},{28,0},{1,29},{... | collective-permute-start | bytes 12296 | tf_op jit(solution)/shard_map/ppermute | solution.py:601
  6.9 7.1 %copy-start.2 = (f32[4,8,128]{2,1,0:T(8,128)S(1)}, f32[4,8,128]{2,1,0:T(8,128)}, u32[]{:S(2)}) copy-start(f32[4,8,128]{2,1,0:T(8,128)} %radial_ref.3) | copy-start | bytes 49156
  6.9 4.8 %collective-permute-start.2 = (f32[3,8,128]{2,1,0:T(8,128)S(1)}, f32[3,8,128]{2,1,0:T(8,128)S(1)}, u32[]{:S(2)}, u32[]{:S(2)}) collective-permute-start(f32[3,8,128]{2,1,0:T(8,128)S(1)} %pad_maximum_fusion.4), channel_id=1, source_target_pairs={{0,1},{1,0},{2,3},{3,2},{4,5},{5,4},{6,7},{7,6},{8,9},{9,8},{10,11... | collective-permute-start | bytes 36872 | tf_op jit(solution)/shard_map/ppermute | solution.py:600
  8.5 5.5 %collective-permute-start.3 = (f32[3,8,128]{2,1,0:T(8,128)S(1)}, f32[3,8,128]{2,1,0:T(8,128)S(1)}, u32[]{:S(2)}, u32[]{:S(2)}) collective-permute-start(f32[3,8,128]{2,1,0:T(8,128)S(1)} %pad_maximum_fusion.4), channel_id=1, source_target_pairs={{0,3},{1,2},{2,1},{3,0},{4,7},{5,6},{6,5},{7,4},{8,11},{9,10},{10,... | collective-permute-start | bytes 36872 | tf_op jit(solution)/shard_map/ppermute | solution.py:601
  11.0 3.0 %copy-start.5 = (f32[6,128]{1,0:T(8,128)S(1)}, f32[6,128]{1,0:T(8,128)}, u32[]{:S(2)}) copy-start(f32[6,128]{1,0:T(8,128)} %embed_ref.3) | copy-start | bytes 9220
  11.0 3.0 %copy-start.4 = (s32[8,16]{1,0:T(8,128)S(1)}, s32[8,16]{1,0:T(8,128)}, u32[]{:S(2)}) copy-start(s32[8,16]{1,0:T(8,128)} %send_ref.7) | copy-start | bytes 1540
  11.7 2.3 %copy-start.6 = (s32[2,6]{1,0:T(2,128)S(1)}, s32[2,6]{1,0:T(2,128)}, u32[]{:S(2)}) copy-start(s32[2,6]{1,0:T(2,128)} %tile_ref.5) | copy-start | bytes 148
  14.0 1.0 %copy-start = (f32[5,128,128]{2,1,0:T(8,128)S(1)}, f32[5,128,128]{2,1,0:T(8,128)}, u32[]{:S(2)}) copy-start(f32[5,128,128]{2,1,0:T(8,128)} %mixing_ref.3) | copy-start | bytes 983044
  15.0 14.6 %copy-start.1 = (f32[5,128,128]{2,1,0:T(8,128)S(1)}, f32[5,128,128]{2,1,0:T(8,128)}, u32[]{:S(2)}) copy-start(f32[5,128,128]{2,1,0:T(8,128)} %mixing_ref.3) | copy-start | bytes 983044
  18.8 1.3 %collective-permute-start.4 = (f32[3,16,256]{2,1,0:T(8,128)S(1)}, f32[3,16,256]{2,1,0:T(8,128)S(1)}, u32[]{:S(2)}, u32[]{:S(2)}) collective-permute-start(f32[3,16,256]{2,1,0:T(8,128)S(1)} %get-tuple-element.66), channel_id=1, source_target_pairs={{0,4},{4,0},{8,12},{12,8},{16,20},{20,16},{24,28},{28,24},{1,5},{5... | collective-permute-start | bytes 147464 | tf_op jit(solution)/shard_map/ppermute | solution.py:600
  18.9 4.5 %collective-permute-start.5 = (f32[3,16,256]{2,1,0:T(8,128)S(1)}, f32[3,16,256]{2,1,0:T(8,128)S(1)}, u32[]{:S(2)}, u32[]{:S(2)}) collective-permute-start(f32[3,16,256]{2,1,0:T(8,128)S(1)} %get-tuple-element.67), channel_id=1, source_target_pairs={{0,28},{4,8},{8,4},{12,16},{16,12},{20,24},{24,20},{28,0},{1,29},{... | collective-permute-start | bytes 147464 | tf_op jit(solution)/shard_map/ppermute | solution.py:601
  23.4 4.2 %collective-permute-start.6 = (f32[3,16,256]{2,1,0:T(8,128)S(1)}, f32[3,16,256]{2,1,0:T(8,128)S(1)}, u32[]{:S(2)}, u32[]{:S(2)}) collective-permute-start(f32[3,16,256]{2,1,0:T(8,128)S(1)} %get-tuple-element.71), channel_id=1, source_target_pairs={{0,1},{1,0},{2,3},{3,2},{4,5},{5,4},{6,7},{7,6},{8,9},{9,8},{10,11... | collective-permute-start | bytes 147464 | tf_op jit(solution)/shard_map/ppermute | solution.py:600
  23.5 6.1 %collective-permute-start.7 = (f32[3,16,256]{2,1,0:T(8,128)S(1)}, f32[3,16,256]{2,1,0:T(8,128)S(1)}, u32[]{:S(2)}, u32[]{:S(2)}) collective-permute-start(f32[3,16,256]{2,1,0:T(8,128)S(1)} %get-tuple-element.72), channel_id=1, source_target_pairs={{0,3},{1,2},{2,1},{3,0},{4,7},{5,6},{6,5},{7,4},{8,11},{9,10},{10,... | collective-permute-start | bytes 147464 | tf_op jit(solution)/shard_map/ppermute | solution.py:601
  29.6 0.7 copy-start.9
  44.6 1.3 %collective-permute-start.8 = (f32[3,16,256]{2,1,0:T(8,128)S(1)}, f32[3,16,256]{2,1,0:T(8,128)S(1)}, u32[]{:S(2)}, u32[]{:S(2)}) collective-permute-start(f32[3,16,256]{2,1,0:T(8,128)S(1)} %get-tuple-element.83), channel_id=1, source_target_pairs={{0,4},{4,0},{8,12},{12,8},{16,20},{20,16},{24,28},{28,24},{1,5},{5... | collective-permute-start | bytes 147464 | tf_op jit(solution)/shard_map/ppermute | solution.py:600
  44.7 4.5 %collective-permute-start.9 = (f32[3,16,256]{2,1,0:T(8,128)S(1)}, f32[3,16,256]{2,1,0:T(8,128)S(1)}, u32[]{:S(2)}, u32[]{:S(2)}) collective-permute-start(f32[3,16,256]{2,1,0:T(8,128)S(1)} %get-tuple-element.84), channel_id=1, source_target_pairs={{0,28},{4,8},{8,4},{12,16},{16,12},{20,24},{24,20},{28,0},{1,29},{... | collective-permute-start | bytes 147464 | tf_op jit(solution)/shard_map/ppermute | solution.py:601
  49.2 4.2 %collective-permute-start.10 = (f32[3,16,256]{2,1,0:T(8,128)S(1)}, f32[3,16,256]{2,1,0:T(8,128)S(1)}, u32[]{:S(2)}, u32[]{:S(2)}) collective-permute-start(f32[3,16,256]{2,1,0:T(8,128)S(1)} %get-tuple-element.88), channel_id=1, source_target_pairs={{0,1},{1,0},{2,3},{3,2},{4,5},{5,4},{6,7},{7,6},{8,9},{9,8},{10,11... | collective-permute-start | bytes 147464 | tf_op jit(solution)/shard_map/ppermute | solution.py:600
  49.3 6.1 %collective-permute-start.11 = (f32[3,16,256]{2,1,0:T(8,128)S(1)}, f32[3,16,256]{2,1,0:T(8,128)S(1)}, u32[]{:S(2)}, u32[]{:S(2)}) collective-permute-start(f32[3,16,256]{2,1,0:T(8,128)S(1)} %get-tuple-element.89), channel_id=1, source_target_pairs={{0,3},{1,2},{2,1},{3,0},{4,7},{5,6},{6,5},{7,4},{8,11},{9,10},{10,... | collective-permute-start | bytes 147464 | tf_op jit(solution)/shard_map/ppermute | solution.py:601
  59.8 1.2 %collective-permute-start.12 = (f32[8,128]{1,0:T(8,128)S(1)}, f32[8,128]{1,0:T(8,128)S(1)}, u32[]{:S(2)}, u32[]{:S(2)}) collective-permute-start(f32[8,128]{1,0:T(8,128)S(1)} %get-tuple-element.97), channel_id=1, source_target_pairs={{0,4},{4,0},{8,12},{12,8},{16,20},{20,16},{24,28},{28,24},{1,5},{5... | collective-permute-start | bytes 12296 | tf_op jit(solution)/shard_map/ppermute | solution.py:600
  59.9 4.0 %collective-permute-start.13 = (f32[8,128]{1,0:T(8,128)S(1)}, f32[8,128]{1,0:T(8,128)S(1)}, u32[]{:S(2)}, u32[]{:S(2)}) collective-permute-start(f32[8,128]{1,0:T(8,128)S(1)} %get-tuple-element.97), channel_id=1, source_target_pairs={{0,28},{4,8},{8,4},{12,16},{16,12},{20,24},{24,20},{28,0},{1,29},{... | collective-permute-start | bytes 12296 | tf_op jit(solution)/shard_map/ppermute | solution.py:601
  63.9 3.7 %collective-permute-start.14 = (f32[3,8,128]{2,1,0:T(8,128)S(1)}, f32[3,8,128]{2,1,0:T(8,128)S(1)}, u32[]{:S(2)}, u32[]{:S(2)}) collective-permute-start(f32[3,8,128]{2,1,0:T(8,128)S(1)} %pad_maximum_fusion.5), channel_id=1, source_target_pairs={{0,1},{1,0},{2,3},{3,2},{4,5},{5,4},{6,7},{7,6},{8,9},{9,8},{10,11... | collective-permute-start | bytes 36872 | tf_op jit(solution)/shard_map/ppermute | solution.py:600
  63.9 5.5 %collective-permute-start.15 = (f32[3,8,128]{2,1,0:T(8,128)S(1)}, f32[3,8,128]{2,1,0:T(8,128)S(1)}, u32[]{:S(2)}, u32[]{:S(2)}) collective-permute-start(f32[3,8,128]{2,1,0:T(8,128)S(1)} %pad_maximum_fusion.5), channel_id=1, source_target_pairs={{0,3},{1,2},{2,1},{3,0},{4,7},{5,6},{6,5},{7,4},{8,11},{9,10},{10,... | collective-permute-start | bytes 36872 | tf_op jit(solution)/shard_map/ppermute | solution.py:601
where the time goes:
time: 71 us; the launch traced here: 70.8 us
  waiting for transfers between devices  29.6 us (42%)
  Pallas kernels  24.3 us (34%)
  starting transfers between devices  11.5 us (16%)
  local copies, waits for them, and re-layouts  3.72 us (5%)
  between operations  1.45 us (2%)
    ppermute x8, waiting for transfers between devices, swap_both(): far = lax.ppermute(to_far, axis, partners(axis, True))  19.8 us
    pallas_call x1, Pallas kernels, shards(): call(second_kernel, [SMEM] * 3 + [VMEM] * 13, [struct(1, atoms)] + packet...  14.4 us
    ppermute x8, waiting for transfers between devices, swap_both(): mate = lax.ppermute(to_mate, axis, partners(axis, False))  9.78 us
    ppermute x8, starting transfers between devices, swap_both(): far = lax.ppermute(to_far, axis, partners(axis, True))  9.62 us
    pallas_call x1, Pallas kernels, shards(): call(third_kernel, [SMEM] * 3 + [VMEM] * 10, [struct(8, atoms), struct(8,...  4.49 us
    pallas_call x1, Pallas kernels, shards(): call(first_kernel, [SMEM] * 4 + [VMEM] * 8, [struct(atoms, HIST)] + packe...  3.83 us
    unnamed x20, local copies, waits for them, and re-layouts  3.7 us
    ppermute x8, starting transfers between devices, swap_both(): mate = lax.ppermute(to_mate, axis, partners(axis, False))  1.92 us
  transfers between devices with their start and end apart: 16, of which 14 were waited for; matrix products, arithmetic and copies ran while one was open for 0% of the time, Pallas kernels for 0%

commit v1 on v0

v1 whole, which is shorter than its diff:
```python
import functools

import jax
import jax.numpy as jnp
from jax import lax
from jax.experimental import pallas as pl
from jax.experimental.pallas import tpu as pltpu
from jax.sharding import PartitionSpec as P

F32 = jnp.float32
BF16 = jnp.bfloat16

BASIS = 8
BLOCK = 64
GHOSTS = 16
SPAN = 8
HIST = BASIS * 4 * SPAN
OFFSETS = ((-1, -1), (-1, 0), (-1, 1), (0, -1), (0, 1), (1, -1), (1, 0), (1, 1))
WIDTHS = (12.0, 12.0, 36.0)
CUT_INV = 1.0 / 25.0
ROOT = 1.6986436005760381
CENTERS = tuple(1.0 + 0.6 * n for n in range(BASIS))
ROWS = 32

VMEM = pl.BlockSpec(memory_space=pltpu.VMEM)
HBM = pl.BlockSpec(memory_space=pltpu.HBM)
PARAMS = pltpu.CompilerParams(vmem_limit_bytes=16 * 1024 * 1024)

ROWROW = (((1,), (1,)), ((), ()))
ROWCOL = (((1,), (0,)), ((), ()))


def split(value):
    high = value.astype(BF16)
    return high, (value - high.astype(F32)).astype(BF16)


def mm(left, right, dims=ROWCOL):
    return lax.dot_general(left, right, dims, preferred_element_type=F32)


def mm3(left, right, dims=ROWCOL):
    (lh, ll), (rh, rl) = left, right
    summed = dims[0][1][0]
    return mm(
        jnp.concatenate([lh, ll, lh], axis=1), jnp.concatenate([rh, rh, rl], axis=summed), dims
    )


def sigmoid(value):
    return 1.0 / (1.0 + jnp.exp(-value))


def iota(shape, dim):
    return lax.broadcasted_iota(jnp.int32, shape, dim)


def low_half():
    return iota((1, 128), 1) < BLOCK


def pick_rows(even_x, even_y, mate, far, zmate, zfar):
    x_up, x_down = jnp.where(even_x, mate, far), jnp.where(even_x, far, mate)
    y_up = [jnp.where(even_y, zmate[i], zfar[i]) for i in range(3)]
    y_down = [jnp.where(even_y, zfar[i], zmate[i]) for i in range(3)]
    sources = {
        (1, 0): x_up,
        (-1, 0): x_down,
        (0, 1): y_up[0],
        (0, -1): y_down[0],
        (1, 1): jnp.where(even_x, y_up[1], y_up[2]),
        (-1, 1): jnp.where(even_x, y_up[2], y_up[1]),
        (1, -1): jnp.where(even_x, y_down[1], y_down[2]),
        (-1, -1): jnp.where(even_x, y_down[2], y_down[1]),
    }
    slot_of = iota((8, 128), 1) // GHOSTS
    total = jnp.zeros((8, 128), F32)
    for slot, offset in enumerate(OFFSETS):
        turned = pltpu.roll(sources[offset], ((2 * slot - 7) * GHOSTS) % 128, 1)
        total = jnp.where(slot_of == slot, turned, total)
    return total


def pick_slot(slot, even_x, even_y, mate, far, zmate, zfar):
    along_x, along_y = OFFSETS[slot]
    if along_y == 0:
        near = even_x if along_x == 1 else jnp.logical_not(even_x)
        return jnp.where(near, mate[1], far[1])
    near = even_y if along_y == 1 else jnp.logical_not(even_y)
    if along_x == 0:
        return jnp.where(near, zmate[2], zfar[2])
    first = even_x if along_x == 1 else jnp.logical_not(even_x)
    return jnp.where(
        near, jnp.where(first, zmate[0], zmate[1]), jnp.where(first, zfar[0], zfar[1])
    )


def pick_all(args):
    return jnp.concatenate([pick_slot(slot, *args) for slot in range(8)], axis=0)


def put_packets(even_x, piece, mate_ref, far_ref, side_ref):
    for part in range(3):
        down, up = piece(part), piece(5 + part)
        mate_ref[part] = jnp.where(even_x, up, down)
        far_ref[part] = jnp.where(even_x, down, up)
    side_ref[0] = piece(3)
    side_ref[1] = piece(4)


def send_columns(send):
    wide = jnp.concatenate([send] * 8, axis=1)
    own = iota((8, 128), 1) // GHOSTS == iota((8, 128), 0)
    return jnp.sum(jnp.where(own, wide, 0), axis=0, keepdims=True)


def chooser(send, atoms):
    return iota((atoms, 128), 0) == send_columns(send)


def block_rows(block, start=0, count=BLOCK):
    return pl.ds(pl.multiple_of(block * BLOCK, BLOCK) + start, count)


def separation(col_ref, col_block, row_ref, row_block, start, sign):
    mine = col_ref[block_rows(col_block, start, ROWS), :]
    other = row_ref[row_block]
    return [sign * (other[a : a + 1, :] - mine[:, a : a + 1]) for a in range(3)]


def envelope(parts, same, start):
    dist_sq = parts[0] * parts[0] + parts[1] * parts[1] + parts[2] * parts[2]
    soft = jnp.sqrt(dist_sq + 1.0)
    rows = iota((ROWS, 128), 0) + start
    columns = iota((ROWS, 128), 1) % BLOCK
    apart = jnp.where(jnp.logical_and(rows == columns, same), 0.0, 1.0)
    margin = jnp.maximum(1.0 - dist_sq * CUT_INV, 0.0) * apart
    return soft, margin


def angular(parts, inverse):
    u = [part * inverse for part in parts]
    low = low_half()
    return jnp.where(low, 1.0, u[0]), jnp.where(low, u[1], u[2])


def pair_forward(col_ref, left, row_ref, right, same, high_ref, low_ref):
    for start in range(0, BLOCK, ROWS):
        parts = separation(col_ref, left, row_ref, right, start, 1.0)
        soft, margin = envelope(parts, same, start)
        first, second = angular(parts, 1.0 / soft)
        weight = margin * margin
        first, second = first * weight, second * weight
        scaled = soft * ROOT
        for n in range(BASIS):
            shift = scaled - ROOT * CENTERS[n]
            bell = jnp.exp2(-(shift * shift))
            here = pl.ds(n * BLOCK + start, ROWS)
            for half, factor in enumerate((first, second)):
                high, low = split(bell * factor)
                high_ref[here, half * 128 : half * 128 + 128] = high
                low_ref[here, half * 128 : half * 128 + 128] = low


def pair_swapped(col_ref, right, row_ref, left, same, high_ref, low_ref):
    low_lanes = low_half()
    for start in range(0, BLOCK, ROWS):
        parts = separation(col_ref, right, row_ref, left, start, -1.0)
        soft, margin = envelope(parts, same, start)
        inverse = 1.0 / soft
        weight = margin * margin
        factors = [weight] + [weight * (part * inverse) for part in parts]
        scaled = soft * ROOT
        for pair in range(BASIS // 2):
            center = jnp.where(low_lanes, ROOT * CENTERS[2 * pair], ROOT * CENTERS[2 * pair + 1])
            shift = scaled - center
            bell = jnp.exp2(-(shift * shift))
            for order in range(4):
                high, low = split(bell * factors[order])
                here = pl.ds(order * BLOCK + start, ROWS)
                high_ref[here, pair * 128 : pair * 128 + 128] = high
                low_ref[here, pair * 128 : pair * 128 + 128] = low


def pair_backward(col_ref, left, row_ref, right, same, pull_ref, grad_row, grad_col):
    low_lanes = low_half()
    lane = iota((1, 128), 1)
    sums = [jnp.zeros((1, 128), F32) for _ in range(3)]
    for start in range(0, BLOCK, ROWS):
        parts = separation(col_ref, left, row_ref, right, start, 1.0)
        soft, margin = envelope(parts, same, start)
        inverse = 1.0 / soft
        first, second = angular(parts, inverse)
        scaled = soft * ROOT
        by_bell = jnp.zeros((ROWS, 128), F32)
        by_shift = jnp.zeros((ROWS, 128), F32)
        by_first = jnp.zeros((ROWS, 128), F32)
        by_second = jnp.zeros((ROWS, 128), F32)
        for n in range(BASIS):
            shift = scaled - ROOT * CENTERS[n]
            bell = jnp.exp2(-(shift * shift))
            here = pl.ds(n * BLOCK + start, ROWS)
            pull_first, pull_second = pull_ref[here, 0:128], pull_ref[here, 128:256]
            both = bell * (first * pull_first + second * pull_second)
            by_bell = by_bell + both
            by_shift = by_shift + shift * both
            by_first = by_first + bell * pull_first
            by_second = by_second + bell * pull_second
        weight = margin * margin
        by_bell = by_bell + pltpu.roll(by_bell, BLOCK, 1)
        by_shift = (by_shift + pltpu.roll(by_shift, BLOCK, 1)) * weight
        by_first, by_second = by_first * weight, by_second * weight
        turned = pltpu.roll(by_second, BLOCK, 1)
        by_u = [
            jnp.where(low_lanes, pltpu.roll(by_first, BLOCK, 1), by_first),
            jnp.where(low_lanes, by_second, turned),
            jnp.where(low_lanes, turned, by_second),
        ]
        along = (by_u[0] * parts[0] + by_u[1] * parts[1] + by_u[2] * parts[2]) * inverse
        by_soft = by_shift * (-4.0 / ROOT) - along * inverse
        radial_part = by_soft * inverse + by_bell * (margin * (-4.0 * CUT_INV))
        column = jnp.zeros((ROWS, 128), F32)
        for a in range(3):
            force = by_u[a] * inverse + parts[a] * radial_part
            sums[a] = sums[a] + jnp.sum(force, axis=0, keepdims=True)
            total = jnp.sum(jnp.where(low_lanes, force, 0.0), axis=1, keepdims=True)
            column = jnp.where(lane == a, total, column)
        grad_col[block_rows(left, start, ROWS), :] -= column
    grad_row[right] += jnp.concatenate(sums + [jnp.zeros((5, 128), F32)], axis=0)


def kind_table(col_ref, block):
    kind = col_ref[block_rows(block), 3:4].astype(jnp.int32)
    lane = iota((BLOCK, 128), 1)
    hit = kind == lane % SPAN
    return jnp.concatenate(
        [
            jnp.where(jnp.logical_and(hit, lane // SPAN % 4 == order), 1.0, 0.0)
            for order in range(4)
        ],
        axis=0,
    ).astype(BF16)


def parities(control_ref):
    return control_ref[1, 2] == 0, control_ref[2, 2] == 0


def own_tiles(control_ref, own_blocks, work):
    def step(slot, carried):
        left, right = control_ref[slot, 0], control_ref[slot, 1]

        @pl.when(right < own_blocks)
        def _():
            work(slot, left, right)

        return carried

    lax.fori_loop(2, control_ref[0, 2], step, 0)


def more_ghost_tiles(control_ref, own_blocks, work):
    def step(slot, carried):
        left, right = control_ref[slot, 0], control_ref[slot, 1]

        @pl.when(right >= own_blocks)
        def _():
            work(slot, left, right - own_blocks)

        return carried

    lax.fori_loop(2, control_ref[0, 2], step, 0)


def exact_pick(rows, chosen):
    high = rows.astype(BF16).astype(F32)
    rest = rows - high
    middle = rest.astype(BF16).astype(F32)
    stacked = jnp.concatenate(
        [high, middle, rest - middle, jnp.zeros_like(rows)], axis=0
    ).astype(BF16)
    picked = mm(stacked, chosen)
    return picked[0:8] + picked[8:16] + picked[16:24]


def fetch(pairs, sems):
    copies = [
        pltpu.make_async_copy(source, target, sems.at[i]) for i, (source, target) in enumerate(pairs)
    ]
    for copy in copies:
        copy.start()
    return copies


def pack_kernel(
    frac_in,
    kind_in,
    send_in,
    tile_in,
    site_ref,
    out_ref,
    send_ref,
    tiles_ref,
    frac_ref,
    kind_ref,
    tile_ref,
    sems,
):
    copies = fetch(
        (
            (frac_in, frac_ref),
            (kind_in, kind_ref),
            (send_in, send_ref),
            (tile_in, tile_ref),
        ),
        sems,
    )
    for copy in copies:
        copy.wait()
    atoms = frac_ref.shape[1]
    rows = jnp.concatenate(
        [frac_ref[...], kind_ref[...].astype(F32), jnp.zeros((4, atoms), F32)], axis=0
    )
    site_ref[...] = rows
    out_ref[...] = exact_pick(rows, chooser(send_ref[...], atoms).astype(F32).astype(BF16))
    slots = tile_ref.shape[1]
    lines = jnp.concatenate([tile_ref[...].astype(F32), jnp.zeros((2, 128 - slots), F32)], axis=1)
    lines = jnp.concatenate([lines, jnp.zeros((126, 128), F32)], axis=0)
    tiles_ref[...] = lines.T[0:8].astype(jnp.int32)


def doubled(rows, block):
    chunk = rows[:, block // 2 * 128 : block // 2 * 128 + 128]
    turned = pltpu.roll(chunk, BLOCK, 1)
    low = low_half()
    return jnp.where(low, chunk, turned) if block % 2 == 0 else jnp.where(low, turned, chunk)


def upright(rows):
    return jnp.concatenate([rows, jnp.zeros((120, rows.shape[1]), F32)], axis=0).T


def radial_row(weight_ref, path, n):
    row = SPAN + path * BASIS + n
    return weight_ref[row : row + 1, :]


def readout_row(weight_ref):
    row = SPAN + 4 * BASIS
    return weight_ref[row : row + 1, :]


def axis_scale():
    row = iota((8, 128), 0)
    return jnp.where(row < 2, WIDTHS[0], jnp.where(row == 2, WIDTHS[2], 1.0))


def add_histogram(col_ref, left, row_ref, right, same, kind_ref, hist_ref, high_ref, low_ref):
    pair_forward(col_ref, left, row_ref, right, same, high_ref, low_ref)
    table = kind_table(kind_ref, right)
    found = mm(high_ref[...], table) + mm(low_ref[...], table)
    lane_basis = iota((1, 128), 1) // (4 * SPAN)
    for half in range(2):
        total = jnp.zeros((BLOCK, 128), F32)
        for n in range(4):
            begin = (half * 4 + n) * BLOCK
            total = jnp.where(lane_basis == n, found[begin : begin + BLOCK], total)
        hist_ref[block_rows(left), half * 128 : half * 128 + 128] += total


def prepare_kernel(
    words_ref,
    tiles_ref,
    site_ref,
    send_ref,
    embed_in,
    radial_in,
    readout_in,
    mixing_in,
    control_ref,
    col_ref,
    row_ref,
    hist_ref,
    pair_high,
    pair_low,
    fold_high,
    fold_low,
    chosen_ref,
    mix_high,
    mix_low,
    weight_ref,
    fold_ref,
    mixing_ref,
    sems,
):
    kinds = embed_in.shape[0]
    paths = radial_in.shape[0]
    copies = fetch(
        (
            (embed_in, weight_ref.at[pl.ds(0, kinds)]),
            (radial_in, weight_ref.at[pl.ds(SPAN, paths)]),
            (readout_in, weight_ref.at[pl.ds(SPAN + paths, 1)]),
            (mixing_in, mixing_ref),
        ),
        sems,
    )
    row = iota((8, 128), 0)
    words = jnp.where(row == 0, words_ref[0, 0], jnp.where(row == 1, words_ref[0, 1], words_ref[0, 2]))
    control_ref[...] = jnp.where(iota((8, 128), 1) == 2, words, tiles_ref[...])
    atoms = site_ref.shape[1]
    blocks = atoms // BLOCK
    own = site_ref[...] * axis_scale()[:, 0:1]
    col_ref[...] = upright(own)
    for block in range(blocks):
        row_ref[block] = doubled(own, block)
    chosen_ref[...] = chooser(send_ref[...], atoms).astype(F32).astype(BF16)
    hist_ref[...] = jnp.zeros_like(hist_ref)

    def work(slot, left, right):
        add_histogram(
            col_ref, left, row_ref, right, left == right, col_ref, hist_ref,
            pair_high.at[slot], pair_low.at[slot],
        )

    own_tiles(control_ref, blocks, work)
    for copy in copies:
        copy.wait()

    embed = jnp.where(iota((SPAN, 128), 0) < kinds, weight_ref[0:SPAN, :], 0.0)
    scalar = jnp.concatenate([radial_row(weight_ref, 0, n) * embed for n in range(BASIS)], axis=0)
    vector = jnp.concatenate([radial_row(weight_ref, 1, n) * embed for n in range(BASIS)], axis=0)
    scalar, vector = split(scalar), split(vector)
    to_self = mm3(scalar, split(mixing_ref[0]))
    to_gate = mm3(scalar, split(mixing_ref[2]))
    to_vector = mm3(vector, split(mixing_ref[1]))
    fold_ref[...] = jnp.zeros_like(fold_ref)
    for n in range(BASIS):
        rows = slice(n * SPAN, n * SPAN + SPAN)
        base = n * 4 * SPAN
        fold_ref[base : base + SPAN, 0:128] = to_self[rows]
        fold_ref[base : base + SPAN, 128:256] = to_gate[rows]
        for a in range(3):
            here = base + (a + 1) * SPAN
            fold_ref[here : here + SPAN, (a + 2) * 128 : (a + 3) * 128] = to_vector[rows]
    fold_high[...], fold_low[...] = split(fold_ref[...])
    for part in range(2):
        mix_high[part], mix_low[part] = split(mixing_ref[3 + part])


def first_kernel(
    control_ref,
    send_in,
    hist_in,
    col_ref,
    mate_in,
    far_in,
    zmate_in,
    zfar_in,
    hist_ref,
    mate_ref,
    far_ref,
    side_ref,
    ghost_col,
    ghost_row,
    pair_high,
    pair_low,
    send_ref,
    sem,
):
    fetching = pltpu.make_async_copy(send_in, send_ref, sem)
    fetching.start()
    blocks = hist_in.shape[0] // BLOCK
    even_x, even_y = parities(control_ref)
    ghosts = pick_rows(even_x, even_y, mate_in[...], far_in[...], zmate_in[...], zfar_in[...])
    row = iota((8, 128), 0)
    slot = iota((8, 128), 1) // GHOSTS
    shift_x = jnp.where(slot < 3, -1.0, jnp.where(slot < 5, 0.0, 1.0))
    down = (slot == 0) | (slot == 3) | (slot == 5)
    level = (slot == 1) | (slot == 6)
    shift_y = jnp.where(down, -1.0, jnp.where(level, 0.0, 1.0))
    shift = jnp.where(row == 0, shift_x, jnp.where(row == 1, shift_y, 0.0))
    ghosts = (ghosts + shift) * axis_scale()
    ghost_col[...] = upright(ghosts)
    for block in range(2):
        ghost_row[block] = doubled(ghosts, block)
    hist_ref[...] = hist_in[...]

    def work(slot, left, right):
        add_histogram(
            col_ref, left, ghost_row, right, False, ghost_col, hist_ref,
            pair_high.at[slot], pair_low.at[slot],
        )

    for slot in range(2):
        work(slot, control_ref[slot, 0], slot)
    more_ghost_tiles(control_ref, blocks, work)
    fetching.wait()

    def piece(slot):
        return jnp.concatenate(
            [hist_ref[pl.ds(send_ref[slot, entry], 1), :] for entry in range(GHOSTS)], axis=0
        )

    put_packets(even_x, piece, mate_ref, far_ref, side_ref)


def make_features(block, col_ref, kinds, weight_ref, pre_ref, feat_high, feat_low, scalar_ref):
    rows = block_rows(block)
    kind = col_ref[rows, 3:4].astype(jnp.int32)
    scalar = jnp.zeros((BLOCK, 128), F32)
    for species in range(kinds):
        scalar = jnp.where(kind == species, weight_ref[species : species + 1, :], scalar)
    pre = pre_ref[rows, 0:128]
    scalar = scalar + pre * sigmoid(pre)
    if scalar_ref is not None:
        scalar_ref[rows, :] = scalar
    gate = sigmoid(pre_ref[rows, 128:256])
    parts = [scalar] + [pre_ref[rows, (a + 2) * 128 : (a + 3) * 128] * gate for a in range(3)]
    empty = jnp.zeros((BLOCK, 128), BF16)
    for order, part in enumerate(parts):
        high, low = split(part)
        here = pl.ds(order * BLOCK, BLOCK)
        used = 0 if order == 0 else 128
        for ref, value in ((feat_high, high), (feat_low, low)):
            ref[block, here, used : used + 128] = value
            ref[block, here, 128 - used : 256 - used] = empty


def add_message(left, right, feat_high, feat_low, weight_ref, message_ref, high_ref, low_ref):
    found = mm3((high_ref[...], low_ref[...]), (feat_high[right], feat_low[right]))
    total = jnp.zeros((BLOCK, 128), F32)
    for n in range(BASIS):
        rows = slice(n * BLOCK, n * BLOCK + BLOCK)
        total = total + found[rows, 0:128] * radial_row(weight_ref, 2, n)
        total = total + found[rows, 128:256] * radial_row(weight_ref, 3, n)
    message_ref[block_rows(left), :] += total


def feature_kernel(
    kinds,
    hist_ref,
    col_ref,
    fold_high,
    fold_low,
    weight_ref,
    pre_ref,
    feat_high,
    feat_low,
    scalar_ref,
):
    blocks = hist_ref.shape[0] // BLOCK
    pre_ref[...] = mm3(split(hist_ref[...]), (fold_high[...], fold_low[...]))

    def features(block, carried):
        make_features(block, col_ref, kinds, weight_ref, pre_ref, feat_high, feat_low, scalar_ref)
        return carried

    lax.fori_loop(0, blocks, features, 0)


def message_kernel(
    control_ref,
    row_ref,
    ghost_col,
    weight_ref,
    feat_high,
    feat_low,
    pair_high,
    pair_low,
    message_ref,
    swap_high,
    swap_low,
):
    blocks = feat_high.shape[0]
    message_ref[...] = jnp.zeros_like(message_ref)

    def work(slot, left, right):
        add_message(
            left, right, feat_high, feat_low, weight_ref, message_ref,
            pair_high.at[slot], pair_low.at[slot],
        )

    own_tiles(control_ref, blocks, work)

    def swapped(slot, left, right):
        pair_swapped(
            ghost_col, right, row_ref, left, False, swap_high.at[slot], swap_low.at[slot]
        )

    for slot in range(2):
        swapped(slot, control_ref[slot, 0], slot)
    more_ghost_tiles(control_ref, blocks, swapped)


def weighted_pull(cotangent, weight_ref, path):
    return split(
        jnp.concatenate([cotangent * radial_row(weight_ref, path, n) for n in range(BASIS)], axis=0)
    )


def add_feature_pull(right, cotangent, weight_ref, grad_feat, swap_high, swap_low):
    to_scalar = mm3(
        (swap_high[0:BLOCK, :], swap_low[0:BLOCK, :]), weighted_pull(cotangent, weight_ref, 2)
    )
    to_vector = mm3(
        (swap_high[BLOCK:, :], swap_low[BLOCK:, :]), weighted_pull(cotangent, weight_ref, 3)
    )
    rows = block_rows(right)
    grad_feat[rows, 0:128] += to_scalar
    for a in range(3):
        grad_feat[rows, (a + 1) * 128 : (a + 2) * 128] += to_vector[a * BLOCK : (a + 1) * BLOCK]


def finish(message, scalar, mix_high, mix_low, weight_ref):
    mix_message, mix_hidden = (mix_high[0], mix_low[0]), (mix_high[1], mix_low[1])
    readout = readout_row(weight_ref)
    mixed = mm3(split(message), mix_message)
    mixed_gate = sigmoid(mixed)
    final = scalar + mixed * mixed_gate
    hidden = mm3(split(final), mix_hidden)
    hidden_gate = sigmoid(hidden)
    pull_hidden = readout * (hidden_gate * (1.0 + hidden * (1.0 - hidden_gate)))
    pull_final = mm3(split(pull_hidden), mix_hidden, ROWROW)
    pull_mixed = pull_final * (mixed_gate * (1.0 + mixed * (1.0 - mixed_gate)))
    pull_message = mm3(split(pull_mixed), mix_message, ROWROW)
    return hidden * hidden_gate * readout, pull_final, pull_message


def pull_features(grad_feat, pre_ref):
    by_scalar = grad_feat[:, 0:128]
    pre = pre_ref[:, 0:128]
    own_gate = sigmoid(pre)
    gate = sigmoid(pre_ref[:, 128:256])
    by_gate = jnp.zeros_like(gate)
    by_vector = []
    for a in range(3):
        pulled = grad_feat[:, (a + 1) * 128 : (a + 2) * 128]
        by_gate = by_gate + pulled * pre_ref[:, (a + 2) * 128 : (a + 3) * 128]
        by_vector.append(pulled * gate)
    by_pre = by_scalar * (own_gate * (1.0 + pre * (1.0 - own_gate)))
    return jnp.concatenate([by_pre, by_gate * gate * (1.0 - gate)] + by_vector, axis=1)


def second_ghost_kernel(
    kinds,
    control_ref,
    mate_in,
    far_in,
    zmate_in,
    zfar_in,
    ghost_col,
    fold_high,
    fold_low,
    mix_high,
    mix_low,
    weight_ref,
    scalar_ref,
    message_in,
    pair_high,
    pair_low,
    swap_high,
    swap_low,
    mate_ref,
    far_ref,
    side_ref,
    feat_high,
    feat_low,
    message_ref,
    pre_ref,
    grad_feat,
):
    blocks = scalar_ref.shape[0] // BLOCK
    even_x, even_y = parities(control_ref)
    fold = (fold_high[...], fold_low[...])
    ghost_hist = pick_all((even_x, even_y, mate_in, far_in, zmate_in, zfar_in))
    pre_ref[...] = mm3(split(ghost_hist), fold)
    for block in range(2):
        make_features(block, ghost_col, kinds, weight_ref, pre_ref, feat_high, feat_low, None)
    message_ref[...] = message_in[...]

    def forward(slot, left, right):
        add_message(
            left, right, feat_high, feat_low, weight_ref, message_ref,
            pair_high.at[slot], pair_low.at[slot],
        )

    lefts = [control_ref[slot, 0] for slot in range(2)]
    for slot in range(2):
        forward(slot, lefts[slot], slot)
    more_ghost_tiles(control_ref, blocks, forward)

    grad_feat[...] = jnp.zeros_like(grad_feat)

    def backward(slot, right, cotangent):
        add_feature_pull(
            right, cotangent, weight_ref, grad_feat, swap_high.at[slot], swap_low.at[slot]
        )

    def finished(rows):
        take = lambda ref: jnp.concatenate([ref[row, :] for row in rows], axis=0)
        return finish(take(message_ref), take(scalar_ref), mix_high, mix_low, weight_ref)[2]

    pulled = finished([block_rows(left) for left in lefts])
    for slot in range(2):
        backward(slot, slot, pulled[slot * BLOCK : slot * BLOCK + BLOCK])
    more_ghost_tiles(
        control_ref,
        blocks,
        lambda slot, left, right: backward(slot, right, finished([block_rows(left)])),
    )

    ghost_pull = mm3(split(pull_features(grad_feat, pre_ref)), fold, ROWROW)
    put_packets(
        even_x,
        lambda slot: ghost_pull[slot * GHOSTS : slot * GHOSTS + GHOSTS],
        mate_ref,
        far_ref,
        side_ref,
    )


def second_pull_kernel(
    control_ref,
    col_ref,
    row_ref,
    mix_high,
    mix_low,
    weight_ref,
    scalar_ref,
    message_ref,
    grad_feat,
    pull_message,
    share_ref,
    swap_high,
    swap_low,
):
    blocks = scalar_ref.shape[0] // BLOCK
    share, direct, pulled = finish(
        message_ref[...], scalar_ref[...], mix_high, mix_low, weight_ref
    )
    share_ref[...] = share
    pull_message[...] = pulled
    grad_feat[:, 0:128] = direct
    grad_feat[:, 128:512] = jnp.zeros((blocks * BLOCK, 384), F32)

    def backward(slot, left, right):
        pair_swapped(col_ref, right, row_ref, left, left == right, swap_high, swap_low)
        cotangent = pull_message[block_rows(left), :]
        add_feature_pull(right, cotangent, weight_ref, grad_feat, swap_high, swap_low)

    own_tiles(control_ref, blocks, backward)


def pair_pull(left, right, pull_message, weight_ref, high_ref, low_ref):
    cotangent = pull_message[block_rows(left), :]
    first = weighted_pull(cotangent, weight_ref, 2)
    second = weighted_pull(cotangent, weight_ref, 3)
    both = [jnp.concatenate([first[part], second[part]], axis=1) for part in range(2)]
    return mm3(both, (high_ref[right], low_ref[right]), ROWROW)


def ghost_pair_kernel(
    control_ref,
    fold_high,
    fold_low,
    weight_ref,
    pre_ref,
    grad_feat,
    pull_message,
    ghost_high,
    ghost_low,
    pull_hist_ref,
    pull_ref,
):
    blocks = pre_ref.shape[0] // BLOCK
    pulled = pull_features(grad_feat, pre_ref)
    pull_hist_ref[...] = mm3(split(pulled), (fold_high[...], fold_low[...]), ROWROW)

    def work(slot, left, right):
        pull_ref[slot] = pair_pull(left, right, pull_message, weight_ref, ghost_high, ghost_low)

    for slot in range(2):
        work(slot, control_ref[slot, 0], slot)
    more_ghost_tiles(control_ref, blocks, work)


def own_pair_kernel(
    control_ref, weight_ref, pull_message, share_ref, feat_high, feat_low, pull_ref, energy_ref
):
    energy_ref[...] = jnp.sum(share_ref[...].T, axis=0, keepdims=True)

    def work(slot, left, right):
        pull_ref[slot] = pair_pull(left, right, pull_message, weight_ref, feat_high, feat_low)

    own_tiles(control_ref, feat_high.shape[0], work)


def both_pulls(total_ref, left, kind_ref, right, pull_in, pull_ref):
    lane_basis = iota((1, 128), 1) // (4 * SPAN)
    parts = []
    for half in range(2):
        here = total_ref[block_rows(left), half * 128 : half * 128 + 128]
        parts += [jnp.where(lane_basis == n, here, 0.0) for n in range(4)]
    high, low = split(jnp.concatenate(parts, axis=0))
    table = kind_table(kind_ref, right)
    pull_ref[...] = pull_in[...] + mm(high, table, ROWROW) + mm(low, table, ROWROW)


def third_ghost_kernel(
    control_ref,
    chosen_ref,
    pull_hist_ref,
    mate_in,
    far_in,
    zmate_in,
    zfar_in,
    col_ref,
    ghost_col,
    ghost_row,
    pull_in,
    out_ref,
    total_ref,
    grad_col,
    grad_ghost,
    pull_refs,
):
    blocks = pull_hist_ref.shape[0] // BLOCK
    even_x, even_y = parities(control_ref)
    returned = split(pick_all((even_x, even_y, mate_in, far_in, zmate_in, zfar_in)))
    chosen = chosen_ref[...]
    total_ref[...] = pull_hist_ref[...] + mm(chosen, returned[0]) + mm(chosen, returned[1])
    grad_ghost[...] = jnp.zeros_like(grad_ghost)
    grad_col[...] = jnp.zeros_like(grad_col)

    def work(slot, left, right, part=0):
        pull_ref = pull_refs.at[part]
        both_pulls(total_ref, left, ghost_col, right, pull_in.at[slot], pull_ref)
        pair_backward(col_ref, left, ghost_row, right, False, pull_ref, grad_ghost, grad_col)

    for slot in range(2):
        work(slot, control_ref[slot, 0], slot, slot)
    more_ghost_tiles(control_ref, blocks, work)
    out_ref[...] = jnp.where(low_half(), grad_ghost[0], grad_ghost[1])


def third_own_kernel(
    control_ref,
    chosen_ref,
    total_ref,
    col_ref,
    row_ref,
    pull_in,
    grad_col_in,
    own_ref,
    turned_ref,
    grad_row,
    grad_col,
    pull_ref,
):
    blocks = total_ref.shape[0] // BLOCK
    turned_ref[...] = chosen_ref[...].astype(F32).T.astype(BF16)
    grad_row[...] = jnp.zeros_like(grad_row)
    grad_col[...] = grad_col_in[...]

    def work(slot, left, right):
        both_pulls(total_ref, left, col_ref, right, pull_in.at[slot], pull_ref)
        pair_backward(col_ref, left, row_ref, right, left == right, pull_ref, grad_row, grad_col)

    own_tiles(control_ref, blocks, work)
    low = low_half()
    by_sender = jnp.concatenate(
        [jnp.where(low, grad_row[2 * k], grad_row[2 * k + 1]) for k in range(blocks // 2)], axis=1
    )
    own_ref[...] = by_sender + grad_col[...].T[0:8]


def last_kernel(control_ref, turned_ref, own_ref, mate_in, far_in, zmate_in, zfar_in, force_ref):
    even_x, even_y = parities(control_ref)
    returned = pick_rows(even_x, even_y, mate_in[...], far_in[...], zmate_in[...], zfar_in[...])
    total = own_ref[...] + exact_pick(returned, turned_ref[...])
    force_ref[...] = -total[0:3]


def partners(axis, far):
    count = lax.axis_size(axis)
    if far:
        return [(i, (i + (1 if i % 2 else -1)) % count) for i in range(count)]
    return [(i, i ^ 1) for i in range(count)]


def swap_both(axis, to_mate, to_far):
    to_mate, to_far = lax.optimization_barrier((to_mate, to_far))
    mate = lax.ppermute(to_mate, axis, partners(axis, False))
    far = lax.ppermute(to_far, axis, partners(axis, True))
    return lax.optimization_barrier((mate, far))


def exchange_rows(rows, beside):
    mate, far = swap_both("gx", rows, rows)
    mate, far, beside = lax.optimization_barrier((mate, far, beside))
    column = jnp.stack([rows, mate, far])
    zmate, zfar = swap_both("gy", column, column)
    return (mate, far, zmate, zfar), beside


def exchange_packets(even_y, to_mate, to_far, side, beside):
    mate, far = swap_both("gx", to_mate, to_far)
    mate, far, beside = lax.optimization_barrier((mate, far, beside))
    up = jnp.concatenate([mate[2:3], far[2:3], side[1:2]], axis=0)
    down = jnp.concatenate([mate[0:1], far[0:1], side[0:1]], axis=0)
    zmate, zfar = swap_both("gy", jnp.where(even_y, up, down), jnp.where(even_y, down, up))
    return (mate, far, zmate, zfar), beside


def struct(*shape, dtype=F32):
    return jax.ShapeDtypeStruct(shape, dtype)


def call(kernel, in_specs, outs, scratch=()):
    return pl.pallas_call(
        kernel,
        in_specs=in_specs,
        out_specs=jax.tree.map(lambda _: VMEM, outs),
        out_shape=outs,
        scratch_shapes=list(scratch),
        compiler_params=PARAMS,
    )


def shards(fractions, species, send_list, tile_list, counts, embedding, radial, mixing, readout):
    atoms = fractions.shape[1]
    blocks = atoms // BLOCK
    kinds = embedding.shape[0]
    slots = tile_list.shape[1]
    parity = [lax.axis_index("gx") % 2, lax.axis_index("gy") % 2]
    even_y = parity[1] == 0
    words = jnp.stack([counts[0], *parity]).astype(jnp.int32)[None]
    far_arrays = [
        pltpu.with_memory_space_constraint(array, pltpu.HBM)
        for array in (
            fractions,
            species[None],
            send_list,
            tile_list,
            embedding,
            radial.reshape(-1, radial.shape[2]),
            readout[None],
            mixing,
        )
    ]
    packets = [struct(3, GHOSTS, HIST), struct(3, GHOSTS, HIST), struct(2, GHOSTS, HIST)]
    hist_struct = struct(atoms, HIST)
    col_struct = struct(atoms, 128)
    own_rows, ghost_rows = struct(blocks, 8, 128), struct(2, 8, 128)
    fold_halves = [struct(HIST, 640, dtype=BF16)] * 2
    mix_halves = [struct(2, 128, 128, dtype=BF16)] * 2
    own_halves = [struct(blocks, 256, 256, dtype=BF16)] * 2
    ghost_halves = [struct(2, 256, 256, dtype=BF16)] * 2
    pairs = [struct(slots, BASIS * BLOCK, 256, dtype=BF16)] * 2
    swaps = [struct(slots, 256, BASIS * BLOCK, dtype=BF16)] * 2
    pulls = struct(slots, BASIS * BLOCK, 256)

    site, rows, send, tiles = call(
        pack_kernel,
        [HBM] * 4,
        [
            struct(8, atoms), struct(8, 128),
            struct(*send_list.shape, dtype=jnp.int32), struct(8, 128, dtype=jnp.int32),
        ],
        [
            pltpu.VMEM(fractions.shape, F32),
            pltpu.VMEM((1, atoms), jnp.int32),
            pltpu.VMEM(tile_list.shape, jnp.int32),
            pltpu.SemaphoreType.DMA((4,)),
        ],
    )(*far_arrays[0:4])
    arrived, (words, site) = exchange_rows(rows, (words, site))
    control, col, row, hist, own_high, own_low, fold_high, fold_low, chosen, *rest = call(
        prepare_kernel,
        [VMEM] * 4 + [HBM] * 4,
        [struct(8, 128, dtype=jnp.int32), col_struct, own_rows, hist_struct]
        + pairs
        + fold_halves
        + [struct(atoms, 128, dtype=BF16)]
        + mix_halves
        + [struct(2 * SPAN + 4 * BASIS, 128)],
        [
            pltpu.VMEM((HIST, 640), F32),
            pltpu.VMEM(mixing.shape, F32),
            pltpu.SemaphoreType.DMA((4,)),
        ],
    )(words, tiles, site, send, *far_arrays[4:])
    mix_high, mix_low, weights = rest
    fold, mix = (fold_high, fold_low), (mix_high, mix_low)
    hist, to_mate, to_far, side, ghost_col, ghost_row, pair_high, pair_low = call(
        first_kernel,
        [VMEM] * 8,
        [hist_struct] + packets + [struct(8 * GHOSTS, 128), ghost_rows] + pairs,
        [pltpu.SMEM(send_list.shape, jnp.int32), pltpu.SemaphoreType.DMA],
    )(control, send, hist, col, *arrived)
    features = call(
        functools.partial(feature_kernel, kinds),
        [VMEM] * 5,
        [struct(atoms, 640)] + own_halves + [col_struct],
    )(hist, col, *fold, weights)
    arrived, features = exchange_packets(even_y, to_mate, to_far, side, features)
    pre, feat_high, feat_low, scalar = features
    message, swap_high, swap_low = call(message_kernel, [VMEM] * 8, [col_struct] + swaps)(
        control, row, ghost_col, weights, feat_high, feat_low, own_high, own_low
    )
    to_mate, to_far, side, ghost_high, ghost_low, message = call(
        functools.partial(second_ghost_kernel, kinds),
        [VMEM] * 17,
        packets + ghost_halves + [col_struct],
        [pltpu.VMEM((8 * GHOSTS, 640), F32), pltpu.VMEM((8 * GHOSTS, 512), F32)],
    )(
        control, *arrived, ghost_col, *fold, *mix, weights, scalar, message,
        pair_high, pair_low, swap_high, swap_low,
    )
    second_pull = call(
        second_pull_kernel,
        [VMEM] * 8,
        [struct(atoms, 512), col_struct, col_struct],
        [pltpu.VMEM((256, BASIS * BLOCK), BF16)] * 2,
    )(control, col, row, *mix, weights, scalar, message)
    arrived, second_pull = exchange_packets(even_y, to_mate, to_far, side, second_pull)
    grad_feat, pull_message, share = second_pull
    pull_hist, pull = call(ghost_pair_kernel, [VMEM] * 9, [hist_struct, pulls])(
        control, *fold, weights, pre, grad_feat, pull_message, ghost_high, ghost_low
    )
    rows, total, grad_col = call(
        third_ghost_kernel,
        [VMEM] * 11,
        [struct(8, 128), hist_struct, col_struct],
        [pltpu.VMEM((2, 8, 128), F32), pltpu.VMEM((2, BASIS * BLOCK, 256), F32)],
    )(control, chosen, pull_hist, *arrived, col, ghost_col, ghost_row, pull)
    share, rows = lax.optimization_barrier((share, rows))
    own_pair = call(own_pair_kernel, [VMEM] * 6, [pulls, struct(1, atoms)])(
        control, weights, pull_message, share, feat_high, feat_low
    )
    arrived, own_pair = exchange_rows(rows, own_pair)
    pull, energy = own_pair
    own, turned = call(
        third_own_kernel,
        [VMEM] * 7,
        [struct(8, atoms), struct(128, atoms, dtype=BF16)],
        [
            pltpu.VMEM((blocks, 8, 128), F32),
            pltpu.VMEM((atoms, 128), F32),
            pltpu.VMEM((BASIS * BLOCK, 256), F32),
        ],
    )(control, chosen, total, col, row, pull, grad_col)
    forces = call(last_kernel, [VMEM] * 7, struct(3, atoms))(control, turned, own, *arrived)
    return energy[0], forces


def solution(mesh):
    placed = (
        P(None, ("gx", "gy")),
        P(("gx", "gy")),
        P(None, ("gx", "gy")),
        P(None, ("gx", "gy")),
        P(("gx", "gy")),
        P(),
        P(),
        P(),
        P(),
    )
    return jax.shard_map(
        shards,
        mesh=mesh,
        in_specs=placed,
        out_specs=(P(("gx", "gy")), P(None, ("gx", "gy"))),
        check_vma=False,
    )
```

time: 71 us -> 54.4 us (0.77)
  the two profiles are of different devices: /device:TPU:4 before, /device:TPU:0 now
where the time goes in v1:
time: 54.4 us; the launch traced here: 53.4 us
  starting transfers between devices  26.6 us (49%)
  Pallas kernels  13.7 us (25%)
  waiting for transfers between devices  11.5 us (21%)
  between operations  1.43 us (3%)
    ppermute x8, starting transfers between devices, swap_both(): far = lax.ppermute(to_far, axis, partners(axis, True))  22.8 us
    ppermute x8, waiting for transfers between devices, swap_both(): far = lax.ppermute(to_far, axis, partners(axis, True))  10.9 us
    ppermute x8, starting transfers between devices, swap_both(): mate = lax.ppermute(to_mate, axis, partners(axis, False))  3.85 us
    pallas_call x1, Pallas kernels, shards(): call(functools.partial(second_ghost_kernel, kinds), [VMEM] * 17, packets...  2.68 us
    pallas_call x1, Pallas kernels, shards(): call(functools.partial(feature_kernel, kinds), [VMEM] * 5, [struct(atoms,...  1.87 us
    pallas_call x1, Pallas kernels, shards(): call(prepare_kernel, [VMEM] * 4 + [HBM] * 4, [struct(8, 128, dtype=jnp.in...  1.35 us
    pallas_call x1, Pallas kernels, shards(): call(ghost_pair_kernel, [VMEM] * 9, [hist_struct, pulls])  1.29 us
    pallas_call x1, Pallas kernels, shards(): call(first_kernel, [VMEM] * 8, [hist_struct] + packets + [struct(8 * GHOS...  1.22 us
  transfers between devices with their start and end apart: 16, of which 9 were waited for; matrix products, arithmetic and copies ran while one was open for 0% of the time, Pallas kernels for 13%

profile of v1, /device:TPU:0, one launch (start us, length us, event | category | flops | bytes accessed | tf_op | source)
XLA Modules:
  0.0 53.4 jit_solution(2096498088066086026)
XLA Ops:
  0.6 1.0 %shard_map.104 = (f32[8,512]{1,0:T(8,128)S(1)}, f32[8,128]{1,0:T(8,128)S(1)}, s32[8,16]{1,0:T(8,128)S(1)}, s32[8,128]{1,0:T(8,128)S(1)}) custom-call(f32[3,512]{1,0:T(4,128)} %frac_in.1, s32[1,512]{1,0:T(1,128)} %bitcast.21, s32[8,16]{1,0:T(8,128)} %send_in.1, s32[2,6]{1,0:T(2,128)} %tile_in.1), custom_call_target="tpu_custom_call" | custom-call | tf_op jit(solution)/shard_map/pallas_call | solution.py:963
  1.6 0.5 collective-permute-start
  2.1 3.6 %collective-permute-start.1 = (f32[8,128]{1,0:T(8,128)S(1)}, f32[8,128]{1,0:T(8,128)S(1)}, u32[]{:S(2)}, u32[]{:S(2)}) collective-permute-start(f32[8,128]{1,0:T(8,128)S(1)} %get-tuple-element.106), channel_id=1, source_target_pairs={{0,28},{4,8},{8,4},{12,16},{16,12},{20,24},{24,20},{28,0},{1,29},{... | collective-permute-start | bytes 12296 | tf_op jit(solution)/shard_map/ppermute | solution.py:894
  6.4 0.1 add_bitcast_fusion.words_ref
  6.4 0.0 collective-permute-done.mate_in
  6.4 0.6 %collective-permute-done.1.far_in = f32[8,128]{1,0:T(8,128)S(1)} collective-permute-done((f32[8,128]{1,0:T(8,128)S(1)}, f32[8,128]{1,0:T(8,128)S(1)}, u32[]{:S(2)}, u32[]{:S(2)}) %collective-permute-start.1) | collective-permute-done | bytes 4128 | tf_op jit(solution)/shard_map/ppermute | solution.py:894
  7.0 1.7 %collective-permute-start.2 = (f32[3,8,128]{2,1,0:T(8,128)S(1)}, f32[3,8,128]{2,1,0:T(8,128)S(1)}, u32[]{:S(2)}, u32[]{:S(2)}) collective-permute-start(f32[3,8,128]{2,1,0:T(8,128)S(1)} %pad_maximum_fusion.4), channel_id=1, source_target_pairs={{0,1},{1,0},{2,3},{3,2},{4,5},{5,4},{6,7},{7,6},{8,9},{9,8},{10,11... | collective-permute-start | bytes 36872 | tf_op jit(solution)/shard_map/ppermute | solution.py:893
  8.7 2.5 %collective-permute-start.3 = (f32[3,8,128]{2,1,0:T(8,128)S(1)}, f32[3,8,128]{2,1,0:T(8,128)S(1)}, u32[]{:S(2)}, u32[]{:S(2)}) collective-permute-start(f32[3,8,128]{2,1,0:T(8,128)S(1)} %pad_maximum_fusion.4), channel_id=1, source_target_pairs={{0,3},{1,2},{2,1},{3,0},{4,7},{5,6},{6,5},{7,4},{8,11},{9,10},{10,... | collective-permute-start | bytes 36872 | tf_op jit(solution)/shard_map/ppermute | solution.py:894
  11.2 1.4 %shard_map.105 = (s32[8,128]{1,0:T(8,128)S(1)}, f32[512,128]{1,0:T(8,128)S(1)}, f32[8,8,128]{2,1,0:T(8,128)S(1)}, f32[512,256]{1,0:T(8,128)S(1)}, bf16[6,512,256...) custom-call(s32[1,3]{1,0:T(1,128)S(1)} %add_bitcast_fusion.words_ref, ...), custom_call_target="tpu_custom_call" | custom-call | tf_op jit(solution)/shard_map/pallas_call | solution.py:978
  12.6 0.0 collective-permute-done.2.zmate_in
  12.6 1.6 %collective-permute-done.3.zfar_in = f32[3,8,128]{2,1,0:T(8,128)S(1)} collective-permute-done((f32[3,8,128]{2,1,0:T(8,128)S(1)}, f32[3,8,128]{2,1,0:T(8,128)S(1)}, u32[]{:S(2)}, u32[]{:S(2)}) %collective-permute-start.3) | collective-permute-done | bytes 12320 | tf_op jit(solution)/shard_map/ppermute | solution.py:894
  14.2 1.2 %shard_map.106 = (f32[512,256]{1,0:T(8,128)S(1)}, f32[3,16,256]{2,1,0:T(8,128)S(1)}, f32[3,16,256]{2,1,0:T(8,128)S(1)}, f32[2,16,256]{2,1,0:T(8,128)S(1)}, f32[1...) custom-call(s32[8,128]{1,0:T(8,128)S(1)} %get-tuple-element.114.cont, ...), custom_call_target="tpu_custom_call" | custom-call | tf_op jit(solution)/shard_map/pallas_call | solution.py:995
  15.5 0.1 collective-permute-start.4
  15.5 1.8 %collective-permute-start.5 = (f32[3,16,256]{2,1,0:T(8,128)S(1)}, f32[3,16,256]{2,1,0:T(8,128)S(1)}, u32[]{:S(2)}, u32[]{:S(2)}) collective-permute-start(f32[3,16,256]{2,1,0:T(8,128)S(1)} %get-tuple-element.126), channel_id=1, source_target_pairs={{0,28},{4,8},{8,4},{12,16},{16,12},{20,24},{24,20},{28,0},{1,29},{... | collective-permute-start | bytes 147464 | tf_op jit(solution)/shard_map/ppermute | solution.py:894
  17.3 1.9 %shard_map.107 = (f32[512,640]{1,0:T(8,128)S(1)}, bf16[8,256,256]{2,1,0:T(8,128)(2,1)S(1)}, bf16[8,256,256]{2,1,0:T(8,128)(2,1)S(1)}, f32[512,128]{1,0:T(8,128)S(1)}) custom-call(f32[512,256]{1,0:T(8,128)S(1)} %get-tuple-element.129.hist_ref, f32[512,128]{1,0:T(8,128)S(1)} %get-tuple-element.116.col_ref, bf16[256,640]{1,0:T(8,128)(2,1)S(1)} %get-tuple-element.130.fold_high, ...), custom_call_target="tpu_custom_call" | custom-call | tf_op jit(solution)/shard_map/pallas_call | solution.py:1001
  19.2 0.0 collective-permute-done.4.mate_in
  19.2 0.8 %collective-permute-done.5.far_in = f32[3,16,256]{2,1,0:T(8,128)S(1)} collective-permute-done((f32[3,16,256]{2,1,0:T(8,128)S(1)}, f32[3,16,256]{2,1,0:T(8,128)S(1)}, u32[]{:S(2)}, u32[]{:S(2)}) %collective-permute-start.5) | collective-permute-done | bytes 49184 | tf_op jit(solution)/shard_map/ppermute | solution.py:894
  20.0 0.1 collective-permute-start.6
  20.1 2.9 %collective-permute-start.7 = (f32[3,16,256]{2,1,0:T(8,128)S(1)}, f32[3,16,256]{2,1,0:T(8,128)S(1)}, u32[]{:S(2)}, u32[]{:S(2)}) collective-permute-start(f32[3,16,256]{2,1,0:T(8,128)S(1)} %get-tuple-element.141), channel_id=1, source_target_pairs={{0,3},{1,2},{2,1},{3,0},{4,7},{5,6},{6,5},{7,4},{8,11},{9,10},{10,... | collective-permute-start | bytes 147464 | tf_op jit(solution)/shard_map/ppermute | solution.py:894
  23.0 0.5 shard_map.108
  23.6 0.6 %collective-permute-done.6.zmate_in = f32[3,16,256]{2,1,0:T(8,128)S(1)} collective-permute-done((f32[3,16,256]{2,1,0:T(8,128)S(1)}, f32[3,16,256]{2,1,0:T(8,128)S(1)}, u32[]{:S(2)}, u32[]{:S(2)}) %collective-permute-start.6) | collective-permute-done | bytes 49184 | tf_op jit(solution)/shard_map/ppermute | solution.py:893
  24.2 2.0 %collective-permute-done.7.zfar_in = f32[3,16,256]{2,1,0:T(8,128)S(1)} collective-permute-done((f32[3,16,256]{2,1,0:T(8,128)S(1)}, f32[3,16,256]{2,1,0:T(8,128)S(1)}, u32[]{:S(2)}, u32[]{:S(2)}) %collective-permute-start.7) | collective-permute-done | bytes 49184 | tf_op jit(solution)/shard_map/ppermute | solution.py:894
  26.2 2.7 %shard_map.109 = (f32[3,16,256]{2,1,0:T(8,128)S(1)}, f32[3,16,256]{2,1,0:T(8,128)S(1)}, f32[2,16,256]{2,1,0:T(8,128)S(1)}, bf16[2,256,256]{2,1,0:T(8,128)(2,1)S(...) custom-call(s32[8,128]{1,0:T(8,128)S(1)} %get-tuple-element.114.control_ref, ...), custom_call_target="tpu_custom_call" | custom-call | tf_op jit(solution)/shard_map/pallas_call | solution.py:1011
  28.9 0.1 collective-permute-start.8
  28.9 1.6 %collective-permute-start.9 = (f32[3,16,256]{2,1,0:T(8,128)S(1)}, f32[3,16,256]{2,1,0:T(8,128)S(1)}, u32[]{:S(2)}, u32[]{:S(2)}) collective-permute-start(f32[3,16,256]{2,1,0:T(8,128)S(1)} %get-tuple-element.161), channel_id=1, source_target_pairs={{0,28},{4,8},{8,4},{12,16},{16,12},{20,24},{24,20},{28,0},{1,29},{... | collective-permute-start | bytes 147464 | tf_op jit(solution)/shard_map/ppermute | solution.py:894
  30.5 0.7 %shard_map.110 = (f32[512,512]{1,0:T(8,128)S(1)}, f32[512,128]{1,0:T(8,128)S(1)}, f32[512,128]{1,0:T(8,128)S(1)}) custom-call(s32[8,128]{1,0:T(8,128)S(1)} %get-tuple-element.114.control_ref, f32[512,128]{1,0:T(8,128)S(1)} %get-tuple-element.116.col_ref, f32[8,8,128]{2,1,0:T(8,128)S(1)} %get-tuple-element.148.row_ref, ...), custom_call_target="tpu_custom_call" | custom-call | tf_op jit(solution)/shard_map/pallas_call | solution.py:1020
  31.2 0.0 collective-permute-done.8.mate_in
  31.2 2.2 %collective-permute-done.9.far_in = f32[3,16,256]{2,1,0:T(8,128)S(1)} collective-permute-done((f32[3,16,256]{2,1,0:T(8,128)S(1)}, f32[3,16,256]{2,1,0:T(8,128)S(1)}, u32[]{:S(2)}, u32[]{:S(2)}) %collective-permute-start.9) | collective-permute-done | bytes 49184 | tf_op jit(solution)/shard_map/ppermute | solution.py:894
  33.4 0.7 %collective-permute-start.10 = (f32[3,16,256]{2,1,0:T(8,128)S(1)}, f32[3,16,256]{2,1,0:T(8,128)S(1)}, u32[]{:S(2)}, u32[]{:S(2)}) collective-permute-start(f32[3,16,256]{2,1,0:T(8,128)S(1)} %get-tuple-element.179), channel_id=1, source_target_pairs={{0,1},{1,0},{2,3},{3,2},{4,5},{5,4},{6,7},{7,6},{8,9},{9,8},{10,11... | collective-permute-start | bytes 147464 | tf_op jit(solution)/shard_map/ppermute | solution.py:893
  34.1 3.4 %collective-permute-start.11 = (f32[3,16,256]{2,1,0:T(8,128)S(1)}, f32[3,16,256]{2,1,0:T(8,128)S(1)}, u32[]{:S(2)}, u32[]{:S(2)}) collective-permute-start(f32[3,16,256]{2,1,0:T(8,128)S(1)} %get-tuple-element.180), channel_id=1, source_target_pairs={{0,3},{1,2},{2,1},{3,0},{4,7},{5,6},{6,5},{7,4},{8,11},{9,10},{10,... | collective-permute-start | bytes 147464 | tf_op jit(solution)/shard_map/ppermute | solution.py:894
  37.6 1.3 %shard_map.111 = (f32[512,256]{1,0:T(8,128)S(1)}, f32[6,512,256]{2,1,0:T(8,128)S(1)}) custom-call(s32[8,128]{1,0:T(8,128)S(1)} %get-tuple-element.114.control_ref, bf16[256,640]{1,0:T(8,128)(2,1)S(1)} %get-tuple-element.130.fold_high, bf16[256,640]{1,0:T(8,128)(2,1)S(1)} %get-tuple-element.131.fold_low, f32[48,128]{1,0:T(8,128)S(1)} %get-tuple-element.132.weight_ref, ...), custom_call_target="tpu_custom_call" | custom-call | tf_op jit(solution)/shard_map/pallas_call | solution.py:1028
  38.9 0.0 collective-permute-done.10.zmate_in
  38.9 1.3 %collective-permute-done.11.zfar_in = f32[3,16,256]{2,1,0:T(8,128)S(1)} collective-permute-done((f32[3,16,256]{2,1,0:T(8,128)S(1)}, f32[3,16,256]{2,1,0:T(8,128)S(1)}, u32[]{:S(2)}, u32[]{:S(2)}) %collective-permute-start.11) | collective-permute-done | bytes 49184 | tf_op jit(solution)/shard_map/ppermute | solution.py:894
  40.2 1.1 %shard_map.112 = (f32[8,128]{1,0:T(8,128)S(1)}, f32[512,256]{1,0:T(8,128)S(1)}, f32[512,128]{1,0:T(8,128)S(1)}) custom-call(s32[8,128]{1,0:T(8,128)S(1)} %get-tuple-element.114.control_ref, bf16[512,128]{1,0:T(8,128)(2,1)S(1)} %get-tuple-element.169.chosen_ref, f32[512,256]{1,0:T(8,128)S(1)} %get-tuple-element.175.pull_hist_ref, ...), custom_call_target="tpu_custom_call" | custom-call | tf_op jit(solution)/shard_map/pallas_call | solution.py:1031
  41.3 0.1 collective-permute-start.12
  41.4 2.4 %collective-permute-start.13 = (f32[8,128]{1,0:T(8,128)S(1)}, f32[8,128]{1,0:T(8,128)S(1)}, u32[]{:S(2)}, u32[]{:S(2)}) collective-permute-start(f32[8,128]{1,0:T(8,128)S(1)} %get-tuple-element.188), channel_id=1, source_target_pairs={{0,28},{4,8},{8,4},{12,16},{16,12},{20,24},{24,20},{28,0},{1,29},{... | collective-permute-start | bytes 12296 | tf_op jit(solution)/shard_map/ppermute | solution.py:894
  43.8 0.7 %shard_map.113 = (f32[6,512,256]{2,1,0:T(8,128)S(1)}, f32[1,512]{1,0:T(1,128)}) custom-call(s32[8,128]{1,0:T(8,128)S(1)} %get-tuple-element.114.control_ref, f32[48,128]{1,0:T(8,128)S(1)} %get-tuple-element.132.weight_ref, f32[512,128]{1,0:T(8,128)S(1)} %get-tuple-element.172.pull_message, f32[512,128]{1,0:T(8,128)S(1)} %get-tuple-element.191.share_ref, ...), custom_call_target="tpu_custom_call" | custom-call | tf_op jit(solution)/shard_map/pallas_call | solution.py:1038
  44.6 0.0 collective-permute-done.12.mate_in
  44.6 0.9 %collective-permute-done.13.far_in = f32[8,128]{1,0:T(8,128)S(1)} collective-permute-done((f32[8,128]{1,0:T(8,128)S(1)}, f32[8,128]{1,0:T(8,128)S(1)}, u32[]{:S(2)}, u32[]{:S(2)}) %collective-permute-start.13) | collective-permute-done | bytes 4128 | tf_op jit(solution)/shard_map/ppermute | solution.py:894
  45.4 0.6 %collective-permute-start.14 = (f32[3,8,128]{2,1,0:T(8,128)S(1)}, f32[3,8,128]{2,1,0:T(8,128)S(1)}, u32[]{:S(2)}, u32[]{:S(2)}) collective-permute-start(f32[3,8,128]{2,1,0:T(8,128)S(1)} %pad_maximum_fusion.5), channel_id=1, source_target_pairs={{0,1},{1,0},{2,3},{3,2},{4,5},{5,4},{6,7},{7,6},{8,9},{9,8},{10,11... | collective-permute-start | bytes 36872 | tf_op jit(solution)/shard_map/ppermute | solution.py:893
  46.1 4.6 %collective-permute-start.15 = (f32[3,8,128]{2,1,0:T(8,128)S(1)}, f32[3,8,128]{2,1,0:T(8,128)S(1)}, u32[]{:S(2)}, u32[]{:S(2)}) collective-permute-start(f32[3,8,128]{2,1,0:T(8,128)S(1)} %pad_maximum_fusion.5), channel_id=1, source_target_pairs={{0,3},{1,2},{2,1},{3,0},{4,7},{5,6},{6,5},{7,4},{8,11},{9,10},{10,... | collective-permute-start | bytes 36872 | tf_op jit(solution)/shard_map/ppermute | solution.py:894
  50.7 0.2 shard_map.114
  50.9 0.0 collective-permute-done.14.zmate_in
  50.9 1.6 %collective-permute-done.15.zfar_in = f32[3,8,128]{2,1,0:T(8,128)S(1)} collective-permute-done((f32[3,8,128]{2,1,0:T(8,128)S(1)}, f32[3,8,128]{2,1,0:T(8,128)S(1)}, u32[]{:S(2)}, u32[]{:S(2)}) %collective-permute-start.15) | collective-permute-done | bytes 12320 | tf_op jit(solution)/shard_map/ppermute | solution.py:894
  52.5 0.9 %shard_map.115 = f32[3,512]{1,0:T(4,128)} custom-call(s32[8,128]{1,0:T(8,128)S(1)} %get-tuple-element.114.control_ref, bf16[128,512]{1,0:T(8,128)(2,1)S(1)} %get-tuple-element.198.turned_ref, f32[8,512]{1,0:T(8,128)S(1)} %get-tuple-element.199.own_ref, f32[8,128]{1,0:T(8,128)S(1)} %collective-permute-done.12.mate_in, ...), custom_call_target="tpu_custom_call" | custom-call | tf_op jit(solution)/shard_map/pallas_call | solution.py:1053
  (9 shorter events, 0.0 us)
Async XLA Ops:
  1.6 4.8 %collective-permute-start = (f32[8,128]{1,0:T(8,128)S(1)}, f32[8,128]{1,0:T(8,128)S(1)}, u32[]{:S(2)}, u32[]{:S(2)}) collective-permute-start(f32[8,128]{1,0:T(8,128)S(1)} %get-tuple-element.106), channel_id=1, source_target_pairs={{0,4},{4,0},{8,12},{12,8},{16,20},{20,16},{24,28},{28,24},{1,5},{5... | collective-permute-start | bytes 12296 | tf_op jit(solution)/shard_map/ppermute | solution.py:893
  2.1 4.9 %collective-permute-start.1 = (f32[8,128]{1,0:T(8,128)S(1)}, f32[8,128]{1,0:T(8,128)S(1)}, u32[]{:S(2)}, u32[]{:S(2)}) collective-permute-start(f32[8,128]{1,0:T(8,128)S(1)} %get-tuple-element.106), channel_id=1, source_target_pairs={{0,28},{4,8},{8,4},{12,16},{16,12},{20,24},{24,20},{28,0},{1,29},{... | collective-permute-start | bytes 12296 | tf_op jit(solution)/shard_map/ppermute | solution.py:894
  7.0 5.5 %collective-permute-start.2 = (f32[3,8,128]{2,1,0:T(8,128)S(1)}, f32[3,8,128]{2,1,0:T(8,128)S(1)}, u32[]{:S(2)}, u32[]{:S(2)}) collective-permute-start(f32[3,8,128]{2,1,0:T(8,128)S(1)} %pad_maximum_fusion.4), channel_id=1, source_target_pairs={{0,1},{1,0},{2,3},{3,2},{4,5},{5,4},{6,7},{7,6},{8,9},{9,8},{10,11... | collective-permute-start | bytes 36872 | tf_op jit(solution)/shard_map/ppermute | solution.py:893
  8.7 5.5 %collective-permute-start.3 = (f32[3,8,128]{2,1,0:T(8,128)S(1)}, f32[3,8,128]{2,1,0:T(8,128)S(1)}, u32[]{:S(2)}, u32[]{:S(2)}) collective-permute-start(f32[3,8,128]{2,1,0:T(8,128)S(1)} %pad_maximum_fusion.4), channel_id=1, source_target_pairs={{0,3},{1,2},{2,1},{3,0},{4,7},{5,6},{6,5},{7,4},{8,11},{9,10},{10,... | collective-permute-start | bytes 36872 | tf_op jit(solution)/shard_map/ppermute | solution.py:894
  15.5 3.7 %collective-permute-start.4 = (f32[3,16,256]{2,1,0:T(8,128)S(1)}, f32[3,16,256]{2,1,0:T(8,128)S(1)}, u32[]{:S(2)}, u32[]{:S(2)}) collective-permute-start(f32[3,16,256]{2,1,0:T(8,128)S(1)} %get-tuple-element.125), channel_id=1, source_target_pairs={{0,4},{4,0},{8,12},{12,8},{16,20},{20,16},{24,28},{28,24},{1,5},{5... | collective-permute-start | bytes 147464 | tf_op jit(solution)/shard_map/ppermute | solution.py:893
  15.5 4.5 %collective-permute-start.5 = (f32[3,16,256]{2,1,0:T(8,128)S(1)}, f32[3,16,256]{2,1,0:T(8,128)S(1)}, u32[]{:S(2)}, u32[]{:S(2)}) collective-permute-start(f32[3,16,256]{2,1,0:T(8,128)S(1)} %get-tuple-element.126), channel_id=1, source_target_pairs={{0,28},{4,8},{8,4},{12,16},{16,12},{20,24},{24,20},{28,0},{1,29},{... | collective-permute-start | bytes 147464 | tf_op jit(solution)/shard_map/ppermute | solution.py:894
  20.0 4.2 %collective-permute-start.6 = (f32[3,16,256]{2,1,0:T(8,128)S(1)}, f32[3,16,256]{2,1,0:T(8,128)S(1)}, u32[]{:S(2)}, u32[]{:S(2)}) collective-permute-start(f32[3,16,256]{2,1,0:T(8,128)S(1)} %get-tuple-element.140), channel_id=1, source_target_pairs={{0,1},{1,0},{2,3},{3,2},{4,5},{5,4},{6,7},{7,6},{8,9},{9,8},{10,11... | collective-permute-start | bytes 147464 | tf_op jit(solution)/shard_map/ppermute | solution.py:893
  20.1 6.1 %collective-permute-start.7 = (f32[3,16,256]{2,1,0:T(8,128)S(1)}, f32[3,16,256]{2,1,0:T(8,128)S(1)}, u32[]{:S(2)}, u32[]{:S(2)}) collective-permute-start(f32[3,16,256]{2,1,0:T(8,128)S(1)} %get-tuple-element.141), channel_id=1, source_target_pairs={{0,3},{1,2},{2,1},{3,0},{4,7},{5,6},{6,5},{7,4},{8,11},{9,10},{10,... | collective-permute-start | bytes 147464 | tf_op jit(solution)/shard_map/ppermute | solution.py:894
  28.9 2.4 %collective-permute-start.8 = (f32[3,16,256]{2,1,0:T(8,128)S(1)}, f32[3,16,256]{2,1,0:T(8,128)S(1)}, u32[]{:S(2)}, u32[]{:S(2)}) collective-permute-start(f32[3,16,256]{2,1,0:T(8,128)S(1)} %get-tuple-element.160), channel_id=1, source_target_pairs={{0,4},{4,0},{8,12},{12,8},{16,20},{20,16},{24,28},{28,24},{1,5},{5... | collective-permute-start | bytes 147464 | tf_op jit(solution)/shard_map/ppermute | solution.py:893
  28.9 4.5 %collective-permute-start.9 = (f32[3,16,256]{2,1,0:T(8,128)S(1)}, f32[3,16,256]{2,1,0:T(8,128)S(1)}, u32[]{:S(2)}, u32[]{:S(2)}) collective-permute-start(f32[3,16,256]{2,1,0:T(8,128)S(1)} %get-tuple-element.161), channel_id=1, source_target_pairs={{0,28},{4,8},{8,4},{12,16},{16,12},{20,24},{24,20},{28,0},{1,29},{... | collective-permute-start | bytes 147464 | tf_op jit(solution)/shard_map/ppermute | solution.py:894
  33.4 5.5 %collective-permute-start.10 = (f32[3,16,256]{2,1,0:T(8,128)S(1)}, f32[3,16,256]{2,1,0:T(8,128)S(1)}, u32[]{:S(2)}, u32[]{:S(2)}) collective-permute-start(f32[3,16,256]{2,1,0:T(8,128)S(1)} %get-tuple-element.179), channel_id=1, source_target_pairs={{0,1},{1,0},{2,3},{3,2},{4,5},{5,4},{6,7},{7,6},{8,9},{9,8},{10,11... | collective-permute-start | bytes 147464 | tf_op jit(solution)/shard_map/ppermute | solution.py:893
  34.1 6.0 %collective-permute-start.11 = (f32[3,16,256]{2,1,0:T(8,128)S(1)}, f32[3,16,256]{2,1,0:T(8,128)S(1)}, u32[]{:S(2)}, u32[]{:S(2)}) collective-permute-start(f32[3,16,256]{2,1,0:T(8,128)S(1)} %get-tuple-element.180), channel_id=1, source_target_pairs={{0,3},{1,2},{2,1},{3,0},{4,7},{5,6},{6,5},{7,4},{8,11},{9,10},{10,... | collective-permute-start | bytes 147464 | tf_op jit(solution)/shard_map/ppermute | solution.py:894
  41.3 3.2 %collective-permute-start.12 = (f32[8,128]{1,0:T(8,128)S(1)}, f32[8,128]{1,0:T(8,128)S(1)}, u32[]{:S(2)}, u32[]{:S(2)}) collective-permute-start(f32[8,128]{1,0:T(8,128)S(1)} %get-tuple-element.188), channel_id=1, source_target_pairs={{0,4},{4,0},{8,12},{12,8},{16,20},{20,16},{24,28},{28,24},{1,5},{5... | collective-permute-start | bytes 12296 | tf_op jit(solution)/shard_map/ppermute | solution.py:893
  41.4 4.0 %collective-permute-start.13 = (f32[8,128]{1,0:T(8,128)S(1)}, f32[8,128]{1,0:T(8,128)S(1)}, u32[]{:S(2)}, u32[]{:S(2)}) collective-permute-start(f32[8,128]{1,0:T(8,128)S(1)} %get-tuple-element.188), channel_id=1, source_target_pairs={{0,28},{4,8},{8,4},{12,16},{16,12},{20,24},{24,20},{28,0},{1,29},{... | collective-permute-start | bytes 12296 | tf_op jit(solution)/shard_map/ppermute | solution.py:894
  45.4 5.5 %collective-permute-start.14 = (f32[3,8,128]{2,1,0:T(8,128)S(1)}, f32[3,8,128]{2,1,0:T(8,128)S(1)}, u32[]{:S(2)}, u32[]{:S(2)}) collective-permute-start(f32[3,8,128]{2,1,0:T(8,128)S(1)} %pad_maximum_fusion.5), channel_id=1, source_target_pairs={{0,1},{1,0},{2,3},{3,2},{4,5},{5,4},{6,7},{7,6},{8,9},{9,8},{10,11... | collective-permute-start | bytes 36872 | tf_op jit(solution)/shard_map/ppermute | solution.py:893
  46.1 6.4 %collective-permute-start.15 = (f32[3,8,128]{2,1,0:T(8,128)S(1)}, f32[3,8,128]{2,1,0:T(8,128)S(1)}, u32[]{:S(2)}, u32[]{:S(2)}) collective-permute-start(f32[3,8,128]{2,1,0:T(8,128)S(1)} %pad_maximum_fusion.5), channel_id=1, source_target_pairs={{0,3},{1,2},{2,1},{3,0},{4,7},{5,6},{6,5},{7,4},{8,11},{9,10},{10,... | collective-permute-start | bytes 36872 | tf_op jit(solution)/shard_map/ppermute | solution.py:894

commit v2 on v1

--- a/solution.py
+++ b/solution.py
@@ -19,7 +19,9 @@
 WIDTHS = (12.0, 12.0, 36.0)
 CUT_INV = 1.0 / 25.0
 ROOT = 1.6986436005760381
-CENTERS = tuple(1.0 + 0.6 * n for n in range(BASIS))
+STEP = ROOT * 0.6
+MIDDLE = 1.0 + 0.6 * (BASIS - 1) / 2
+REACH = 5.125
 ROWS = 32
 
 VMEM = pl.BlockSpec(memory_space=pltpu.VMEM)
@@ -144,22 +146,30 @@
     return jnp.where(low, 1.0, u[0]), jnp.where(low, u[1], u[2])
 
 
+def basis_scale(shape):
+    step = (iota(shape, 0) % BASIS).astype(F32) - (BASIS - 1) / 2
+    return jnp.exp2(-(STEP * STEP) * (step * step))
+
+
+def centered(soft):
+    return ROOT * (jnp.minimum(soft, REACH) - MIDDLE)
+
+
 def pair_forward(col_ref, left, row_ref, right, same, high_ref, low_ref):
     for start in range(0, BLOCK, ROWS):
         parts = separation(col_ref, left, row_ref, right, start, 1.0)
         soft, margin = envelope(parts, same, start)
         first, second = angular(parts, 1.0 / soft)
-        weight = margin * margin
-        first, second = first * weight, second * weight
-        scaled = soft * ROOT
+        z = centered(soft)
+        bell = jnp.exp2(-z * (z + (BASIS - 1) * STEP)) * (margin * margin)
+        growth = jnp.exp2((2.0 * STEP) * z)
         for n in range(BASIS):
-            shift = scaled - ROOT * CENTERS[n]
-            bell = jnp.exp2(-(shift * shift))
             here = pl.ds(n * BLOCK + start, ROWS)
             for half, factor in enumerate((first, second)):
                 high, low = split(bell * factor)
                 high_ref[here, half * 128 : half * 128 + 128] = high
                 low_ref[here, half * 128 : half * 128 + 128] = low
+            bell = bell * growth
 
 
 def pair_swapped(col_ref, right, row_ref, left, same, high_ref, low_ref):
@@ -168,47 +178,51 @@
         parts = separation(col_ref, right, row_ref, left, start, -1.0)
         soft, margin = envelope(parts, same, start)
         inverse = 1.0 / soft
-        weight = margin * margin
-        factors = [weight] + [weight * (part * inverse) for part in parts]
-        scaled = soft * ROOT
+        u = [part * inverse for part in parts]
+        z = centered(soft)
+        bell = jnp.exp2(-z * (z + jnp.where(low_lanes, (BASIS - 1) * STEP, (BASIS - 3) * STEP)))
+        bell = bell * (margin * margin)
+        growth = jnp.exp2((4.0 * STEP) * z)
         for pair in range(BASIS // 2):
-            center = jnp.where(low_lanes, ROOT * CENTERS[2 * pair], ROOT * CENTERS[2 * pair + 1])
-            shift = scaled - center
-            bell = jnp.exp2(-(shift * shift))
             for order in range(4):
-                high, low = split(bell * factors[order])
+                high, low = split(bell if order == 0 else bell * u[order - 1])
                 here = pl.ds(order * BLOCK + start, ROWS)
                 high_ref[here, pair * 128 : pair * 128 + 128] = high
                 low_ref[here, pair * 128 : pair * 128 + 128] = low
-
-
-def pair_backward(col_ref, left, row_ref, right, same, pull_ref, grad_row, grad_col):
+            bell = bell * growth
+
+
+def pair_backward(col_ref, left, row_ref, right, same, pull_ref):
     low_lanes = low_half()
     lane = iota((1, 128), 1)
     sums = [jnp.zeros((1, 128), F32) for _ in range(3)]
+    columns = []
     for start in range(0, BLOCK, ROWS):
         parts = separation(col_ref, left, row_ref, right, start, 1.0)
         soft, margin = envelope(parts, same, start)
         inverse = 1.0 / soft
         first, second = angular(parts, inverse)
-        scaled = soft * ROOT
-        by_bell = jnp.zeros((ROWS, 128), F32)
-        by_shift = jnp.zeros((ROWS, 128), F32)
+        z = centered(soft)
+        bell = jnp.exp2(-z * (z - (BASIS - 1) * STEP))
+        shrink = jnp.exp2((-2.0 * STEP) * z)
         by_first = jnp.zeros((ROWS, 128), F32)
         by_second = jnp.zeros((ROWS, 128), F32)
-        for n in range(BASIS):
-            shift = scaled - ROOT * CENTERS[n]
-            bell = jnp.exp2(-(shift * shift))
+        count_first = jnp.zeros((ROWS, 128), F32)
+        count_second = jnp.zeros((ROWS, 128), F32)
+        for n in reversed(range(BASIS)):
             here = pl.ds(n * BLOCK + start, ROWS)
-            pull_first, pull_second = pull_ref[here, 0:128], pull_ref[here, 128:256]
-            both = bell * (first * pull_first + second * pull_second)
-            by_bell = by_bell + both
-            by_shift = by_shift + shift * both
-            by_first = by_first + bell * pull_first
-            by_second = by_second + bell * pull_second
+            by_first = by_first + bell * pull_ref[here, 0:128]
+            by_second = by_second + bell * pull_ref[here, 128:256]
+            if n > 0:
+                count_first = count_first + by_first
+                count_second = count_second + by_second
+                bell = bell * shrink
         weight = margin * margin
+        by_bell = first * by_first + second * by_second
+        by_count = first * count_first + second * count_second
         by_bell = by_bell + pltpu.roll(by_bell, BLOCK, 1)
-        by_shift = (by_shift + pltpu.roll(by_shift, BLOCK, 1)) * weight
+        by_count = by_count + pltpu.roll(by_count, BLOCK, 1)
+        by_shift = (ROOT * (soft - 1.0) * by_bell - STEP * by_count) * weight
         by_first, by_second = by_first * weight, by_second * weight
         turned = pltpu.roll(by_second, BLOCK, 1)
         by_u = [
@@ -225,8 +239,11 @@
             sums[a] = sums[a] + jnp.sum(force, axis=0, keepdims=True)
             total = jnp.sum(jnp.where(low_lanes, force, 0.0), axis=1, keepdims=True)
             column = jnp.where(lane == a, total, column)
-        grad_col[block_rows(left, start, ROWS), :] -= column
-    grad_row[right] += jnp.concatenate(sums + [jnp.zeros((5, 128), F32)], axis=0)
+        columns.append(column)
+    return (
+        jnp.concatenate(sums + [jnp.zeros((5, 128), F32)], axis=0),
+        jnp.concatenate(columns, axis=0),
+    )
 
 
 def kind_table(col_ref, block):
@@ -246,30 +263,52 @@
     return control_ref[1, 2] == 0, control_ref[2, 2] == 0
 
 
-def own_tiles(control_ref, own_blocks, work):
-    def step(slot, carried):
-        left, right = control_ref[slot, 0], control_ref[slot, 1]
-
-        @pl.when(right < own_blocks)
-        def _():
-            work(slot, left, right)
-
+def fill_control(control_ref, words_ref, tiles_ref, slots, own_blocks):
+    row, lane = iota((8, 128), 0), iota((8, 128), 1)
+    live = words_ref[0, 0]
+    table = jnp.where(lane < 2, tiles_ref[...], 0)
+    lengths = [jnp.int32(0), jnp.int32(0)]
+    for slot in range(2, slots):
+        left, right = tiles_ref[slot, 0], tiles_ref[slot, 1]
+        for which in range(2):
+            ghost = which == 0
+            sending = right - own_blocks if ghost else right
+            member = (slot < live) & ((right >= own_blocks) if ghost else (right < own_blocks))
+            first = 3 + 3 * which
+            entry = jnp.where(lane == first, slot, jnp.where(lane == first + 1, left, sending))
+            place = (lane >= first) & (lane < first + 3) & (row == lengths[which]) & member
+            table = jnp.where(place, entry, table)
+            lengths[which] = lengths[which] + member.astype(jnp.int32)
+    for place, word in enumerate([live, words_ref[0, 1], words_ref[0, 2], *lengths]):
+        table = jnp.where((lane == 2) & (row == place), word, table)
+    control_ref[...] = table
+
+
+def listed_tiles(control_ref, which, work):
+    first = 3 + 3 * which
+    count = control_ref[3 + which, 2]
+
+    def entry(place):
+        return tuple(control_ref[place, first + k] for k in range(3))
+
+    def step(half, carried):
+        work([entry(2 * half), entry(2 * half + 1)])
         return carried
 
-    lax.fori_loop(2, control_ref[0, 2], step, 0)
-
-
-def more_ghost_tiles(control_ref, own_blocks, work):
-    def step(slot, carried):
-        left, right = control_ref[slot, 0], control_ref[slot, 1]
-
-        @pl.when(right >= own_blocks)
-        def _():
-            work(slot, left, right - own_blocks)
-
-        return carried
-
-    lax.fori_loop(2, control_ref[0, 2], step, 0)
+    lax.fori_loop(0, count // 2, step, 0)
+
+    @pl.when(count % 2 == 1)
+    def _():
+        work([entry(count - 1)])
+
+
+def own_tiles(control_ref, work):
+    listed_tiles(control_ref, 1, work)
+
+
+def ghost_tiles(control_ref, work):
+    work([(slot, control_ref[slot, 0], slot) for slot in range(2)])
+    listed_tiles(control_ref, 0, work)
 
 
 def exact_pick(rows, chosen):
@@ -355,17 +394,23 @@
     return jnp.where(row < 2, WIDTHS[0], jnp.where(row == 2, WIDTHS[2], 1.0))
 
 
-def add_histogram(col_ref, left, row_ref, right, same, kind_ref, hist_ref, high_ref, low_ref):
-    pair_forward(col_ref, left, row_ref, right, same, high_ref, low_ref)
-    table = kind_table(kind_ref, right)
-    found = mm(high_ref[...], table) + mm(low_ref[...], table)
+def add_histograms(tiles, col_ref, row_ref, own, kind_ref, hist_ref, pair_high, pair_low):
+    for slot, left, right in tiles:
+        same = left == right if own else False
+        pair_forward(col_ref, left, row_ref, right, same, pair_high.at[slot], pair_low.at[slot])
+    tables = [kind_table(kind_ref, right) for _, _, right in tiles]
+    found = [
+        mm(pair_high[slot], table) + mm(pair_low[slot], table)
+        for (slot, _, _), table in zip(tiles, tables)
+    ]
     lane_basis = iota((1, 128), 1) // (4 * SPAN)
-    for half in range(2):
-        total = jnp.zeros((BLOCK, 128), F32)
-        for n in range(4):
-            begin = (half * 4 + n) * BLOCK
-            total = jnp.where(lane_basis == n, found[begin : begin + BLOCK], total)
-        hist_ref[block_rows(left), half * 128 : half * 128 + 128] += total
+    for (_, left, _), one in zip(tiles, found):
+        for half in range(2):
+            total = jnp.zeros((BLOCK, 128), F32)
+            for n in range(4):
+                begin = (half * 4 + n) * BLOCK
+                total = jnp.where(lane_basis == n, one[begin : begin + BLOCK], total)
+            hist_ref[block_rows(left), half * 128 : half * 128 + 128] += total
 
 
 def prepare_kernel(
@@ -373,19 +418,39 @@
     tiles_ref,
     site_ref,
     send_ref,
-    embed_in,
-    radial_in,
-    readout_in,
-    mixing_in,
     control_ref,
     col_ref,
     row_ref,
     hist_ref,
     pair_high,
     pair_low,
+    chosen_ref,
+):
+    atoms = site_ref.shape[1]
+    blocks = atoms // BLOCK
+    fill_control(control_ref, words_ref, tiles_ref, pair_high.shape[0], blocks)
+    own = site_ref[...] * axis_scale()[:, 0:1]
+    col_ref[...] = upright(own)
+    for block in range(blocks):
+        row_ref[block] = doubled(own, block)
+    chosen_ref[...] = chooser(send_ref[...], atoms).astype(F32).astype(BF16)
+    hist_ref[...] = jnp.zeros_like(hist_ref)
+
+    own_tiles(
+        control_ref,
+        lambda tiles: add_histograms(
+            tiles, col_ref, row_ref, True, col_ref, hist_ref, pair_high, pair_low
+        ),
+    )
+
+
+def fold_kernel(
+    embed_in,
+    radial_in,
+    readout_in,
+    mixing_in,
     fold_high,
     fold_low,
-    chosen_ref,
     mix_high,
     mix_low,
     weight_ref,
@@ -404,27 +469,11 @@
         ),
         sems,
     )
-    row = iota((8, 128), 0)
-    words = jnp.where(row == 0, words_ref[0, 0], jnp.where(row == 1, words_ref[0, 1], words_ref[0, 2]))
-    control_ref[...] = jnp.where(iota((8, 128), 1) == 2, words, tiles_ref[...])
-    atoms = site_ref.shape[1]
-    blocks = atoms // BLOCK
-    own = site_ref[...] * axis_scale()[:, 0:1]
-    col_ref[...] = upright(own)
-    for block in range(blocks):
-        row_ref[block] = doubled(own, block)
-    chosen_ref[...] = chooser(send_ref[...], atoms).astype(F32).astype(BF16)
-    hist_ref[...] = jnp.zeros_like(hist_ref)
-
-    def work(slot, left, right):
-        add_histogram(
-            col_ref, left, row_ref, right, left == right, col_ref, hist_ref,
-            pair_high.at[slot], pair_low.at[slot],
-        )
-
-    own_tiles(control_ref, blocks, work)
     for copy in copies:
         copy.wait()
+
+    radial = weight_ref[SPAN : SPAN + paths, :]
+    weight_ref[SPAN : SPAN + paths, :] = radial * basis_scale(radial.shape)
 
     embed = jnp.where(iota((SPAN, 128), 0) < kinds, weight_ref[0:SPAN, :], 0.0)
     scalar = jnp.concatenate([radial_row(weight_ref, 0, n) * embed for n in range(BASIS)], axis=0)
@@ -469,7 +518,6 @@
 ):
     fetching = pltpu.make_async_copy(send_in, send_ref, sem)
     fetching.start()
-    blocks = hist_in.shape[0] // BLOCK
     even_x, even_y = parities(control_ref)
     ghosts = pick_rows(even_x, even_y, mate_in[...], far_in[...], zmate_in[...], zfar_in[...])
     row = iota((8, 128), 0)
@@ -485,23 +533,21 @@
         ghost_row[block] = doubled(ghosts, block)
     hist_ref[...] = hist_in[...]
 
-    def work(slot, left, right):
-        add_histogram(
-            col_ref, left, ghost_row, right, False, ghost_col, hist_ref,
-            pair_high.at[slot], pair_low.at[slot],
-        )
-
-    for slot in range(2):
-        work(slot, control_ref[slot, 0], slot)
-    more_ghost_tiles(control_ref, blocks, work)
+    ghost_tiles(
+        control_ref,
+        lambda tiles: add_histograms(
+            tiles, col_ref, ghost_row, False, ghost_col, hist_ref, pair_high, pair_low
+        ),
+    )
     fetching.wait()
 
-    def piece(slot):
-        return jnp.concatenate(
-            [hist_ref[pl.ds(send_ref[slot, entry], 1), :] for entry in range(GHOSTS)], axis=0
-        )
-
-    put_packets(even_x, piece, mate_ref, far_ref, side_ref)
+    up, down = jnp.where(even_x, 5, 0), jnp.where(even_x, 0, 5)
+    places = [(mate_ref, part, up + part) for part in range(3)]
+    places += [(far_ref, part, down + part) for part in range(3)]
+    places += [(side_ref, part, 3 + part) for part in range(2)]
+    for ref, part, slot in places:
+        for entry in range(GHOSTS):
+            ref[part, entry : entry + 1, :] = hist_ref[pl.ds(send_ref[slot, entry], 1), :]
 
 
 def make_features(block, col_ref, kinds, weight_ref, pre_ref, feat_high, feat_low, scalar_ref):
@@ -526,14 +572,18 @@
             ref[block, here, 128 - used : 256 - used] = empty
 
 
-def add_message(left, right, feat_high, feat_low, weight_ref, message_ref, high_ref, low_ref):
-    found = mm3((high_ref[...], low_ref[...]), (feat_high[right], feat_low[right]))
-    total = jnp.zeros((BLOCK, 128), F32)
-    for n in range(BASIS):
-        rows = slice(n * BLOCK, n * BLOCK + BLOCK)
-        total = total + found[rows, 0:128] * radial_row(weight_ref, 2, n)
-        total = total + found[rows, 128:256] * radial_row(weight_ref, 3, n)
-    message_ref[block_rows(left), :] += total
+def add_messages(tiles, feat_high, feat_low, weight_ref, message_ref, pair_high, pair_low):
+    found = [
+        mm3((pair_high[slot], pair_low[slot]), (feat_high[right], feat_low[right]))
+        for slot, _, right in tiles
+    ]
+    for (_, left, _), one in zip(tiles, found):
+        total = jnp.zeros((BLOCK, 128), F32)
+        for n in range(BASIS):
+            rows = slice(n * BLOCK, n * BLOCK + BLOCK)
+            total = total + one[rows, 0:128] * radial_row(weight_ref, 2, n)
+            total = total + one[rows, 128:256] * radial_row(weight_ref, 3, n)
+        message_ref[block_rows(left), :] += total
 
 
 def feature_kernel(
@@ -574,22 +624,20 @@
     blocks = feat_high.shape[0]
     message_ref[...] = jnp.zeros_like(message_ref)
 
-    def work(slot, left, right):
-        add_message(
-            left, right, feat_high, feat_low, weight_ref, message_ref,
-            pair_high.at[slot], pair_low.at[slot],
-        )
-
-    own_tiles(control_ref, blocks, work)
-
-    def swapped(slot, left, right):
-        pair_swapped(
-            ghost_col, right, row_ref, left, False, swap_high.at[slot], swap_low.at[slot]
-        )
-
-    for slot in range(2):
-        swapped(slot, control_ref[slot, 0], slot)
-    more_ghost_tiles(control_ref, blocks, swapped)
+    own_tiles(
+        control_ref,
+        lambda tiles: add_messages(
+            tiles, feat_high, feat_low, weight_ref, message_ref, pair_high, pair_low
+        ),
+    )
+
+    def swapped(tiles):
+        for slot, left, right in tiles:
+            pair_swapped(
+                ghost_col, right, row_ref, left, False, swap_high.at[slot], swap_low.at[slot]
+            )
+
+    ghost_tiles(control_ref, swapped)
 
 
 def weighted_pull(cotangent, weight_ref, path):
@@ -598,17 +646,23 @@
     )
 
 
-def add_feature_pull(right, cotangent, weight_ref, grad_feat, swap_high, swap_low):
-    to_scalar = mm3(
-        (swap_high[0:BLOCK, :], swap_low[0:BLOCK, :]), weighted_pull(cotangent, weight_ref, 2)
-    )
-    to_vector = mm3(
-        (swap_high[BLOCK:, :], swap_low[BLOCK:, :]), weighted_pull(cotangent, weight_ref, 3)
-    )
-    rows = block_rows(right)
-    grad_feat[rows, 0:128] += to_scalar
-    for a in range(3):
-        grad_feat[rows, (a + 1) * 128 : (a + 2) * 128] += to_vector[a * BLOCK : (a + 1) * BLOCK]
+def add_feature_pulls(tiles, places, pull_message, weight_ref, grad_feat, swap_high, swap_low):
+    weighted = []
+    for _, left, _ in tiles:
+        cotangent = pull_message[block_rows(left), :]
+        weighted.append([weighted_pull(cotangent, weight_ref, path) for path in (2, 3)])
+    found = []
+    for place, (by_scalar, by_vector) in zip(places, weighted):
+        high, low = swap_high.at[place], swap_low.at[place]
+        to_scalar = mm3((high[0:BLOCK, :], low[0:BLOCK, :]), by_scalar)
+        to_vector = mm3((high[BLOCK:, :], low[BLOCK:, :]), by_vector)
+        found.append((to_scalar, to_vector))
+    for (_, _, right), (to_scalar, to_vector) in zip(tiles, found):
+        rows = block_rows(right)
+        grad_feat[rows, 0:128] += to_scalar
+        for a in range(3):
+            here = slice(a * BLOCK, (a + 1) * BLOCK)
+            grad_feat[rows, (a + 1) * 128 : (a + 2) * 128] += to_vector[here]
 
 
 def finish(message, scalar, mix_high, mix_low, weight_ref):
@@ -665,11 +719,13 @@
     side_ref,
     feat_high,
     feat_low,
+    pull_message,
+    direct_ref,
+    share_ref,
     message_ref,
     pre_ref,
     grad_feat,
 ):
-    blocks = scalar_ref.shape[0] // BLOCK
     even_x, even_y = parities(control_ref)
     fold = (fold_high[...], fold_low[...])
     ghost_hist = pick_all((even_x, even_y, mate_in, far_in, zmate_in, zfar_in))
@@ -678,35 +734,24 @@
         make_features(block, ghost_col, kinds, weight_ref, pre_ref, feat_high, feat_low, None)
     message_ref[...] = message_in[...]
 
-    def forward(slot, left, right):
-        add_message(
-            left, right, feat_high, feat_low, weight_ref, message_ref,
-            pair_high.at[slot], pair_low.at[slot],
-        )
-
-    lefts = [control_ref[slot, 0] for slot in range(2)]
-    for slot in range(2):
-        forward(slot, lefts[slot], slot)
-    more_ghost_tiles(control_ref, blocks, forward)
-
+    ghost_tiles(
+        control_ref,
+        lambda tiles: add_messages(
+            tiles, feat_high, feat_low, weight_ref, message_ref, pair_high, pair_low
+        ),
+    )
+
+    share_ref[...], direct_ref[...], pull_message[...] = finish(
+        message_ref[...], scalar_ref[...], mix_high, mix_low, weight_ref
+    )
     grad_feat[...] = jnp.zeros_like(grad_feat)
 
-    def backward(slot, right, cotangent):
-        add_feature_pull(
-            right, cotangent, weight_ref, grad_feat, swap_high.at[slot], swap_low.at[slot]
-        )
-
-    def finished(rows):
-        take = lambda ref: jnp.concatenate([ref[row, :] for row in rows], axis=0)
-        return finish(take(message_ref), take(scalar_ref), mix_high, mix_low, weight_ref)[2]
-
-    pulled = finished([block_rows(left) for left in lefts])
-    for slot in range(2):
-        backward(slot, slot, pulled[slot * BLOCK : slot * BLOCK + BLOCK])
-    more_ghost_tiles(
+    ghost_tiles(
         control_ref,
-        blocks,
-        lambda slot, left, right: backward(slot, right, finished([block_rows(left)])),
+        lambda tiles: add_feature_pulls(
+            tiles, [slot for slot, _, _ in tiles], pull_message, weight_ref, grad_feat,
+            swap_high, swap_low,
+        ),
     )
 
     ghost_pull = mm3(split(pull_features(grad_feat, pre_ref)), fold, ROWROW)
@@ -723,40 +768,44 @@
     control_ref,
     col_ref,
     row_ref,
-    mix_high,
-    mix_low,
     weight_ref,
-    scalar_ref,
-    message_ref,
+    pull_message,
+    direct_ref,
     grad_feat,
-    pull_message,
-    share_ref,
     swap_high,
     swap_low,
 ):
-    blocks = scalar_ref.shape[0] // BLOCK
-    share, direct, pulled = finish(
-        message_ref[...], scalar_ref[...], mix_high, mix_low, weight_ref
-    )
-    share_ref[...] = share
-    pull_message[...] = pulled
-    grad_feat[:, 0:128] = direct
-    grad_feat[:, 128:512] = jnp.zeros((blocks * BLOCK, 384), F32)
-
-    def backward(slot, left, right):
-        pair_swapped(col_ref, right, row_ref, left, left == right, swap_high, swap_low)
+    grad_feat[:, 0:128] = direct_ref[...]
+    grad_feat[:, 128:512] = jnp.zeros((direct_ref.shape[0], 384), F32)
+
+    def backward(tiles):
+        for place, (_, left, right) in enumerate(tiles):
+            pair_swapped(
+                col_ref, right, row_ref, left, left == right,
+                swap_high.at[place], swap_low.at[place],
+            )
+        add_feature_pulls(
+            tiles, range(len(tiles)), pull_message, weight_ref, grad_feat, swap_high, swap_low
+        )
+
+    own_tiles(control_ref, backward)
+
+
+def pair_pulls(tiles, pull_message, weight_ref, high_ref, low_ref, pull_ref):
+    weighted = []
+    for _, left, _ in tiles:
         cotangent = pull_message[block_rows(left), :]
-        add_feature_pull(right, cotangent, weight_ref, grad_feat, swap_high, swap_low)
-
-    own_tiles(control_ref, blocks, backward)
-
-
-def pair_pull(left, right, pull_message, weight_ref, high_ref, low_ref):
-    cotangent = pull_message[block_rows(left), :]
-    first = weighted_pull(cotangent, weight_ref, 2)
-    second = weighted_pull(cotangent, weight_ref, 3)
-    both = [jnp.concatenate([first[part], second[part]], axis=1) for part in range(2)]
-    return mm3(both, (high_ref[right], low_ref[right]), ROWROW)
+        first = weighted_pull(cotangent, weight_ref, 2)
+        second = weighted_pull(cotangent, weight_ref, 3)
+        weighted.append(
+            [jnp.concatenate([first[part], second[part]], axis=1) for part in range(2)]
+        )
+    found = [
+        mm3(one, (high_ref[right], low_ref[right]), ROWROW)
+        for one, (_, _, right) in zip(weighted, tiles)
+    ]
+    for one, (slot, _, _) in zip(found, tiles):
+        pull_ref[slot] = one
 
 
 def ghost_pair_kernel(
@@ -772,16 +821,13 @@
     pull_hist_ref,
     pull_ref,
 ):
-    blocks = pre_ref.shape[0] // BLOCK
     pulled = pull_features(grad_feat, pre_ref)
     pull_hist_ref[...] = mm3(split(pulled), (fold_high[...], fold_low[...]), ROWROW)
 
-    def work(slot, left, right):
-        pull_ref[slot] = pair_pull(left, right, pull_message, weight_ref, ghost_high, ghost_low)
-
-    for slot in range(2):
-        work(slot, control_ref[slot, 0], slot)
-    more_ghost_tiles(control_ref, blocks, work)
+    ghost_tiles(
+        control_ref,
+        lambda tiles: pair_pulls(tiles, pull_message, weight_ref, ghost_high, ghost_low, pull_ref),
+    )
 
 
 def own_pair_kernel(
@@ -789,21 +835,39 @@
 ):
     energy_ref[...] = jnp.sum(share_ref[...].T, axis=0, keepdims=True)
 
-    def work(slot, left, right):
-        pull_ref[slot] = pair_pull(left, right, pull_message, weight_ref, feat_high, feat_low)
-
-    own_tiles(control_ref, feat_high.shape[0], work)
-
-
-def both_pulls(total_ref, left, kind_ref, right, pull_in, pull_ref):
+    own_tiles(
+        control_ref,
+        lambda tiles: pair_pulls(tiles, pull_message, weight_ref, feat_high, feat_low, pull_ref),
+    )
+
+
+def add_position_pulls(
+    tiles, total_ref, kind_ref, col_ref, row_ref, own, pull_in, pull_refs, grad_row, grad_col
+):
     lane_basis = iota((1, 128), 1) // (4 * SPAN)
-    parts = []
-    for half in range(2):
-        here = total_ref[block_rows(left), half * 128 : half * 128 + 128]
-        parts += [jnp.where(lane_basis == n, here, 0.0) for n in range(4)]
-    high, low = split(jnp.concatenate(parts, axis=0))
-    table = kind_table(kind_ref, right)
-    pull_ref[...] = pull_in[...] + mm(high, table, ROWROW) + mm(low, table, ROWROW)
+    built = []
+    for _, left, right in tiles:
+        parts = []
+        for half in range(2):
+            here = total_ref[block_rows(left), half * 128 : half * 128 + 128]
+            parts += [jnp.where(lane_basis == n, here, 0.0) for n in range(4)]
+        high, low = split(jnp.concatenate(parts, axis=0))
+        table = kind_table(kind_ref, right)
+        built.append(
+            (jnp.concatenate([high, low], axis=1), jnp.concatenate([table, table], axis=1))
+        )
+    found = [mm(both, table, ROWROW) for both, table in built]
+    for place, ((slot, _, _), one) in enumerate(zip(tiles, found)):
+        pull_refs[place] = pull_in[slot] + one
+    grads = [
+        pair_backward(
+            col_ref, left, row_ref, right, left == right if own else False, pull_refs.at[place]
+        )
+        for place, (_, left, right) in enumerate(tiles)
+    ]
+    for (_, left, right), (by_row, by_col) in zip(tiles, grads):
+        grad_row[right] += by_row
+        grad_col[block_rows(left), :] -= by_col
 
 
 def third_ghost_kernel(
@@ -824,7 +888,6 @@
     grad_ghost,
     pull_refs,
 ):
-    blocks = pull_hist_ref.shape[0] // BLOCK
     even_x, even_y = parities(control_ref)
     returned = split(pick_all((even_x, even_y, mate_in, far_in, zmate_in, zfar_in)))
     chosen = chosen_ref[...]
@@ -832,14 +895,13 @@
     grad_ghost[...] = jnp.zeros_like(grad_ghost)
     grad_col[...] = jnp.zeros_like(grad_col)
 
-    def work(slot, left, right, part=0):
-        pull_ref = pull_refs.at[part]
-        both_pulls(total_ref, left, ghost_col, right, pull_in.at[slot], pull_ref)
-        pair_backward(col_ref, left, ghost_row, right, False, pull_ref, grad_ghost, grad_col)
-
-    for slot in range(2):
-        work(slot, control_ref[slot, 0], slot, slot)
-    more_ghost_tiles(control_ref, blocks, work)
+    ghost_tiles(
+        control_ref,
+        lambda tiles: add_position_pulls(
+            tiles, total_ref, ghost_col, col_ref, ghost_row, False, pull_in, pull_refs,
+            grad_ghost, grad_col,
+        ),
+    )
     out_ref[...] = jnp.where(low_half(), grad_ghost[0], grad_ghost[1])
 
 
@@ -855,18 +917,20 @@
     turned_ref,
     grad_row,
     grad_col,
-    pull_ref,
+    pull_refs,
 ):
     blocks = total_ref.shape[0] // BLOCK
     turned_ref[...] = chosen_ref[...].astype(F32).T.astype(BF16)
     grad_row[...] = jnp.zeros_like(grad_row)
     grad_col[...] = grad_col_in[...]
 
-    def work(slot, left, right):
-        both_pulls(total_ref, left, col_ref, right, pull_in.at[slot], pull_ref)
-        pair_backward(col_ref, left, row_ref, right, left == right, pull_ref, grad_row, grad_col)
-
-    own_tiles(control_ref, blocks, work)
+    own_tiles(
+        control_ref,
+        lambda tiles: add_position_pulls(
+            tiles, total_ref, col_ref, col_ref, row_ref, True, pull_in, pull_refs,
+            grad_row, grad_col,
+        ),
+    )
     low = low_half()
     by_sender = jnp.concatenate(
         [jnp.where(low, grad_row[2 * k], grad_row[2 * k + 1]) for k in range(blocks // 2)], axis=1
@@ -889,15 +953,16 @@
 
 
 def swap_both(axis, to_mate, to_far):
-    to_mate, to_far = lax.optimization_barrier((to_mate, to_far))
+    to_far, to_mate = lax.optimization_barrier((to_far, to_mate))
+    far = lax.ppermute(to_far, axis, partners(axis, True))
     mate = lax.ppermute(to_mate, axis, partners(axis, False))
-    far = lax.ppermute(to_far, axis, partners(axis, True))
-    return lax.optimization_barrier((mate, far))
+    far, mate = lax.optimization_barrier((far, mate))
+    return mate, far
 
 
 def exchange_rows(rows, beside):
     mate, far = swap_both("gx", rows, rows)
-    mate, far, beside = lax.optimization_barrier((mate, far, beside))
+    far, mate, beside = lax.optimization_barrier((far, mate, beside))
     column = jnp.stack([rows, mate, far])
     zmate, zfar = swap_both("gy", column, column)
     return (mate, far, zmate, zfar), beside
@@ -905,7 +970,7 @@
 
 def exchange_packets(even_y, to_mate, to_far, side, beside):
     mate, far = swap_both("gx", to_mate, to_far)
-    mate, far, beside = lax.optimization_barrier((mate, far, beside))
+    far, mate, beside = lax.optimization_barrier((far, mate, beside))
     up = jnp.concatenate([mate[2:3], far[2:3], side[1:2]], axis=0)
     down = jnp.concatenate([mate[0:1], far[0:1], side[0:1]], axis=0)
     zmate, zfar = swap_both("gy", jnp.where(even_y, up, down), jnp.where(even_y, down, up))
@@ -917,7 +982,7 @@
 
 
 def call(kernel, in_specs, outs, scratch=()):
-    return pl.pallas_call(
+    made = pl.pallas_call(
         kernel,
         in_specs=in_specs,
         out_specs=jax.tree.map(lambda _: VMEM, outs),
@@ -925,6 +990,15 @@
         scratch_shapes=list(scratch),
         compiler_params=PARAMS,
     )
+
+    def run(*args):
+        placed = [
+            pltpu.with_memory_space_constraint(arg, pltpu.HBM if spec is HBM else pltpu.VMEM)
+            for arg, spec in zip(args, in_specs, strict=True)
+        ]
+        return made(*placed)
+
+    return run
 
 
 def shards(fractions, species, send_list, tile_list, counts, embedding, radial, mixing, readout):
@@ -935,19 +1009,16 @@
     parity = [lax.axis_index("gx") % 2, lax.axis_index("gy") % 2]
     even_y = parity[1] == 0
     words = jnp.stack([counts[0], *parity]).astype(jnp.int32)[None]
-    far_arrays = [
-        pltpu.with_memory_space_constraint(array, pltpu.HBM)
-        for array in (
-            fractions,
-            species[None],
-            send_list,
-            tile_list,
-            embedding,
-            radial.reshape(-1, radial.shape[2]),
-            readout[None],
-            mixing,
-        )
-    ]
+    far_arrays = (
+        fractions,
+        species[None],
+        send_list,
+        tile_list,
+        embedding,
+        radial.reshape(-1, radial.shape[2]),
+        readout[None],
+        mixing,
+    )
     packets = [struct(3, GHOSTS, HIST), struct(3, GHOSTS, HIST), struct(2, GHOSTS, HIST)]
     hist_struct = struct(atoms, HIST)
     col_struct = struct(atoms, 128)
@@ -974,24 +1045,26 @@
             pltpu.SemaphoreType.DMA((4,)),
         ],
     )(*far_arrays[0:4])
-    arrived, (words, site) = exchange_rows(rows, (words, site))
-    control, col, row, hist, own_high, own_low, fold_high, fold_low, chosen, *rest = call(
-        prepare_kernel,
-        [VMEM] * 4 + [HBM] * 4,
-        [struct(8, 128, dtype=jnp.int32), col_struct, own_rows, hist_struct]
-        + pairs
-        + fold_halves
-        + [struct(atoms, 128, dtype=BF16)]
-        + mix_halves
-        + [struct(2 * SPAN + 4 * BASIS, 128)],
+    folded = call(
+        fold_kernel,
+        [HBM] * 4,
+        fold_halves + mix_halves + [struct(2 * SPAN + 4 * BASIS, 128)],
         [
             pltpu.VMEM((HIST, 640), F32),
             pltpu.VMEM(mixing.shape, F32),
             pltpu.SemaphoreType.DMA((4,)),
         ],
-    )(words, tiles, site, send, *far_arrays[4:])
-    mix_high, mix_low, weights = rest
+    )(*far_arrays[4:])
+    arrived, (words, site, folded) = exchange_rows(rows, (words, site, folded))
+    fold_high, fold_low, mix_high, mix_low, weights = folded
     fold, mix = (fold_high, fold_low), (mix_high, mix_low)
+    control, col, row, hist, own_high, own_low, chosen = call(
+        prepare_kernel,
+        [VMEM] * 4,
+        [struct(8, 128, dtype=jnp.int32), col_struct, own_rows, hist_struct]
+        + pairs
+        + [struct(atoms, 128, dtype=BF16)],
+    )(words, tiles, site, send)
     hist, to_mate, to_far, side, ghost_col, ghost_row, pair_high, pair_low = call(
         first_kernel,
         [VMEM] * 8,
@@ -1008,23 +1081,28 @@
     message, swap_high, swap_low = call(message_kernel, [VMEM] * 8, [col_struct] + swaps)(
         control, row, ghost_col, weights, feat_high, feat_low, own_high, own_low
     )
-    to_mate, to_far, side, ghost_high, ghost_low, message = call(
+    (
+        to_mate, to_far, side, ghost_high, ghost_low, pull_message, direct, share,
+    ) = call(
         functools.partial(second_ghost_kernel, kinds),
         [VMEM] * 17,
-        packets + ghost_halves + [col_struct],
-        [pltpu.VMEM((8 * GHOSTS, 640), F32), pltpu.VMEM((8 * GHOSTS, 512), F32)],
+        packets + ghost_halves + [col_struct] * 3,
+        [
+            pltpu.VMEM((atoms, 128), F32),
+            pltpu.VMEM((8 * GHOSTS, 640), F32),
+            pltpu.VMEM((8 * GHOSTS, 512), F32),
+        ],
     )(
         control, *arrived, ghost_col, *fold, *mix, weights, scalar, message,
         pair_high, pair_low, swap_high, swap_low,
     )
-    second_pull = call(
+    grad_feat = call(
         second_pull_kernel,
-        [VMEM] * 8,
-        [struct(atoms, 512), col_struct, col_struct],
-        [pltpu.VMEM((256, BASIS * BLOCK), BF16)] * 2,
-    )(control, col, row, *mix, weights, scalar, message)
-    arrived, second_pull = exchange_packets(even_y, to_mate, to_far, side, second_pull)
-    grad_feat, pull_message, share = second_pull
+        [VMEM] * 6,
+        struct(atoms, 512),
+        [pltpu.VMEM((2, 256, BASIS * BLOCK), BF16)] * 2,
+    )(control, col, row, weights, pull_message, direct)
+    arrived, grad_feat = exchange_packets(even_y, to_mate, to_far, side, grad_feat)
     pull_hist, pull = call(ghost_pair_kernel, [VMEM] * 9, [hist_struct, pulls])(
         control, *fold, weights, pre, grad_feat, pull_message, ghost_high, ghost_low
     )
@@ -1047,7 +1125,7 @@
         [
             pltpu.VMEM((blocks, 8, 128), F32),
             pltpu.VMEM((atoms, 128), F32),
-            pltpu.VMEM((BASIS * BLOCK, 256), F32),
+            pltpu.VMEM((2, BASIS * BLOCK, 256), F32),
         ],
     )(control, chosen, total, col, row, pull, grad_col)
     forces = call(last_kernel, [VMEM] * 7, struct(3, atoms))(control, turned, own, *arrived)

time: 54.4 us -> 52.4 us (0.963); the launches traced: 53.4 us -> 52.2 us
  starting transfers between devices: 26.6 us -> 16 us
  waiting for transfers between devices: 11.5 us -> 20.9 us
    ppermute x8, starting transfers between devices: 22.8 us -> 14.4 us  [swap_both(): far = lax.ppermute(to_far, axis, partners(axis, True))]
    ppermute x8, waiting for transfers between devices: 10.9 us -> 18.1 us  [swap_both(): far = lax.ppermute(to_far, axis, partners(axis, True))]
    ppermute x8, starting transfers between devices: 3.85 us -> 1.65 us  [swap_both(): mate = lax.ppermute(to_mate, axis, partners(axis, False))]
    ppermute x8, waiting for transfers between devices: 0.63 us -> 2.81 us  [swap_both(): mate = lax.ppermute(to_mate, axis, partners(axis, False))]
    pallas_call x12 -> x13, Pallas kernels: 13.7 us -> 13.7 us  [run(): return made(*placed)]
  transfers between devices with their start and end apart: 16 -> 16, of which waited for: 9 -> 11; matrix products, arithmetic and copies ran while one was open for 0% -> 0% of each run, Pallas kernels for 13% -> 13%
where the time goes in v2:
time: 52.4 us; the launch traced here: 52.2 us
  waiting for transfers between devices  20.9 us (40%)
  starting transfers between devices  16 us (31%)
  Pallas kernels  13.7 us (26%)
  between operations  1.43 us (3%)
    ppermute x8, waiting for transfers between devices, swap_both(): far = lax.ppermute(to_far, axis, partners(axis, True))  18.1 us
    ppermute x8, starting transfers between devices, swap_both(): far = lax.ppermute(to_far, axis, partners(axis, True))  14.4 us
    pallas_call x13, Pallas kernels, run(): return made(*placed)  13.7 us
    ppermute x8, waiting for transfers between devices, swap_both(): mate = lax.ppermute(to_mate, axis, partners(axis, False))  2.81 us
    ppermute x8, starting transfers between devices, swap_both(): mate = lax.ppermute(to_mate, axis, partners(axis, False))  1.65 us
  transfers between devices with their start and end apart: 16, of which 11 were waited for; matrix products, arithmetic and copies ran while one was open for 0% of the time, Pallas kernels for 13%

profile of v2, /device:TPU:0, one launch (start us, length us, event | category | flops | bytes accessed | tf_op | source)
XLA Modules:
  0.0 52.2 jit_solution(6928983418822954492)
XLA Ops:
  0.6 1.0 %shard_map.104 = (f32[8,512]{1,0:T(8,128)S(1)}, f32[8,128]{1,0:T(8,128)S(1)}, s32[8,16]{1,0:T(8,128)S(1)}, s32[8,128]{1,0:T(8,128)S(1)}) custom-call(f32[3,512]{1,0:T(4,128)} %frac_in.1, s32[1,512]{1,0:T(1,128)} %bitcast.21, s32[8,16]{1,0:T(8,128)} %send_in.1, s32[2,6]{1,0:T(2,128)} %tile_in.1), custom_call_target="tpu_custom_call" | custom-call | tf_op jit(solution)/shard_map/pallas_call | solution.py:999
  1.6 3.4 %collective-permute-start = (f32[8,128]{1,0:T(8,128)S(1)}, f32[8,128]{1,0:T(8,128)S(1)}, u32[]{:S(2)}, u32[]{:S(2)}) collective-permute-start(f32[8,128]{1,0:T(8,128)S(1)} %get-tuple-element.108), channel_id=1, source_target_pairs={{0,28},{4,8},{8,4},{12,16},{16,12},{20,24},{24,20},{28,0},{1,29},{... | collective-permute-start | bytes 12296 | tf_op jit(solution)/shard_map/ppermute | solution.py:957
  5.0 0.0 collective-permute-start.1
  5.7 0.1 add_bitcast_fusion.words_ref
  5.8 1.3 %shard_map.105 = (bf16[256,640]{1,0:T(8,128)(2,1)S(1)}, bf16[256,640]{1,0:T(8,128)(2,1)S(1)}, bf16[2,128,128]{2,1,0:T(8,128)(2,1)S(1)}, bf16[2,128,128]{2,1,0:T(8,128)(2,1)S(1)}, f32[48,128]{1,0:T(8,128)S(1)}) custom-call(f32[6,128]{1,0:T(8,128)} %embed_in.1, f32[32,128]{1,0:T(8,128)} %bitcast.20, f32[1,128]{1,0:T(1,128)} %bitcast.22, f32[5,128,128]{2,1,0:T(8,128)} %mixing_in.1), custom_call_target="tpu_custom_call" | custom-call | tf_op jit(solution)/shard_map/pallas_call | solution.py:999
  7.1 0.0 collective-permute-done.far_in
  7.1 0.0 collective-permute-done.1.mate_in
  7.1 3.7 %collective-permute-start.2 = (f32[3,8,128]{2,1,0:T(8,128)S(1)}, f32[3,8,128]{2,1,0:T(8,128)S(1)}, u32[]{:S(2)}, u32[]{:S(2)}) collective-permute-start(f32[3,8,128]{2,1,0:T(8,128)S(1)} %pad_maximum_fusion.4), channel_id=1, source_target_pairs={{0,3},{1,2},{2,1},{3,0},{4,7},{5,6},{6,5},{7,4},{8,11},{9,10},{10,... | collective-permute-start | bytes 36872 | tf_op jit(solution)/shard_map/ppermute | solution.py:957
  10.8 0.0 collective-permute-start.3
  10.8 0.3 shard_map.106
  11.1 1.6 %collective-permute-done.2.zfar_in = f32[3,8,128]{2,1,0:T(8,128)S(1)} collective-permute-done((f32[3,8,128]{2,1,0:T(8,128)S(1)}, f32[3,8,128]{2,1,0:T(8,128)S(1)}, u32[]{:S(2)}, u32[]{:S(2)}) %collective-permute-start.2) | collective-permute-done | bytes 12320 | tf_op jit(solution)/shard_map/ppermute | solution.py:957
  12.7 1.7 %collective-permute-done.3.zmate_in = f32[3,8,128]{2,1,0:T(8,128)S(1)} collective-permute-done((f32[3,8,128]{2,1,0:T(8,128)S(1)}, f32[3,8,128]{2,1,0:T(8,128)S(1)}, u32[]{:S(2)}, u32[]{:S(2)}) %collective-permute-start.3) | collective-permute-done | bytes 12320 | tf_op jit(solution)/shard_map/ppermute | solution.py:958
  14.5 1.2 %shard_map.107 = (f32[512,256]{1,0:T(8,128)S(1)}, f32[3,16,256]{2,1,0:T(8,128)S(1)}, f32[3,16,256]{2,1,0:T(8,128)S(1)}, f32[2,16,256]{2,1,0:T(8,128)S(1)}, f32[1...) custom-call(s32[8,128]{1,0:T(8,128)S(1)} %get-tuple-element.121.cont, ...), custom_call_target="tpu_custom_call" | custom-call | tf_op jit(solution)/shard_map/pallas_call | solution.py:999
  15.7 0.4 collective-permute-start.4
  16.1 0.9 %collective-permute-start.5 = (f32[3,16,256]{2,1,0:T(8,128)S(1)}, f32[3,16,256]{2,1,0:T(8,128)S(1)}, u32[]{:S(2)}, u32[]{:S(2)}) collective-permute-start(f32[3,16,256]{2,1,0:T(8,128)S(1)} %get-tuple-element.133), channel_id=1, source_target_pairs={{0,4},{4,0},{8,12},{12,8},{16,20},{20,16},{24,28},{28,24},{1,5},{5... | collective-permute-start | bytes 147464 | tf_op jit(solution)/shard_map/ppermute | solution.py:958
  17.1 1.9 %shard_map.108 = (f32[512,640]{1,0:T(8,128)S(1)}, bf16[8,256,256]{2,1,0:T(8,128)(2,1)S(1)}, bf16[8,256,256]{2,1,0:T(8,128)(2,1)S(1)}, f32[512,128]{1,0:T(8,128)S(1)}) custom-call(f32[512,256]{1,0:T(8,128)S(1)} %get-tuple-element.136.hist_ref, f32[512,128]{1,0:T(8,128)S(1)} %get-tuple-element.123.col_ref, bf16[256,640]{1,0:T(8,128)(2,1)S(1)} %get-tuple-element.137.fold_high, ...), custom_call_target="tpu_custom_call" | custom-call | tf_op jit(solution)/shard_map/pallas_call | solution.py:999
  18.9 1.2 %collective-permute-done.4.far_in = f32[3,16,256]{2,1,0:T(8,128)S(1)} collective-permute-done((f32[3,16,256]{2,1,0:T(8,128)S(1)}, f32[3,16,256]{2,1,0:T(8,128)S(1)}, u32[]{:S(2)}, u32[]{:S(2)}) %collective-permute-start.4) | collective-permute-done | bytes 49184 | tf_op jit(solution)/shard_map/ppermute | solution.py:957
  20.1 0.0 collective-permute-done.5.mate_in
  20.2 1.9 %collective-permute-start.6 = (f32[3,16,256]{2,1,0:T(8,128)S(1)}, f32[3,16,256]{2,1,0:T(8,128)S(1)}, u32[]{:S(2)}, u32[]{:S(2)}) collective-permute-start(f32[3,16,256]{2,1,0:T(8,128)S(1)} %get-tuple-element.147), channel_id=1, source_target_pairs={{0,3},{1,2},{2,1},{3,0},{4,7},{5,6},{6,5},{7,4},{8,11},{9,10},{10,... | collective-permute-start | bytes 147464 | tf_op jit(solution)/shard_map/ppermute | solution.py:957
  22.0 0.0 collective-permute-start.7
  22.0 0.5 shard_map.109
  22.6 3.6 %collective-permute-done.6.zfar_in = f32[3,16,256]{2,1,0:T(8,128)S(1)} collective-permute-done((f32[3,16,256]{2,1,0:T(8,128)S(1)}, f32[3,16,256]{2,1,0:T(8,128)S(1)}, u32[]{:S(2)}, u32[]{:S(2)}) %collective-permute-start.6) | collective-permute-done | bytes 49184 | tf_op jit(solution)/shard_map/ppermute | solution.py:957
  26.2 0.5 collective-permute-done.7.zmate_in
  26.7 2.8 %shard_map.110 = (f32[3,16,256]{2,1,0:T(8,128)S(1)}, f32[3,16,256]{2,1,0:T(8,128)S(1)}, f32[2,16,256]{2,1,0:T(8,128)S(1)}, bf16[2,256,256]{2,1,0:T(8,128)(2,1)S(...) custom-call(s32[8,128]{1,0:T(8,128)S(1)} %get-tuple-element.121.cont, ...), custom_call_target="tpu_custom_call" | custom-call | tf_op jit(solution)/shard_map/pallas_call | solution.py:999
  29.5 0.9 %collective-permute-start.8 = (f32[3,16,256]{2,1,0:T(8,128)S(1)}, f32[3,16,256]{2,1,0:T(8,128)S(1)}, u32[]{:S(2)}, u32[]{:S(2)}) collective-permute-start(f32[3,16,256]{2,1,0:T(8,128)S(1)} %get-tuple-element.170), channel_id=1, source_target_pairs={{0,28},{4,8},{8,4},{12,16},{16,12},{20,24},{24,20},{28,0},{1,29},{... | collective-permute-start | bytes 147464 | tf_op jit(solution)/shard_map/ppermute | solution.py:957
  30.4 0.2 collective-permute-start.9
  30.6 0.3 shard_map.111.grad_feat
  31.0 3.0 %collective-permute-done.8.far_in = f32[3,16,256]{2,1,0:T(8,128)S(1)} collective-permute-done((f32[3,16,256]{2,1,0:T(8,128)S(1)}, f32[3,16,256]{2,1,0:T(8,128)S(1)}, u32[]{:S(2)}, u32[]{:S(2)}) %collective-permute-start.8) | collective-permute-done | bytes 49184 | tf_op jit(solution)/shard_map/ppermute | solution.py:957
  34.0 0.0 collective-permute-done.9.mate_in
  34.0 1.9 %collective-permute-start.10 = (f32[3,16,256]{2,1,0:T(8,128)S(1)}, f32[3,16,256]{2,1,0:T(8,128)S(1)}, u32[]{:S(2)}, u32[]{:S(2)}) collective-permute-start(f32[3,16,256]{2,1,0:T(8,128)S(1)} %get-tuple-element.183), channel_id=1, source_target_pairs={{0,3},{1,2},{2,1},{3,0},{4,7},{5,6},{6,5},{7,4},{8,11},{9,10},{10,... | collective-permute-start | bytes 147464 | tf_op jit(solution)/shard_map/ppermute | solution.py:957
  35.9 0.0 collective-permute-start.11
  35.9 1.3 %shard_map.112 = (f32[512,256]{1,0:T(8,128)S(1)}, f32[6,512,256]{2,1,0:T(8,128)S(1)}) custom-call(s32[8,128]{1,0:T(8,128)S(1)} %get-tuple-element.121.control_ref, bf16[256,640]{1,0:T(8,128)(2,1)S(1)} %get-tuple-element.137.fold_high, bf16[256,640]{1,0:T(8,128)(2,1)S(1)} %get-tuple-element.138.fold_low, f32[48,128]{1,0:T(8,128)S(1)} %get-tuple-element.139.weight_ref, ...), custom_call_target="tpu_custom_call" | custom-call | tf_op jit(solution)/shard_map/pallas_call | solution.py:999
  37.2 2.8 %collective-permute-done.10.zfar_in = f32[3,16,256]{2,1,0:T(8,128)S(1)} collective-permute-done((f32[3,16,256]{2,1,0:T(8,128)S(1)}, f32[3,16,256]{2,1,0:T(8,128)S(1)}, u32[]{:S(2)}, u32[]{:S(2)}) %collective-permute-start.10) | collective-permute-done | bytes 49184 | tf_op jit(solution)/shard_map/ppermute | solution.py:957
  40.0 0.5 collective-permute-done.11.zmate_in
  40.5 1.1 %shard_map.113 = (f32[8,128]{1,0:T(8,128)S(1)}, f32[512,256]{1,0:T(8,128)S(1)}, f32[512,128]{1,0:T(8,128)S(1)}) custom-call(s32[8,128]{1,0:T(8,128)S(1)} %get-tuple-element.121.control_ref, bf16[512,128]{1,0:T(8,128)(2,1)S(1)} %get-tuple-element.166.chosen_ref, f32[512,256]{1,0:T(8,128)S(1)} %get-tuple-element.179.pull_hist_ref, ...), custom_call_target="tpu_custom_call" | custom-call | tf_op jit(solution)/shard_map/pallas_call | solution.py:999
  41.7 0.4 collective-permute-start.12
  42.1 0.5 collective-permute-start.13
  42.6 0.8 %shard_map.114 = (f32[6,512,256]{2,1,0:T(8,128)S(1)}, f32[1,512]{1,0:T(1,128)}) custom-call(s32[8,128]{1,0:T(8,128)S(1)} %get-tuple-element.121.control_ref, f32[48,128]{1,0:T(8,128)S(1)} %get-tuple-element.139.weight_ref, f32[512,128]{1,0:T(8,128)S(1)} %get-tuple-element.174.pull_message, f32[512,128]{1,0:T(8,128)S(1)} %get-tuple-element.195.share_ref, ...), custom_call_target="tpu_custom_call" | custom-call | tf_op jit(solution)/shard_map/pallas_call | solution.py:999
  43.3 2.3 %collective-permute-done.12.far_in = f32[8,128]{1,0:T(8,128)S(1)} collective-permute-done((f32[8,128]{1,0:T(8,128)S(1)}, f32[8,128]{1,0:T(8,128)S(1)}, u32[]{:S(2)}, u32[]{:S(2)}) %collective-permute-start.12) | collective-permute-done | bytes 4128 | tf_op jit(solution)/shard_map/ppermute | solution.py:957
  45.7 0.0 collective-permute-done.13.mate_in
  45.7 1.8 %collective-permute-start.14 = (f32[3,8,128]{2,1,0:T(8,128)S(1)}, f32[3,8,128]{2,1,0:T(8,128)S(1)}, u32[]{:S(2)}, u32[]{:S(2)}) collective-permute-start(f32[3,8,128]{2,1,0:T(8,128)S(1)} %pad_maximum_fusion.5), channel_id=1, source_target_pairs={{0,3},{1,2},{2,1},{3,0},{4,7},{5,6},{6,5},{7,4},{8,11},{9,10},{10,... | collective-permute-start | bytes 36872 | tf_op jit(solution)/shard_map/ppermute | solution.py:957
  47.5 0.0 collective-permute-start.15
  47.5 0.2 shard_map.115
  47.7 3.5 %collective-permute-done.14.zfar_in = f32[3,8,128]{2,1,0:T(8,128)S(1)} collective-permute-done((f32[3,8,128]{2,1,0:T(8,128)S(1)}, f32[3,8,128]{2,1,0:T(8,128)S(1)}, u32[]{:S(2)}, u32[]{:S(2)}) %collective-permute-start.14) | collective-permute-done | bytes 12320 | tf_op jit(solution)/shard_map/ppermute | solution.py:957
  51.2 0.1 collective-permute-done.15.zmate_in
  51.3 0.9 %shard_map.116 = f32[3,512]{1,0:T(4,128)} custom-call(s32[8,128]{1,0:T(8,128)S(1)} %get-tuple-element.121.control_ref, bf16[128,512]{1,0:T(8,128)(2,1)S(1)} %get-tuple-element.202.turned_ref, f32[8,512]{1,0:T(8,128)S(1)} %get-tuple-element.203.own_ref, f32[8,128]{1,0:T(8,128)S(1)} %collective-permute-done.13.mate_in, ...), custom_call_target="tpu_custom_call" | custom-call | tf_op jit(solution)/shard_map/pallas_call | solution.py:999
  (9 shorter events, 0.0 us)
Async XLA Ops:
  1.6 5.4 %collective-permute-start = (f32[8,128]{1,0:T(8,128)S(1)}, f32[8,128]{1,0:T(8,128)S(1)}, u32[]{:S(2)}, u32[]{:S(2)}) collective-permute-start(f32[8,128]{1,0:T(8,128)S(1)} %get-tuple-element.108), channel_id=1, source_target_pairs={{0,28},{4,8},{8,4},{12,16},{16,12},{20,24},{24,20},{28,0},{1,29},{... | collective-permute-start | bytes 12296 | tf_op jit(solution)/shard_map/ppermute | solution.py:957
  5.0 2.0 %collective-permute-start.1 = (f32[8,128]{1,0:T(8,128)S(1)}, f32[8,128]{1,0:T(8,128)S(1)}, u32[]{:S(2)}, u32[]{:S(2)}) collective-permute-start(f32[8,128]{1,0:T(8,128)S(1)} %get-tuple-element.108), channel_id=1, source_target_pairs={{0,4},{4,0},{8,12},{12,8},{16,20},{20,16},{24,28},{28,24},{1,5},{5... | collective-permute-start | bytes 12296 | tf_op jit(solution)/shard_map/ppermute | solution.py:958
  7.1 5.6 %collective-permute-start.2 = (f32[3,8,128]{2,1,0:T(8,128)S(1)}, f32[3,8,128]{2,1,0:T(8,128)S(1)}, u32[]{:S(2)}, u32[]{:S(2)}) collective-permute-start(f32[3,8,128]{2,1,0:T(8,128)S(1)} %pad_maximum_fusion.4), channel_id=1, source_target_pairs={{0,3},{1,2},{2,1},{3,0},{4,7},{5,6},{6,5},{7,4},{8,11},{9,10},{10,... | collective-permute-start | bytes 36872 | tf_op jit(solution)/shard_map/ppermute | solution.py:957
  10.8 3.7 %collective-permute-start.3 = (f32[3,8,128]{2,1,0:T(8,128)S(1)}, f32[3,8,128]{2,1,0:T(8,128)S(1)}, u32[]{:S(2)}, u32[]{:S(2)}) collective-permute-start(f32[3,8,128]{2,1,0:T(8,128)S(1)} %pad_maximum_fusion.4), channel_id=1, source_target_pairs={{0,1},{1,0},{2,3},{3,2},{4,5},{5,4},{6,7},{7,6},{8,9},{9,8},{10,11... | collective-permute-start | bytes 36872 | tf_op jit(solution)/shard_map/ppermute | solution.py:958
  15.7 4.5 %collective-permute-start.4 = (f32[3,16,256]{2,1,0:T(8,128)S(1)}, f32[3,16,256]{2,1,0:T(8,128)S(1)}, u32[]{:S(2)}, u32[]{:S(2)}) collective-permute-start(f32[3,16,256]{2,1,0:T(8,128)S(1)} %get-tuple-element.132), channel_id=1, source_target_pairs={{0,28},{4,8},{8,4},{12,16},{16,12},{20,24},{24,20},{28,0},{1,29},{... | collective-permute-start | bytes 147464 | tf_op jit(solution)/shard_map/ppermute | solution.py:957
  16.1 4.0 %collective-permute-start.5 = (f32[3,16,256]{2,1,0:T(8,128)S(1)}, f32[3,16,256]{2,1,0:T(8,128)S(1)}, u32[]{:S(2)}, u32[]{:S(2)}) collective-permute-start(f32[3,16,256]{2,1,0:T(8,128)S(1)} %get-tuple-element.133), channel_id=1, source_target_pairs={{0,4},{4,0},{8,12},{12,8},{16,20},{20,16},{24,28},{28,24},{1,5},{5... | collective-permute-start | bytes 147464 | tf_op jit(solution)/shard_map/ppermute | solution.py:958
  20.2 6.0 %collective-permute-start.6 = (f32[3,16,256]{2,1,0:T(8,128)S(1)}, f32[3,16,256]{2,1,0:T(8,128)S(1)}, u32[]{:S(2)}, u32[]{:S(2)}) collective-permute-start(f32[3,16,256]{2,1,0:T(8,128)S(1)} %get-tuple-element.147), channel_id=1, source_target_pairs={{0,3},{1,2},{2,1},{3,0},{4,7},{5,6},{6,5},{7,4},{8,11},{9,10},{10,... | collective-permute-start | bytes 147464 | tf_op jit(solution)/shard_map/ppermute | solution.py:957
  22.0 4.6 %collective-permute-start.7 = (f32[3,16,256]{2,1,0:T(8,128)S(1)}, f32[3,16,256]{2,1,0:T(8,128)S(1)}, u32[]{:S(2)}, u32[]{:S(2)}) collective-permute-start(f32[3,16,256]{2,1,0:T(8,128)S(1)} %get-tuple-element.148), channel_id=1, source_target_pairs={{0,1},{1,0},{2,3},{3,2},{4,5},{5,4},{6,7},{7,6},{8,9},{9,8},{10,11... | collective-permute-start | bytes 147464 | tf_op jit(solution)/shard_map/ppermute | solution.py:958
  29.5 4.5 %collective-permute-start.8 = (f32[3,16,256]{2,1,0:T(8,128)S(1)}, f32[3,16,256]{2,1,0:T(8,128)S(1)}, u32[]{:S(2)}, u32[]{:S(2)}) collective-permute-start(f32[3,16,256]{2,1,0:T(8,128)S(1)} %get-tuple-element.170), channel_id=1, source_target_pairs={{0,28},{4,8},{8,4},{12,16},{16,12},{20,24},{24,20},{28,0},{1,29},{... | collective-permute-start | bytes 147464 | tf_op jit(solution)/shard_map/ppermute | solution.py:957
  30.4 3.6 %collective-permute-start.9 = (f32[3,16,256]{2,1,0:T(8,128)S(1)}, f32[3,16,256]{2,1,0:T(8,128)S(1)}, u32[]{:S(2)}, u32[]{:S(2)}) collective-permute-start(f32[3,16,256]{2,1,0:T(8,128)S(1)} %get-tuple-element.171), channel_id=1, source_target_pairs={{0,4},{4,0},{8,12},{12,8},{16,20},{20,16},{24,28},{28,24},{1,5},{5... | collective-permute-start | bytes 147464 | tf_op jit(solution)/shard_map/ppermute | solution.py:958
  34.0 6.0 %collective-permute-start.10 = (f32[3,16,256]{2,1,0:T(8,128)S(1)}, f32[3,16,256]{2,1,0:T(8,128)S(1)}, u32[]{:S(2)}, u32[]{:S(2)}) collective-permute-start(f32[3,16,256]{2,1,0:T(8,128)S(1)} %get-tuple-element.183), channel_id=1, source_target_pairs={{0,3},{1,2},{2,1},{3,0},{4,7},{5,6},{6,5},{7,4},{8,11},{9,10},{10,... | collective-permute-start | bytes 147464 | tf_op jit(solution)/shard_map/ppermute | solution.py:957
  35.9 4.6 %collective-permute-start.11 = (f32[3,16,256]{2,1,0:T(8,128)S(1)}, f32[3,16,256]{2,1,0:T(8,128)S(1)}, u32[]{:S(2)}, u32[]{:S(2)}) collective-permute-start(f32[3,16,256]{2,1,0:T(8,128)S(1)} %get-tuple-element.184), channel_id=1, source_target_pairs={{0,1},{1,0},{2,3},{3,2},{4,5},{5,4},{6,7},{7,6},{8,9},{9,8},{10,11... | collective-permute-start | bytes 147464 | tf_op jit(solution)/shard_map/ppermute | solution.py:958
  41.7 4.0 %collective-permute-start.12 = (f32[8,128]{1,0:T(8,128)S(1)}, f32[8,128]{1,0:T(8,128)S(1)}, u32[]{:S(2)}, u32[]{:S(2)}) collective-permute-start(f32[8,128]{1,0:T(8,128)S(1)} %get-tuple-element.192), channel_id=1, source_target_pairs={{0,28},{4,8},{8,4},{12,16},{16,12},{20,24},{24,20},{28,0},{1,29},{... | collective-permute-start | bytes 12296 | tf_op jit(solution)/shard_map/ppermute | solution.py:957
  42.1 3.6 %collective-permute-start.13 = (f32[8,128]{1,0:T(8,128)S(1)}, f32[8,128]{1,0:T(8,128)S(1)}, u32[]{:S(2)}, u32[]{:S(2)}) collective-permute-start(f32[8,128]{1,0:T(8,128)S(1)} %get-tuple-element.192), channel_id=1, source_target_pairs={{0,4},{4,0},{8,12},{12,8},{16,20},{20,16},{24,28},{28,24},{1,5},{5... | collective-permute-start | bytes 12296 | tf_op jit(solution)/shard_map/ppermute | solution.py:958
  45.7 5.5 %collective-permute-start.14 = (f32[3,8,128]{2,1,0:T(8,128)S(1)}, f32[3,8,128]{2,1,0:T(8,128)S(1)}, u32[]{:S(2)}, u32[]{:S(2)}) collective-permute-start(f32[3,8,128]{2,1,0:T(8,128)S(1)} %pad_maximum_fusion.5), channel_id=1, source_target_pairs={{0,3},{1,2},{2,1},{3,0},{4,7},{5,6},{6,5},{7,4},{8,11},{9,10},{10,... | collective-permute-start | bytes 36872 | tf_op jit(solution)/shard_map/ppermute | solution.py:957
  47.5 3.8 %collective-permute-start.15 = (f32[3,8,128]{2,1,0:T(8,128)S(1)}, f32[3,8,128]{2,1,0:T(8,128)S(1)}, u32[]{:S(2)}, u32[]{:S(2)}) collective-permute-start(f32[3,8,128]{2,1,0:T(8,128)S(1)} %pad_maximum_fusion.5), channel_id=1, source_target_pairs={{0,1},{1,0},{2,3},{3,2},{4,5},{5,4},{6,7},{7,6},{8,9},{9,8},{10,11... | collective-permute-start | bytes 36872 | tf_op jit(solution)/shard_map/ppermute | solution.py:958

commit v3 on v2

--- a/solution.py
+++ b/solution.py
@@ -98,16 +98,40 @@
 
 
 def pick_all(args):
-    return jnp.concatenate([pick_slot(slot, *args) for slot in range(8)], axis=0)
+    return jnp.concatenate([unpack(pick_slot(slot, *args)) for slot in range(8)], axis=0)
+
+
+def pack(rows):
+    free = iota((8, 128), 1) % SPAN >= 6
+    carried = rows[8:16, 128:256]
+    quarters = (rows[0:8, 0:128], rows[8:16, 0:128], rows[0:8, 128:256])
+    return jnp.concatenate(
+        [
+            jnp.where(free, pltpu.roll(carried, 6 - 2 * part, 1), quarter)
+            for part, quarter in enumerate(quarters)
+        ],
+        axis=0,
+    )
+
+
+def unpack(packet):
+    place = iota((8, 128), 1) % SPAN
+    turned = [
+        pltpu.roll(packet[8 * part : 8 * part + 8], 128 - (6 - 2 * part), 1) for part in range(3)
+    ]
+    carried = jnp.where(place < 2, turned[0], jnp.where(place < 4, turned[1], turned[2]))
+    return jnp.concatenate(
+        [packet[0:16], jnp.concatenate([packet[16:24], carried], axis=0)], axis=1
+    )
 
 
 def put_packets(even_x, piece, mate_ref, far_ref, side_ref):
     for part in range(3):
-        down, up = piece(part), piece(5 + part)
+        down, up = pack(piece(part)), pack(piece(5 + part))
         mate_ref[part] = jnp.where(even_x, up, down)
         far_ref[part] = jnp.where(even_x, down, up)
-    side_ref[0] = piece(3)
-    side_ref[1] = piece(4)
+    side_ref[0] = pack(piece(3))
+    side_ref[1] = pack(piece(4))
 
 
 def send_columns(send):
@@ -284,22 +308,24 @@
     control_ref[...] = table
 
 
-def listed_tiles(control_ref, which, work):
+def listed_tile(control_ref, which, place):
     first = 3 + 3 * which
-    count = control_ref[3 + which, 2]
-
-    def entry(place):
-        return tuple(control_ref[place, first + k] for k in range(3))
+    return tuple(control_ref[place, first + k] for k in range(3))
+
+
+def listed_tiles(control_ref, which, work, start=0):
+    count = control_ref[3 + which, 2] - start
 
     def step(half, carried):
-        work([entry(2 * half), entry(2 * half + 1)])
+        place = start + 2 * half
+        work([listed_tile(control_ref, which, place + k) for k in range(2)])
         return carried
 
     lax.fori_loop(0, count // 2, step, 0)
 
     @pl.when(count % 2 == 1)
     def _():
-        work([entry(count - 1)])
+        work([listed_tile(control_ref, which, start + count - 1)])
 
 
 def own_tiles(control_ref, work):
@@ -307,8 +333,25 @@
 
 
 def ghost_tiles(control_ref, work):
-    work([(slot, control_ref[slot, 0], slot) for slot in range(2)])
-    listed_tiles(control_ref, 0, work)
+    more = control_ref[3, 2]
+
+    def fixed():
+        return [(slot, control_ref[slot, 0], slot) for slot in range(2)]
+
+    @pl.when(more == 0)
+    def _():
+        work(fixed())
+
+    @pl.when(more > 0)
+    def _():
+        @pl.when(more == 1)
+        def _():
+            work(fixed() + [listed_tile(control_ref, 0, 0)])
+
+        @pl.when(more > 1)
+        def _():
+            work(fixed() + [listed_tile(control_ref, 0, place) for place in range(2)])
+            listed_tiles(control_ref, 0, work, 2)
 
 
 def exact_pick(rows, chosen):
@@ -413,29 +456,10 @@
             hist_ref[block_rows(left), half * 128 : half * 128 + 128] += total
 
 
-def prepare_kernel(
-    words_ref,
-    tiles_ref,
-    site_ref,
-    send_ref,
-    control_ref,
-    col_ref,
-    row_ref,
-    hist_ref,
-    pair_high,
-    pair_low,
-    chosen_ref,
+def own_histogram_kernel(
+    control_ref, col_ref, row_ref, hist_ref, pair_high, pair_low
 ):
-    atoms = site_ref.shape[1]
-    blocks = atoms // BLOCK
-    fill_control(control_ref, words_ref, tiles_ref, pair_high.shape[0], blocks)
-    own = site_ref[...] * axis_scale()[:, 0:1]
-    col_ref[...] = upright(own)
-    for block in range(blocks):
-        row_ref[block] = doubled(own, block)
-    chosen_ref[...] = chooser(send_ref[...], atoms).astype(F32).astype(BF16)
     hist_ref[...] = jnp.zeros_like(hist_ref)
-
     own_tiles(
         control_ref,
         lambda tiles: add_histograms(
@@ -444,11 +468,20 @@
     )
 
 
-def fold_kernel(
+def prepare_kernel(
+    slots,
+    words_ref,
+    tiles_ref,
+    site_ref,
+    send_ref,
     embed_in,
     radial_in,
     readout_in,
     mixing_in,
+    control_ref,
+    col_ref,
+    row_ref,
+    chosen_ref,
     fold_high,
     fold_low,
     mix_high,
@@ -469,6 +502,14 @@
         ),
         sems,
     )
+    atoms = site_ref.shape[1]
+    blocks = atoms // BLOCK
+    fill_control(control_ref, words_ref, tiles_ref, slots, blocks)
+    own = site_ref[...] * axis_scale()[:, 0:1]
+    col_ref[...] = upright(own)
+    for block in range(blocks):
+        row_ref[block] = doubled(own, block)
+    chosen_ref[...] = chooser(send_ref[...], atoms).astype(F32).astype(BF16)
     for copy in copies:
         copy.wait()
 
@@ -513,6 +554,7 @@
     ghost_row,
     pair_high,
     pair_low,
+    gather_ref,
     send_ref,
     sem,
 ):
@@ -545,9 +587,12 @@
     places = [(mate_ref, part, up + part) for part in range(3)]
     places += [(far_ref, part, down + part) for part in range(3)]
     places += [(side_ref, part, 3 + part) for part in range(2)]
-    for ref, part, slot in places:
+    for place, (_, _, slot) in enumerate(places):
         for entry in range(GHOSTS):
-            ref[part, entry : entry + 1, :] = hist_ref[pl.ds(send_ref[slot, entry], 1), :]
+            row = place * GHOSTS + entry
+            gather_ref[row : row + 1, :] = hist_ref[pl.ds(send_ref[slot, entry], 1), :]
+    for place, (ref, part, _) in enumerate(places):
+        ref[part] = pack(gather_ref[place * GHOSTS : place * GHOSTS + GHOSTS, :])
 
 
 def make_features(block, col_ref, kinds, weight_ref, pre_ref, feat_high, feat_low, scalar_ref):
@@ -764,13 +809,17 @@
     )
 
 
-def second_pull_kernel(
+def own_pull_kernel(
     control_ref,
     col_ref,
     row_ref,
+    fold_high,
+    fold_low,
     weight_ref,
+    pre_ref,
     pull_message,
     direct_ref,
+    pull_hist_ref,
     grad_feat,
     swap_high,
     swap_low,
@@ -789,6 +838,8 @@
         )
 
     own_tiles(control_ref, backward)
+    pulled = pull_features(grad_feat, pre_ref)
+    pull_hist_ref[...] = mm3(split(pulled), (fold_high[...], fold_low[...]), ROWROW)
 
 
 def pair_pulls(tiles, pull_message, weight_ref, high_ref, low_ref, pull_ref):
@@ -808,22 +859,7 @@
         pull_ref[slot] = one
 
 
-def ghost_pair_kernel(
-    control_ref,
-    fold_high,
-    fold_low,
-    weight_ref,
-    pre_ref,
-    grad_feat,
-    pull_message,
-    ghost_high,
-    ghost_low,
-    pull_hist_ref,
-    pull_ref,
-):
-    pulled = pull_features(grad_feat, pre_ref)
-    pull_hist_ref[...] = mm3(split(pulled), (fold_high[...], fold_low[...]), ROWROW)
-
+def ghost_pair_kernel(control_ref, weight_ref, pull_message, ghost_high, ghost_low, pull_ref):
     ghost_tiles(
         control_ref,
         lambda tiles: pair_pulls(tiles, pull_message, weight_ref, ghost_high, ghost_low, pull_ref),
@@ -1019,7 +1055,7 @@
         readout[None],
         mixing,
     )
-    packets = [struct(3, GHOSTS, HIST), struct(3, GHOSTS, HIST), struct(2, GHOSTS, HIST)]
+    packets = [struct(3, 24, 128), struct(3, 24, 128), struct(2, 24, 128)]
     hist_struct = struct(atoms, HIST)
     col_struct = struct(atoms, 128)
     own_rows, ghost_rows = struct(blocks, 8, 128), struct(2, 8, 128)
@@ -1045,31 +1081,37 @@
             pltpu.SemaphoreType.DMA((4,)),
         ],
     )(*far_arrays[0:4])
-    folded = call(
-        fold_kernel,
-        [HBM] * 4,
-        fold_halves + mix_halves + [struct(2 * SPAN + 4 * BASIS, 128)],
+    prepared = call(
+        functools.partial(prepare_kernel, slots),
+        [VMEM] * 4 + [HBM] * 4,
+        [
+            struct(8, 128, dtype=jnp.int32), col_struct, own_rows,
+            struct(atoms, 128, dtype=BF16),
+        ]
+        + fold_halves
+        + mix_halves
+        + [struct(2 * SPAN + 4 * BASIS, 128)],
         [
             pltpu.VMEM((HIST, 640), F32),
             pltpu.VMEM(mixing.shape, F32),
             pltpu.SemaphoreType.DMA((4,)),
         ],
-    )(*far_arrays[4:])
-    arrived, (words, site, folded) = exchange_rows(rows, (words, site, folded))
-    fold_high, fold_low, mix_high, mix_low, weights = folded
+    )(words, tiles, site, send, *far_arrays[4:])
+    arrived, prepared = exchange_rows(rows, prepared)
+    control, col, row, chosen, fold_high, fold_low, mix_high, mix_low, weights = prepared
     fold, mix = (fold_high, fold_low), (mix_high, mix_low)
-    control, col, row, hist, own_high, own_low, chosen = call(
-        prepare_kernel,
-        [VMEM] * 4,
-        [struct(8, 128, dtype=jnp.int32), col_struct, own_rows, hist_struct]
-        + pairs
-        + [struct(atoms, 128, dtype=BF16)],
-    )(words, tiles, site, send)
+    hist, own_high, own_low = call(
+        own_histogram_kernel, [VMEM] * 3, [hist_struct] + pairs
+    )(control, col, row)
     hist, to_mate, to_far, side, ghost_col, ghost_row, pair_high, pair_low = call(
         first_kernel,
         [VMEM] * 8,
         [hist_struct] + packets + [struct(8 * GHOSTS, 128), ghost_rows] + pairs,
-        [pltpu.SMEM(send_list.shape, jnp.int32), pltpu.SemaphoreType.DMA],
+        [
+            pltpu.VMEM((8 * GHOSTS, HIST), F32),
+            pltpu.SMEM(send_list.shape, jnp.int32),
+            pltpu.SemaphoreType.DMA,
+        ],
     )(control, send, hist, col, *arrived)
     features = call(
         functools.partial(feature_kernel, kinds),
@@ -1096,21 +1138,21 @@
         control, *arrived, ghost_col, *fold, *mix, weights, scalar, message,
         pair_high, pair_low, swap_high, swap_low,
     )
-    grad_feat = call(
-        second_pull_kernel,
-        [VMEM] * 6,
-        struct(atoms, 512),
-        [pltpu.VMEM((2, 256, BASIS * BLOCK), BF16)] * 2,
-    )(control, col, row, weights, pull_message, direct)
-    arrived, grad_feat = exchange_packets(even_y, to_mate, to_far, side, grad_feat)
-    pull_hist, pull = call(ghost_pair_kernel, [VMEM] * 9, [hist_struct, pulls])(
-        control, *fold, weights, pre, grad_feat, pull_message, ghost_high, ghost_low
-    )
+    pull = call(ghost_pair_kernel, [VMEM] * 5, pulls)(
+        control, weights, pull_message, ghost_high, ghost_low
+    )
+    arrived, (pull, direct) = exchange_packets(even_y, to_mate, to_far, side, (pull, direct))
+    pull_hist = call(
+        own_pull_kernel,
+        [VMEM] * 9,
+        hist_struct,
+        [pltpu.VMEM((atoms, 512), F32)] + [pltpu.VMEM((2, 256, BASIS * BLOCK), BF16)] * 2,
+    )(control, col, row, *fold, weights, pre, pull_message, direct)
     rows, total, grad_col = call(
         third_ghost_kernel,
         [VMEM] * 11,
         [struct(8, 128), hist_struct, col_struct],
-        [pltpu.VMEM((2, 8, 128), F32), pltpu.VMEM((2, BASIS * BLOCK, 256), F32)],
+        [pltpu.VMEM((2, 8, 128), F32), pltpu.VMEM((4, BASIS * BLOCK, 256), F32)],
     )(control, chosen, pull_hist, *arrived, col, ghost_col, ghost_row, pull)
     share, rows = lax.optimization_barrier((share, rows))
     own_pair = call(own_pair_kernel, [VMEM] * 6, [pulls, struct(1, atoms)])(

time: 52.4 us -> 53.1 us (1.013)
  starting transfers between devices: 16 us -> 12 us
  Pallas kernels: 13.7 us -> 17.5 us
  waiting for transfers between devices: 20.9 us -> 22.3 us
    pallas_call x13, Pallas kernels: 13.7 us -> 17.5 us  [run(): return made(*placed)]
    ppermute x8, starting transfers between devices: 14.4 us -> 11.3 us  [swap_both(): far = lax.ppermute(to_far, axis, partners(axis, True))]
    ppermute x8, waiting for transfers between devices: 18.1 us -> 20.5 us  [swap_both(): far = lax.ppermute(to_far, axis, partners(axis, True))]
    ppermute x8, waiting for transfers between devices: 2.81 us -> 1.76 us  [swap_both(): mate = lax.ppermute(to_mate, axis, partners(axis, False))]
    ppermute x8, starting transfers between devices: 1.65 us -> 0.78 us  [swap_both(): mate = lax.ppermute(to_mate, axis, partners(axis, False))]
  transfers between devices with their start and end apart: 16 -> 16, of which waited for: 11 -> 8; matrix products, arithmetic and copies ran while one was open for 0% -> 0% of each run, Pallas kernels for 13% -> 14%
where the time goes in v3:
time: 53.1 us; the launch traced here: 53.4 us
  waiting for transfers between devices  22.3 us (42%)
  Pallas kernels  17.5 us (33%)
  starting transfers between devices  12 us (23%)
  between operations  1.48 us (3%)
    ppermute x8, waiting for transfers between devices, swap_both(): far = lax.ppermute(to_far, axis, partners(axis, True))  20.5 us
    pallas_call x13, Pallas kernels, run(): return made(*placed)  17.5 us
    ppermute x8, starting transfers between devices, swap_both(): far = lax.ppermute(to_far, axis, partners(axis, True))  11.3 us
    ppermute x8, waiting for transfers between devices, swap_both(): mate = lax.ppermute(to_mate, axis, partners(axis, False))  1.76 us
  transfers between devices with their start and end apart: 16, of which 8 were waited for; matrix products, arithmetic and copies ran while one was open for 0% of the time, Pallas kernels for 14%

profile of v3, /device:TPU:0, one launch (start us, length us, event | category | flops | bytes accessed | tf_op | source)
XLA Modules:
  0.0 53.4 jit_solution(17987878671406527363)
XLA Ops:
  0.6 1.0 %shard_map.104 = (f32[8,512]{1,0:T(8,128)S(1)}, f32[8,128]{1,0:T(8,128)S(1)}, s32[8,16]{1,0:T(8,128)S(1)}, s32[8,128]{1,0:T(8,128)S(1)}) custom-call(f32[3,512]{1,0:T(4,128)} %frac_in.1, s32[1,512]{1,0:T(1,128)} %bitcast.21, s32[8,16]{1,0:T(8,128)} %send_in.1, s32[2,6]{1,0:T(2,128)} %tile_in.1), custom_call_target="tpu_custom_call" | custom-call | tf_op jit(solution)/shard_map/pallas_call | solution.py:1035
  1.6 3.4 %collective-permute-start = (f32[8,128]{1,0:T(8,128)S(1)}, f32[8,128]{1,0:T(8,128)S(1)}, u32[]{:S(2)}, u32[]{:S(2)}) collective-permute-start(f32[8,128]{1,0:T(8,128)S(1)} %get-tuple-element.109), channel_id=1, source_target_pairs={{0,28},{4,8},{8,4},{12,16},{16,12},{20,24},{24,20},{28,0},{1,29},{... | collective-permute-start | bytes 12296 | tf_op jit(solution)/shard_map/ppermute | solution.py:993
  5.0 0.0 collective-permute-start.1
  5.7 0.1 add_bitcast_fusion.words_ref
  5.8 1.4 %shard_map.105 = (s32[8,128]{1,0:T(8,128)S(1)}, f32[512,128]{1,0:T(8,128)S(1)}, f32[8,8,128]{2,1,0:T(8,128)S(1)}, bf16[512,128]{1,0:T(8,128)(2,1)S(1)}, bf16[256...) custom-call(s32[1,3]{1,0:T(1,128)S(1)} %add_bitcast_fusion.words_ref, ...), custom_call_target="tpu_custom_call" | custom-call | tf_op jit(solution)/shard_map/pallas_call | solution.py:1035
  7.2 0.0 collective-permute-done.far_in
  7.2 0.0 collective-permute-done.1.mate_in
  7.2 3.7 %collective-permute-start.2 = (f32[3,8,128]{2,1,0:T(8,128)S(1)}, f32[3,8,128]{2,1,0:T(8,128)S(1)}, u32[]{:S(2)}, u32[]{:S(2)}) collective-permute-start(f32[3,8,128]{2,1,0:T(8,128)S(1)} %pad_maximum_fusion.4), channel_id=1, source_target_pairs={{0,3},{1,2},{2,1},{3,0},{4,7},{5,6},{6,5},{7,4},{8,11},{9,10},{10,... | collective-permute-start | bytes 36872 | tf_op jit(solution)/shard_map/ppermute | solution.py:993
  10.9 0.0 collective-permute-start.3
  10.9 0.1 shard_map.106
  11.0 1.8 %collective-permute-done.2.zfar_in = f32[3,8,128]{2,1,0:T(8,128)S(1)} collective-permute-done((f32[3,8,128]{2,1,0:T(8,128)S(1)}, f32[3,8,128]{2,1,0:T(8,128)S(1)}, u32[]{:S(2)}, u32[]{:S(2)}) %collective-permute-start.2) | collective-permute-done | bytes 12320 | tf_op jit(solution)/shard_map/ppermute | solution.py:993
  12.8 1.7 %collective-permute-done.3.zmate_in = f32[3,8,128]{2,1,0:T(8,128)S(1)} collective-permute-done((f32[3,8,128]{2,1,0:T(8,128)S(1)}, f32[3,8,128]{2,1,0:T(8,128)S(1)}, u32[]{:S(2)}, u32[]{:S(2)}) %collective-permute-start.3) | collective-permute-done | bytes 12320 | tf_op jit(solution)/shard_map/ppermute | solution.py:994
  14.6 2.0 %shard_map.107 = (f32[512,256]{1,0:T(8,128)S(1)}, f32[3,24,128]{2,1,0:T(8,128)S(1)}, f32[3,24,128]{2,1,0:T(8,128)S(1)}, f32[2,24,128]{2,1,0:T(8,128)S(1)}, f32[1...) custom-call(s32[8,128]{1,0:T(8,128)S(1)} %get-tuple-element.124.cont, ...), custom_call_target="tpu_custom_call" | custom-call | tf_op jit(solution)/shard_map/pallas_call | solution.py:1035
  16.6 0.1 collective-permute-start.4
  16.7 0.6 %collective-permute-start.5 = (f32[3,24,128]{2,1,0:T(8,128)S(1)}, f32[3,24,128]{2,1,0:T(8,128)S(1)}, u32[]{:S(2)}, u32[]{:S(2)}) collective-permute-start(f32[3,24,128]{2,1,0:T(8,128)S(1)} %get-tuple-element.137), channel_id=1, source_target_pairs={{0,4},{4,0},{8,12},{12,8},{16,20},{20,16},{24,28},{28,24},{1,5},{5... | collective-permute-start | bytes 110600 | tf_op jit(solution)/shard_map/ppermute | solution.py:994
  17.3 1.9 %shard_map.108 = (f32[512,640]{1,0:T(8,128)S(1)}, bf16[8,256,256]{2,1,0:T(8,128)(2,1)S(1)}, bf16[8,256,256]{2,1,0:T(8,128)(2,1)S(1)}, f32[512,128]{1,0:T(8,128)S(1)}) custom-call(f32[512,256]{1,0:T(8,128)S(1)} %get-tuple-element.140.hist_ref, f32[512,128]{1,0:T(8,128)S(1)} %get-tuple-element.125.col_ref, bf16[256,640]{1,0:T(8,128)(2,1)S(1)} %get-tuple-element.141.fold_high, ...), custom_call_target="tpu_custom_call" | custom-call | tf_op jit(solution)/shard_map/pallas_call | solution.py:1035
  19.2 1.8 %collective-permute-done.4.far_in = f32[3,24,128]{2,1,0:T(8,128)S(1)} collective-permute-done((f32[3,24,128]{2,1,0:T(8,128)S(1)}, f32[3,24,128]{2,1,0:T(8,128)S(1)}, u32[]{:S(2)}, u32[]{:S(2)}) %collective-permute-start.4) | collective-permute-done | bytes 36896 | tf_op jit(solution)/shard_map/ppermute | solution.py:993
  21.0 0.0 collective-permute-done.5.mate_in
  21.0 1.2 %collective-permute-start.6 = (f32[3,24,128]{2,1,0:T(8,128)S(1)}, f32[3,24,128]{2,1,0:T(8,128)S(1)}, u32[]{:S(2)}, u32[]{:S(2)}) collective-permute-start(f32[3,24,128]{2,1,0:T(8,128)S(1)} %get-tuple-element.151), channel_id=1, source_target_pairs={{0,3},{1,2},{2,1},{3,0},{4,7},{5,6},{6,5},{7,4},{8,11},{9,10},{10,... | collective-permute-start | bytes 110600 | tf_op jit(solution)/shard_map/ppermute | solution.py:993
  22.2 0.0 collective-permute-start.7
  22.2 0.9 %shard_map.109 = (f32[512,128]{1,0:T(8,128)S(1)}, bf16[6,256,512]{2,1,0:T(8,128)(2,1)S(1)}, bf16[6,256,512]{2,1,0:T(8,128)(2,1)S(1)}) custom-call(s32[8,128]{1,0:T(8,128)S(1)} %get-tuple-element.124.control_ref, f32[8,8,128]{2,1,0:T(8,128)S(1)} %get-tuple-element.126.row_ref, f32[128,128]{1,0:T(8,128)S(1)} %get-tuple-element.155.ghost_col, ...), custom_call_target="tpu_custom_call" | custom-call | tf_op jit(solution)/shard_map/pallas_call | solution.py:1035
  23.1 3.7 %collective-permute-done.6.zfar_in = f32[3,24,128]{2,1,0:T(8,128)S(1)} collective-permute-done((f32[3,24,128]{2,1,0:T(8,128)S(1)}, f32[3,24,128]{2,1,0:T(8,128)S(1)}, u32[]{:S(2)}, u32[]{:S(2)}) %collective-permute-start.6) | collective-permute-done | bytes 36896 | tf_op jit(solution)/shard_map/ppermute | solution.py:993
  26.8 0.0 collective-permute-done.7.zmate_in
  26.8 4.2 %shard_map.110 = (f32[3,24,128]{2,1,0:T(8,128)S(1)}, f32[3,24,128]{2,1,0:T(8,128)S(1)}, f32[2,24,128]{2,1,0:T(8,128)S(1)}, bf16[2,256,256]{2,1,0:T(8,128)(2,1)S(...) custom-call(s32[8,128]{1,0:T(8,128)S(1)} %get-tuple-element.124.cont, ...), custom_call_target="tpu_custom_call" | custom-call | tf_op jit(solution)/shard_map/pallas_call | solution.py:1035
  31.0 0.1 collective-permute-start.8
  31.1 0.1 collective-permute-start.9
  31.2 1.2 %shard_map.111.pull_in = f32[6,512,256]{2,1,0:T(8,128)S(1)} custom-call(s32[8,128]{1,0:T(8,128)S(1)} %get-tuple-element.124.control_ref, f32[48,128]{1,0:T(8,128)S(1)} %get-tuple-element.143.weight_ref, f32[512,128]{1,0:T(8,128)S(1)} %get-tuple-element.171.pull_message, bf16[2,256,256]{2,1,0:T(8,128)(2,1)S(1)} %get-tuple-element.178.ghost_high, ...), custom_call_target="tpu_custom_call" | custom-call | tf_op jit(solution)/shard_map/pallas_call | solution.py:1035
  32.4 2.9 %collective-permute-done.8.far_in = f32[3,24,128]{2,1,0:T(8,128)S(1)} collective-permute-done((f32[3,24,128]{2,1,0:T(8,128)S(1)}, f32[3,24,128]{2,1,0:T(8,128)S(1)}, u32[]{:S(2)}, u32[]{:S(2)}) %collective-permute-start.8) | collective-permute-done | bytes 36896 | tf_op jit(solution)/shard_map/ppermute | solution.py:993
  35.3 0.0 collective-permute-done.9.mate_in
  35.4 1.1 %collective-permute-start.10 = (f32[3,24,128]{2,1,0:T(8,128)S(1)}, f32[3,24,128]{2,1,0:T(8,128)S(1)}, u32[]{:S(2)}, u32[]{:S(2)}) collective-permute-start(f32[3,24,128]{2,1,0:T(8,128)S(1)} %get-tuple-element.185), channel_id=1, source_target_pairs={{0,3},{1,2},{2,1},{3,0},{4,7},{5,6},{6,5},{7,4},{8,11},{9,10},{10,... | collective-permute-start | bytes 110600 | tf_op jit(solution)/shard_map/ppermute | solution.py:993
  36.5 0.0 collective-permute-start.11
  36.5 1.1 %shard_map.112.pull_hist_ref = f32[512,256]{1,0:T(8,128)S(1)} custom-call(s32[8,128]{1,0:T(8,128)S(1)} %get-tuple-element.124.control_ref, f32[512,128]{1,0:T(8,128)S(1)} %get-tuple-element.125.col_ref, f32[8,8,128]{2,1,0:T(8,128)S(1)} %get-tuple-element.126.row_ref, bf16[256,640]{1,0:T(8,128)(2,1)S(1)} %get-tuple-element.141.fold_high, ...), custom_call_target="tpu_custom_call" | custom-call | tf_op jit(solution)/shard_map/pallas_call | solution.py:1035
  37.6 3.6 %collective-permute-done.10.zfar_in = f32[3,24,128]{2,1,0:T(8,128)S(1)} collective-permute-done((f32[3,24,128]{2,1,0:T(8,128)S(1)}, f32[3,24,128]{2,1,0:T(8,128)S(1)}, u32[]{:S(2)}, u32[]{:S(2)}) %collective-permute-start.10) | collective-permute-done | bytes 36896 | tf_op jit(solution)/shard_map/ppermute | solution.py:993
  41.2 0.0 collective-permute-done.11.zmate_in
  41.2 1.8 %shard_map.113 = (f32[8,128]{1,0:T(8,128)S(1)}, f32[512,256]{1,0:T(8,128)S(1)}, f32[512,128]{1,0:T(8,128)S(1)}) custom-call(s32[8,128]{1,0:T(8,128)S(1)} %get-tuple-element.124.control_ref, bf16[512,128]{1,0:T(8,128)(2,1)S(1)} %get-tuple-element.169.chosen_ref, f32[512,256]{1,0:T(8,128)S(1)} %shard_map.112.pull_hist_ref, ...), custom_call_target="tpu_custom_call" | custom-call | tf_op jit(solution)/shard_map/pallas_call | solution.py:1035
  43.0 0.1 collective-permute-start.12
  43.1 0.1 collective-permute-start.13
  43.1 0.8 %shard_map.114 = (f32[6,512,256]{2,1,0:T(8,128)S(1)}, f32[1,512]{1,0:T(1,128)}) custom-call(s32[8,128]{1,0:T(8,128)S(1)} %get-tuple-element.124.control_ref, f32[48,128]{1,0:T(8,128)S(1)} %get-tuple-element.143.weight_ref, f32[512,128]{1,0:T(8,128)S(1)} %get-tuple-element.171.pull_message, f32[512,128]{1,0:T(8,128)S(1)} %get-tuple-element.197.share_ref, ...), custom_call_target="tpu_custom_call" | custom-call | tf_op jit(solution)/shard_map/pallas_call | solution.py:1035
  43.9 3.1 %collective-permute-done.12.far_in = f32[8,128]{1,0:T(8,128)S(1)} collective-permute-done((f32[8,128]{1,0:T(8,128)S(1)}, f32[8,128]{1,0:T(8,128)S(1)}, u32[]{:S(2)}, u32[]{:S(2)}) %collective-permute-start.12) | collective-permute-done | bytes 4128 | tf_op jit(solution)/shard_map/ppermute | solution.py:993
  47.0 0.0 collective-permute-done.13.mate_in
  47.0 1.7 %collective-permute-start.14 = (f32[3,8,128]{2,1,0:T(8,128)S(1)}, f32[3,8,128]{2,1,0:T(8,128)S(1)}, u32[]{:S(2)}, u32[]{:S(2)}) collective-permute-start(f32[3,8,128]{2,1,0:T(8,128)S(1)} %pad_maximum_fusion.5), channel_id=1, source_target_pairs={{0,3},{1,2},{2,1},{3,0},{4,7},{5,6},{6,5},{7,4},{8,11},{9,10},{10,... | collective-permute-start | bytes 36872 | tf_op jit(solution)/shard_map/ppermute | solution.py:993
  48.7 0.0 collective-permute-start.15
  48.7 0.2 shard_map.115
  48.9 3.6 %collective-permute-done.14.zfar_in = f32[3,8,128]{2,1,0:T(8,128)S(1)} collective-permute-done((f32[3,8,128]{2,1,0:T(8,128)S(1)}, f32[3,8,128]{2,1,0:T(8,128)S(1)}, u32[]{:S(2)}, u32[]{:S(2)}) %collective-permute-start.14) | collective-permute-done | bytes 12320 | tf_op jit(solution)/shard_map/ppermute | solution.py:993
  52.5 0.0 collective-permute-done.15.zmate_in
  52.5 0.9 %shard_map.116 = f32[3,512]{1,0:T(4,128)} custom-call(s32[8,128]{1,0:T(8,128)S(1)} %get-tuple-element.124.control_ref, bf16[128,512]{1,0:T(8,128)(2,1)S(1)} %get-tuple-element.204.turned_ref, f32[8,512]{1,0:T(8,128)S(1)} %get-tuple-element.205.own_ref, f32[8,128]{1,0:T(8,128)S(1)} %collective-permute-done.13.mate_in, ...), custom_call_target="tpu_custom_call" | custom-call | tf_op jit(solution)/shard_map/pallas_call | solution.py:1035
  (9 shorter events, 0.0 us)
Async XLA Ops:
  1.6 5.6 %collective-permute-start = (f32[8,128]{1,0:T(8,128)S(1)}, f32[8,128]{1,0:T(8,128)S(1)}, u32[]{:S(2)}, u32[]{:S(2)}) collective-permute-start(f32[8,128]{1,0:T(8,128)S(1)} %get-tuple-element.109), channel_id=1, source_target_pairs={{0,28},{4,8},{8,4},{12,16},{16,12},{20,24},{24,20},{28,0},{1,29},{... | collective-permute-start | bytes 12296 | tf_op jit(solution)/shard_map/ppermute | solution.py:993
  5.0 2.2 %collective-permute-start.1 = (f32[8,128]{1,0:T(8,128)S(1)}, f32[8,128]{1,0:T(8,128)S(1)}, u32[]{:S(2)}, u32[]{:S(2)}) collective-permute-start(f32[8,128]{1,0:T(8,128)S(1)} %get-tuple-element.109), channel_id=1, source_target_pairs={{0,4},{4,0},{8,12},{12,8},{16,20},{20,16},{24,28},{28,24},{1,5},{5... | collective-permute-start | bytes 12296 | tf_op jit(solution)/shard_map/ppermute | solution.py:994
  7.2 5.6 %collective-permute-start.2 = (f32[3,8,128]{2,1,0:T(8,128)S(1)}, f32[3,8,128]{2,1,0:T(8,128)S(1)}, u32[]{:S(2)}, u32[]{:S(2)}) collective-permute-start(f32[3,8,128]{2,1,0:T(8,128)S(1)} %pad_maximum_fusion.4), channel_id=1, source_target_pairs={{0,3},{1,2},{2,1},{3,0},{4,7},{5,6},{6,5},{7,4},{8,11},{9,10},{10,... | collective-permute-start | bytes 36872 | tf_op jit(solution)/shard_map/ppermute | solution.py:993
  10.9 3.7 %collective-permute-start.3 = (f32[3,8,128]{2,1,0:T(8,128)S(1)}, f32[3,8,128]{2,1,0:T(8,128)S(1)}, u32[]{:S(2)}, u32[]{:S(2)}) collective-permute-start(f32[3,8,128]{2,1,0:T(8,128)S(1)} %pad_maximum_fusion.4), channel_id=1, source_target_pairs={{0,1},{1,0},{2,3},{3,2},{4,5},{5,4},{6,7},{7,6},{8,9},{9,8},{10,11... | collective-permute-start | bytes 36872 | tf_op jit(solution)/shard_map/ppermute | solution.py:994
  16.6 4.3 %collective-permute-start.4 = (f32[3,24,128]{2,1,0:T(8,128)S(1)}, f32[3,24,128]{2,1,0:T(8,128)S(1)}, u32[]{:S(2)}, u32[]{:S(2)}) collective-permute-start(f32[3,24,128]{2,1,0:T(8,128)S(1)} %get-tuple-element.136), channel_id=1, source_target_pairs={{0,28},{4,8},{8,4},{12,16},{16,12},{20,24},{24,20},{28,0},{1,29},{... | collective-permute-start | bytes 110600 | tf_op jit(solution)/shard_map/ppermute | solution.py:993
  16.7 4.3 %collective-permute-start.5 = (f32[3,24,128]{2,1,0:T(8,128)S(1)}, f32[3,24,128]{2,1,0:T(8,128)S(1)}, u32[]{:S(2)}, u32[]{:S(2)}) collective-permute-start(f32[3,24,128]{2,1,0:T(8,128)S(1)} %get-tuple-element.137), channel_id=1, source_target_pairs={{0,4},{4,0},{8,12},{12,8},{16,20},{20,16},{24,28},{28,24},{1,5},{5... | collective-permute-start | bytes 110600 | tf_op jit(solution)/shard_map/ppermute | solution.py:994
  21.0 5.8 %collective-permute-start.6 = (f32[3,24,128]{2,1,0:T(8,128)S(1)}, f32[3,24,128]{2,1,0:T(8,128)S(1)}, u32[]{:S(2)}, u32[]{:S(2)}) collective-permute-start(f32[3,24,128]{2,1,0:T(8,128)S(1)} %get-tuple-element.151), channel_id=1, source_target_pairs={{0,3},{1,2},{2,1},{3,0},{4,7},{5,6},{6,5},{7,4},{8,11},{9,10},{10,... | collective-permute-start | bytes 110600 | tf_op jit(solution)/shard_map/ppermute | solution.py:993
  22.2 4.6 %collective-permute-start.7 = (f32[3,24,128]{2,1,0:T(8,128)S(1)}, f32[3,24,128]{2,1,0:T(8,128)S(1)}, u32[]{:S(2)}, u32[]{:S(2)}) collective-permute-start(f32[3,24,128]{2,1,0:T(8,128)S(1)} %get-tuple-element.152), channel_id=1, source_target_pairs={{0,1},{1,0},{2,3},{3,2},{4,5},{5,4},{6,7},{7,6},{8,9},{9,8},{10,11... | collective-permute-start | bytes 110600 | tf_op jit(solution)/shard_map/ppermute | solution.py:994
  31.0 4.3 %collective-permute-start.8 = (f32[3,24,128]{2,1,0:T(8,128)S(1)}, f32[3,24,128]{2,1,0:T(8,128)S(1)}, u32[]{:S(2)}, u32[]{:S(2)}) collective-permute-start(f32[3,24,128]{2,1,0:T(8,128)S(1)} %get-tuple-element.174), channel_id=1, source_target_pairs={{0,28},{4,8},{8,4},{12,16},{16,12},{20,24},{24,20},{28,0},{1,29},{... | collective-permute-start | bytes 110600 | tf_op jit(solution)/shard_map/ppermute | solution.py:993
  31.1 4.3 %collective-permute-start.9 = (f32[3,24,128]{2,1,0:T(8,128)S(1)}, f32[3,24,128]{2,1,0:T(8,128)S(1)}, u32[]{:S(2)}, u32[]{:S(2)}) collective-permute-start(f32[3,24,128]{2,1,0:T(8,128)S(1)} %get-tuple-element.175), channel_id=1, source_target_pairs={{0,4},{4,0},{8,12},{12,8},{16,20},{20,16},{24,28},{28,24},{1,5},{5... | collective-permute-start | bytes 110600 | tf_op jit(solution)/shard_map/ppermute | solution.py:994
  35.4 5.8 %collective-permute-start.10 = (f32[3,24,128]{2,1,0:T(8,128)S(1)}, f32[3,24,128]{2,1,0:T(8,128)S(1)}, u32[]{:S(2)}, u32[]{:S(2)}) collective-permute-start(f32[3,24,128]{2,1,0:T(8,128)S(1)} %get-tuple-element.185), channel_id=1, source_target_pairs={{0,3},{1,2},{2,1},{3,0},{4,7},{5,6},{6,5},{7,4},{8,11},{9,10},{10,... | collective-permute-start | bytes 110600 | tf_op jit(solution)/shard_map/ppermute | solution.py:993
  36.5 4.7 %collective-permute-start.11 = (f32[3,24,128]{2,1,0:T(8,128)S(1)}, f32[3,24,128]{2,1,0:T(8,128)S(1)}, u32[]{:S(2)}, u32[]{:S(2)}) collective-permute-start(f32[3,24,128]{2,1,0:T(8,128)S(1)} %get-tuple-element.186), channel_id=1, source_target_pairs={{0,1},{1,0},{2,3},{3,2},{4,5},{5,4},{6,7},{7,6},{8,9},{9,8},{10,11... | collective-permute-start | bytes 110600 | tf_op jit(solution)/shard_map/ppermute | solution.py:994
  43.0 4.0 %collective-permute-start.12 = (f32[8,128]{1,0:T(8,128)S(1)}, f32[8,128]{1,0:T(8,128)S(1)}, u32[]{:S(2)}, u32[]{:S(2)}) collective-permute-start(f32[8,128]{1,0:T(8,128)S(1)} %get-tuple-element.194), channel_id=1, source_target_pairs={{0,28},{4,8},{8,4},{12,16},{16,12},{20,24},{24,20},{28,0},{1,29},{... | collective-permute-start | bytes 12296 | tf_op jit(solution)/shard_map/ppermute | solution.py:993
  43.1 3.9 %collective-permute-start.13 = (f32[8,128]{1,0:T(8,128)S(1)}, f32[8,128]{1,0:T(8,128)S(1)}, u32[]{:S(2)}, u32[]{:S(2)}) collective-permute-start(f32[8,128]{1,0:T(8,128)S(1)} %get-tuple-element.194), channel_id=1, source_target_pairs={{0,4},{4,0},{8,12},{12,8},{16,20},{20,16},{24,28},{28,24},{1,5},{5... | collective-permute-start | bytes 12296 | tf_op jit(solution)/shard_map/ppermute | solution.py:994
  47.0 5.5 %collective-permute-start.14 = (f32[3,8,128]{2,1,0:T(8,128)S(1)}, f32[3,8,128]{2,1,0:T(8,128)S(1)}, u32[]{:S(2)}, u32[]{:S(2)}) collective-permute-start(f32[3,8,128]{2,1,0:T(8,128)S(1)} %pad_maximum_fusion.5), channel_id=1, source_target_pairs={{0,3},{1,2},{2,1},{3,0},{4,7},{5,6},{6,5},{7,4},{8,11},{9,10},{10,... | collective-permute-start | bytes 36872 | tf_op jit(solution)/shard_map/ppermute | solution.py:993
  48.7 3.8 %collective-permute-start.15 = (f32[3,8,128]{2,1,0:T(8,128)S(1)}, f32[3,8,128]{2,1,0:T(8,128)S(1)}, u32[]{:S(2)}, u32[]{:S(2)}) collective-permute-start(f32[3,8,128]{2,1,0:T(8,128)S(1)} %pad_maximum_fusion.5), channel_id=1, source_target_pairs={{0,1},{1,0},{2,3},{3,2},{4,5},{5,4},{6,7},{7,6},{8,9},{9,8},{10,11... | collective-permute-start | bytes 36872 | tf_op jit(solution)/shard_map/ppermute | solution.py:994

commit v4 on v3

--- a/solution.py
+++ b/solution.py
@@ -313,23 +313,34 @@
     return tuple(control_ref[place, first + k] for k in range(3))
 
 
-def listed_tiles(control_ref, which, work, start=0):
-    count = control_ref[3 + which, 2] - start
-
-    def step(half, carried):
-        place = start + 2 * half
-        work([listed_tile(control_ref, which, place + k) for k in range(2)])
+def single_tiles(control_ref, which, work, start):
+    def step(place, carried):
+        work([listed_tile(control_ref, which, place)])
         return carried
 
-    lax.fori_loop(0, count // 2, step, 0)
-
-    @pl.when(count % 2 == 1)
+    lax.fori_loop(start, control_ref[3 + which, 2], step, 0)
+
+
+def own_tiles(control_ref, work):
+    count = control_ref[4, 2]
+
+    def group(place, size):
+        work([listed_tile(control_ref, 1, place + k) for k in range(size)])
+
+    def step(quarter, carried):
+        group(4 * quarter, 4)
+        return carried
+
+    lax.fori_loop(0, count // 4, step, 0)
+    rest = count % 4
+
+    @pl.when(rest >= 2)
     def _():
-        work([listed_tile(control_ref, which, start + count - 1)])
-
-
-def own_tiles(control_ref, work):
-    listed_tiles(control_ref, 1, work)
+        group(count - rest, 2)
+
+    @pl.when(rest % 2 == 1)
+    def _():
+        group(count - 1, 1)
 
 
 def ghost_tiles(control_ref, work):
@@ -351,7 +362,7 @@
         @pl.when(more > 1)
         def _():
             work(fixed() + [listed_tile(control_ref, 0, place) for place in range(2)])
-            listed_tiles(control_ref, 0, work, 2)
+            single_tiles(control_ref, 0, work, 2)
 
 
 def exact_pick(rows, chosen):
@@ -482,12 +493,7 @@
     col_ref,
     row_ref,
     chosen_ref,
-    fold_high,
-    fold_low,
-    mix_high,
-    mix_low,
     weight_ref,
-    fold_ref,
     mixing_ref,
     sems,
 ):
@@ -512,29 +518,8 @@
     chosen_ref[...] = chooser(send_ref[...], atoms).astype(F32).astype(BF16)
     for copy in copies:
         copy.wait()
-
     radial = weight_ref[SPAN : SPAN + paths, :]
     weight_ref[SPAN : SPAN + paths, :] = radial * basis_scale(radial.shape)
-
-    embed = jnp.where(iota((SPAN, 128), 0) < kinds, weight_ref[0:SPAN, :], 0.0)
-    scalar = jnp.concatenate([radial_row(weight_ref, 0, n) * embed for n in range(BASIS)], axis=0)
-    vector = jnp.concatenate([radial_row(weight_ref, 1, n) * embed for n in range(BASIS)], axis=0)
-    scalar, vector = split(scalar), split(vector)
-    to_self = mm3(scalar, split(mixing_ref[0]))
-    to_gate = mm3(scalar, split(mixing_ref[2]))
-    to_vector = mm3(vector, split(mixing_ref[1]))
-    fold_ref[...] = jnp.zeros_like(fold_ref)
-    for n in range(BASIS):
-        rows = slice(n * SPAN, n * SPAN + SPAN)
-        base = n * 4 * SPAN
-        fold_ref[base : base + SPAN, 0:128] = to_self[rows]
-        fold_ref[base : base + SPAN, 128:256] = to_gate[rows]
-        for a in range(3):
-            here = base + (a + 1) * SPAN
-            fold_ref[here : here + SPAN, (a + 2) * 128 : (a + 3) * 128] = to_vector[rows]
-    fold_high[...], fold_low[...] = split(fold_ref[...])
-    for part in range(2):
-        mix_high[part], mix_low[part] = split(mixing_ref[3 + part])
 
 
 def first_kernel(
@@ -635,14 +620,37 @@
     kinds,
     hist_ref,
     col_ref,
-    fold_high,
-    fold_low,
     weight_ref,
+    mixing_ref,
     pre_ref,
     feat_high,
     feat_low,
     scalar_ref,
+    fold_high,
+    fold_low,
+    mix_high,
+    mix_low,
+    fold_ref,
 ):
+    embed = jnp.where(iota((SPAN, 128), 0) < kinds, weight_ref[0:SPAN, :], 0.0)
+    scalar = jnp.concatenate([radial_row(weight_ref, 0, n) * embed for n in range(BASIS)], axis=0)
+    vector = jnp.concatenate([radial_row(weight_ref, 1, n) * embed for n in range(BASIS)], axis=0)
+    scalar, vector = split(scalar), split(vector)
+    to_self = mm3(scalar, split(mixing_ref[0]))
+    to_gate = mm3(scalar, split(mixing_ref[2]))
+    to_vector = mm3(vector, split(mixing_ref[1]))
+    fold_ref[...] = jnp.zeros_like(fold_ref)
+    for n in range(BASIS):
+        rows = slice(n * SPAN, n * SPAN + SPAN)
+        base = n * 4 * SPAN
+        fold_ref[base : base + SPAN, 0:128] = to_self[rows]
+        fold_ref[base : base + SPAN, 128:256] = to_gate[rows]
+        for a in range(3):
+            here = base + (a + 1) * SPAN
+            fold_ref[here : here + SPAN, (a + 2) * 128 : (a + 3) * 128] = to_vector[rows]
+    fold_high[...], fold_low[...] = split(fold_ref[...])
+    for part in range(2):
+        mix_high[part], mix_low[part] = split(mixing_ref[3 + part])
     blocks = hist_ref.shape[0] // BLOCK
     pre_ref[...] = mm3(split(hist_ref[...]), (fold_high[...], fold_low[...]))
 
@@ -682,7 +690,9 @@
                 ghost_col, right, row_ref, left, False, swap_high.at[slot], swap_low.at[slot]
             )
 
-    ghost_tiles(control_ref, swapped)
+    for slot in range(2):
+        swapped([(slot, control_ref[slot, 0], slot)])
+    single_tiles(control_ref, 0, swapped, 0)
 
 
 def weighted_pull(cotangent, weight_ref, path):
@@ -988,28 +998,34 @@
     return [(i, i ^ 1) for i in range(count)]
 
 
-def swap_both(axis, to_mate, to_far):
-    to_far, to_mate = lax.optimization_barrier((to_far, to_mate))
-    far = lax.ppermute(to_far, axis, partners(axis, True))
-    mate = lax.ppermute(to_mate, axis, partners(axis, False))
-    far, mate = lax.optimization_barrier((far, mate))
+def swap_both(axis, to_mate, to_far, far_first):
+    def swap(value, far):
+        return lax.ppermute(value, axis, partners(axis, far))
+
+    if far_first:
+        to_far, to_mate = lax.optimization_barrier((to_far, to_mate))
+        far, mate = lax.optimization_barrier((swap(to_far, True), swap(to_mate, False)))
+    else:
+        to_mate, to_far = lax.optimization_barrier((to_mate, to_far))
+        mate, far = lax.optimization_barrier((swap(to_mate, False), swap(to_far, True)))
     return mate, far
 
 
 def exchange_rows(rows, beside):
-    mate, far = swap_both("gx", rows, rows)
+    mate, far = swap_both("gx", rows, rows, True)
     far, mate, beside = lax.optimization_barrier((far, mate, beside))
     column = jnp.stack([rows, mate, far])
-    zmate, zfar = swap_both("gy", column, column)
+    zmate, zfar = swap_both("gy", column, column, False)
     return (mate, far, zmate, zfar), beside
 
 
 def exchange_packets(even_y, to_mate, to_far, side, beside):
-    mate, far = swap_both("gx", to_mate, to_far)
+    mate, far = swap_both("gx", to_mate, to_far, True)
     far, mate, beside = lax.optimization_barrier((far, mate, beside))
     up = jnp.concatenate([mate[2:3], far[2:3], side[1:2]], axis=0)
     down = jnp.concatenate([mate[0:1], far[0:1], side[0:1]], axis=0)
-    zmate, zfar = swap_both("gy", jnp.where(even_y, up, down), jnp.where(even_y, down, up))
+    to_mate, to_far = jnp.where(even_y, up, down), jnp.where(even_y, down, up)
+    zmate, zfar = swap_both("gy", to_mate, to_far, False)
     return (mate, far, zmate, zfar), beside
 
 
@@ -1088,18 +1104,11 @@
             struct(8, 128, dtype=jnp.int32), col_struct, own_rows,
             struct(atoms, 128, dtype=BF16),
         ]
-        + fold_halves
-        + mix_halves
-        + [struct(2 * SPAN + 4 * BASIS, 128)],
-        [
-            pltpu.VMEM((HIST, 640), F32),
-            pltpu.VMEM(mixing.shape, F32),
-            pltpu.SemaphoreType.DMA((4,)),
-        ],
+        + [struct(2 * SPAN + 4 * BASIS, 128), struct(*mixing.shape)],
+        [pltpu.SemaphoreType.DMA((4,))],
     )(words, tiles, site, send, *far_arrays[4:])
     arrived, prepared = exchange_rows(rows, prepared)
-    control, col, row, chosen, fold_high, fold_low, mix_high, mix_low, weights = prepared
-    fold, mix = (fold_high, fold_low), (mix_high, mix_low)
+    control, col, row, chosen, weights, mixers = prepared
     hist, own_high, own_low = call(
         own_histogram_kernel, [VMEM] * 3, [hist_struct] + pairs
     )(control, col, row)
@@ -1115,11 +1124,13 @@
     )(control, send, hist, col, *arrived)
     features = call(
         functools.partial(feature_kernel, kinds),
-        [VMEM] * 5,
-        [struct(atoms, 640)] + own_halves + [col_struct],
-    )(hist, col, *fold, weights)
+        [VMEM] * 4,
+        [struct(atoms, 640)] + own_halves + [col_struct] + fold_halves + mix_halves,
+        [pltpu.VMEM((HIST, 640), F32)],
+    )(hist, col, weights, mixers)
     arrived, features = exchange_packets(even_y, to_mate, to_far, side, features)
-    pre, feat_high, feat_low, scalar = features
+    pre, feat_high, feat_low, scalar, *folded = features
+    fold, mix = folded[0:2], folded[2:4]
     message, swap_high, swap_low = call(message_kernel, [VMEM] * 8, [col_struct] + swaps)(
         control, row, ghost_col, weights, feat_high, feat_low, own_high, own_low
     )
@@ -1146,7 +1157,7 @@
         own_pull_kernel,
         [VMEM] * 9,
         hist_struct,
-        [pltpu.VMEM((atoms, 512), F32)] + [pltpu.VMEM((2, 256, BASIS * BLOCK), BF16)] * 2,
+        [pltpu.VMEM((atoms, 512), F32)] + [pltpu.VMEM((4, 256, BASIS * BLOCK), BF16)] * 2,
     )(control, col, row, *fold, weights, pre, pull_message, direct)
     rows, total, grad_col = call(
         third_ghost_kernel,
@@ -1167,7 +1178,7 @@
         [
             pltpu.VMEM((blocks, 8, 128), F32),
             pltpu.VMEM((atoms, 128), F32),
-            pltpu.VMEM((2, BASIS * BLOCK, 256), F32),
+            pltpu.VMEM((4, BASIS * BLOCK, 256), F32),
         ],
     )(control, chosen, total, col, row, pull, grad_col)
     forces = call(last_kernel, [VMEM] * 7, struct(3, atoms))(control, turned, own, *arrived)

time: 53.1 us -> 51.7 us (0.974); the launches traced: 53.4 us -> 51.3 us
  starting transfers between devices: 12 us -> 19.4 us
  waiting for transfers between devices: 22.3 us -> 15.7 us
  Pallas kernels: 17.5 us -> 14.5 us
    ppermute x16, starting transfers between devices: 12 us -> 19.4 us  [swap(): return lax.ppermute(value, axis, partners(axis, far))]
    ppermute x16, waiting for transfers between devices: 22.3 us -> 15.7 us  [swap(): return lax.ppermute(value, axis, partners(axis, far))]
    pallas_call x13, Pallas kernels: 17.5 us -> 14.5 us  [run(): return made(*placed)]
  transfers between devices with their start and end apart: 16 -> 16, of which waited for: 8 -> 10; matrix products, arithmetic and copies ran while one was open for 0% -> 0% of each run, Pallas kernels for 14% -> 13%
where the time goes in v4:
time: 51.7 us; the launch traced here: 51.3 us
  starting transfers between devices  19.4 us (38%)
  waiting for transfers between devices  15.7 us (30%)
  Pallas kernels  14.5 us (28%)
  between operations  1.46 us (3%)
    ppermute x16, starting transfers between devices, swap(): return lax.ppermute(value, axis, partners(axis, far))  19.4 us
    ppermute x16, waiting for transfers between devices, swap(): return lax.ppermute(value, axis, partners(axis, far))  15.7 us
    pallas_call x13, Pallas kernels, run(): return made(*placed)  14.5 us
  transfers between devices with their start and end apart: 16, of which 10 were waited for; matrix products, arithmetic and copies ran while one was open for 0% of the time, Pallas kernels for 13%

profile of v4, /device:TPU:0, one launch (start us, length us, event | category | flops | bytes accessed | tf_op | source)
XLA Modules:
  0.0 51.3 jit_solution(10798260084577141910)
XLA Ops:
  0.6 1.0 %shard_map.104 = (f32[8,512]{1,0:T(8,128)S(1)}, f32[8,128]{1,0:T(8,128)S(1)}, s32[8,16]{1,0:T(8,128)S(1)}, s32[8,128]{1,0:T(8,128)S(1)}) custom-call(f32[3,512]{1,0:T(4,128)} %frac_in.1, s32[1,512]{1,0:T(1,128)} %bitcast.21, s32[8,16]{1,0:T(8,128)} %send_in.1, s32[2,6]{1,0:T(2,128)} %tile_in.1), custom_call_target="tpu_custom_call" | custom-call | tf_op jit(solution)/shard_map/pallas_call | solution.py:1051
  1.6 3.4 %collective-permute-start = (f32[8,128]{1,0:T(8,128)S(1)}, f32[8,128]{1,0:T(8,128)S(1)}, u32[]{:S(2)}, u32[]{:S(2)}) collective-permute-start(f32[8,128]{1,0:T(8,128)S(1)} %get-tuple-element.111), channel_id=1, source_target_pairs={{0,28},{4,8},{8,4},{12,16},{16,12},{20,24},{24,20},{28,0},{1,29},{... | collective-permute-start | bytes 12296 | tf_op jit(solution)/shard_map/ppermute | solution.py:1003
  5.0 0.0 collective-permute-start.1
  5.7 0.1 add_bitcast_fusion.words_ref
  5.8 1.2 %shard_map.105 = (s32[8,128]{1,0:T(8,128)S(1)}, f32[512,128]{1,0:T(8,128)S(1)}, f32[8,8,128]{2,1,0:T(8,128)S(1)}, bf16[512,128]{1,0:T(8,128)(2,1)S(1)}, f32[48,1...) custom-call(s32[1,3]{1,0:T(1,128)S(1)} %add_bitcast_fusion.words_ref, s32[8,128]{1,0:T(8,128)S(1)} %get-tuple-element.114.tiles_ref, ...), custom_call_target="tpu_custom_call" | custom-call | tf_op jit(solution)/shard_map/pallas_call | solution.py:1051
  7.0 0.0 collective-permute-done.far_in
  7.0 0.0 collective-permute-done.1.mate_in
  7.0 1.7 %collective-permute-start.2 = (f32[3,8,128]{2,1,0:T(8,128)S(1)}, f32[3,8,128]{2,1,0:T(8,128)S(1)}, u32[]{:S(2)}, u32[]{:S(2)}) collective-permute-start(f32[3,8,128]{2,1,0:T(8,128)S(1)} %pad_maximum_fusion.4), channel_id=1, source_target_pairs={{0,1},{1,0},{2,3},{3,2},{4,5},{5,4},{6,7},{7,6},{8,9},{9,8},{10,11... | collective-permute-start | bytes 36872 | tf_op jit(solution)/shard_map/ppermute | solution.py:1003
  8.7 2.5 %collective-permute-start.3 = (f32[3,8,128]{2,1,0:T(8,128)S(1)}, f32[3,8,128]{2,1,0:T(8,128)S(1)}, u32[]{:S(2)}, u32[]{:S(2)}) collective-permute-start(f32[3,8,128]{2,1,0:T(8,128)S(1)} %pad_maximum_fusion.4), channel_id=1, source_target_pairs={{0,3},{1,2},{2,1},{3,0},{4,7},{5,6},{6,5},{7,4},{8,11},{9,10},{10,... | collective-permute-start | bytes 36872 | tf_op jit(solution)/shard_map/ppermute | solution.py:1003
  11.2 0.1 shard_map.106
  11.3 0.0 collective-permute-done.2.zmate_in
  11.3 2.9 %collective-permute-done.3.zfar_in = f32[3,8,128]{2,1,0:T(8,128)S(1)} collective-permute-done((f32[3,8,128]{2,1,0:T(8,128)S(1)}, f32[3,8,128]{2,1,0:T(8,128)S(1)}, u32[]{:S(2)}, u32[]{:S(2)}) %collective-permute-start.3) | collective-permute-done | bytes 12320 | tf_op jit(solution)/shard_map/ppermute | solution.py:1003
  14.2 1.3 %shard_map.107 = (f32[512,256]{1,0:T(8,128)S(1)}, f32[3,24,128]{2,1,0:T(8,128)S(1)}, f32[3,24,128]{2,1,0:T(8,128)S(1)}, f32[2,24,128]{2,1,0:T(8,128)S(1)}, f32[1...) custom-call(s32[8,128]{1,0:T(8,128)S(1)} %get-tuple-element.123.cont, ...), custom_call_target="tpu_custom_call" | custom-call | tf_op jit(solution)/shard_map/pallas_call | solution.py:1051
  15.5 0.5 collective-permute-start.4
  16.0 0.9 %collective-permute-start.5 = (f32[3,24,128]{2,1,0:T(8,128)S(1)}, f32[3,24,128]{2,1,0:T(8,128)S(1)}, u32[]{:S(2)}, u32[]{:S(2)}) collective-permute-start(f32[3,24,128]{2,1,0:T(8,128)S(1)} %get-tuple-element.136), channel_id=1, source_target_pairs={{0,4},{4,0},{8,12},{12,8},{16,20},{20,16},{24,28},{28,24},{1,5},{5... | collective-permute-start | bytes 110600 | tf_op jit(solution)/shard_map/ppermute | solution.py:1003
  16.9 2.0 %shard_map.108 = (f32[512,640]{1,0:T(8,128)S(1)}, bf16[8,256,256]{2,1,0:T(8,128)(2,1)S(1)}, bf16[8,256,256]{2,1,0:T(8,128)(2,1)S(1)}, f32[512,128]{1,0:T(8,128)S...) custom-call(f32[512,256]{1,0:T(8,128)S(1)} %get-tuple-element.139.hi, ...), custom_call_target="tpu_custom_call" | custom-call | tf_op jit(solution)/shard_map/pallas_call | solution.py:1051
  18.9 0.9 %collective-permute-done.4.far_in = f32[3,24,128]{2,1,0:T(8,128)S(1)} collective-permute-done((f32[3,24,128]{2,1,0:T(8,128)S(1)}, f32[3,24,128]{2,1,0:T(8,128)S(1)}, u32[]{:S(2)}, u32[]{:S(2)}) %collective-permute-start.4) | collective-permute-done | bytes 36896 | tf_op jit(solution)/shard_map/ppermute | solution.py:1003
  19.9 0.0 collective-permute-done.5.mate_in
  19.9 0.1 collective-permute-start.6
  20.0 2.5 %collective-permute-start.7 = (f32[3,24,128]{2,1,0:T(8,128)S(1)}, f32[3,24,128]{2,1,0:T(8,128)S(1)}, u32[]{:S(2)}, u32[]{:S(2)}) collective-permute-start(f32[3,24,128]{2,1,0:T(8,128)S(1)} %get-tuple-element.154), channel_id=1, source_target_pairs={{0,3},{1,2},{2,1},{3,0},{4,7},{5,6},{6,5},{7,4},{8,11},{9,10},{10,... | collective-permute-start | bytes 110600 | tf_op jit(solution)/shard_map/ppermute | solution.py:1003
  22.5 0.5 %shard_map.109 = (f32[512,128]{1,0:T(8,128)S(1)}, bf16[6,256,512]{2,1,0:T(8,128)(2,1)S(1)}, bf16[6,256,512]{2,1,0:T(8,128)(2,1)S(1)}) custom-call(s32[8,128]{1,0:T(8,128)S(1)} %get-tuple-element.123.control_ref, f32[8,8,128]{2,1,0:T(8,128)S(1)} %get-tuple-element.125.row_ref, f32[128,128]{1,0:T(8,128)S(1)} %get-tuple-element.157.ghost_col, ...), custom_call_target="tpu_custom_call" | custom-call | tf_op jit(solution)/shard_map/pallas_call | solution.py:1051
  23.0 1.3 %collective-permute-done.6.zmate_in = f32[3,24,128]{2,1,0:T(8,128)S(1)} collective-permute-done((f32[3,24,128]{2,1,0:T(8,128)S(1)}, f32[3,24,128]{2,1,0:T(8,128)S(1)}, u32[]{:S(2)}, u32[]{:S(2)}) %collective-permute-start.6) | collective-permute-done | bytes 36896 | tf_op jit(solution)/shard_map/ppermute | solution.py:1003
  24.3 1.5 %collective-permute-done.7.zfar_in = f32[3,24,128]{2,1,0:T(8,128)S(1)} collective-permute-done((f32[3,24,128]{2,1,0:T(8,128)S(1)}, f32[3,24,128]{2,1,0:T(8,128)S(1)}, u32[]{:S(2)}, u32[]{:S(2)}) %collective-permute-start.7) | collective-permute-done | bytes 36896 | tf_op jit(solution)/shard_map/ppermute | solution.py:1003
  25.8 3.2 %shard_map.110 = (f32[3,24,128]{2,1,0:T(8,128)S(1)}, f32[3,24,128]{2,1,0:T(8,128)S(1)}, f32[2,24,128]{2,1,0:T(8,128)S(1)}, bf16[2,256,256]{2,1,0:T(8,128)(2,1)S(...) custom-call(s32[8,128]{1,0:T(8,128)S(1)} %get-tuple-element.123.cont, ...), custom_call_target="tpu_custom_call" | custom-call | tf_op jit(solution)/shard_map/pallas_call | solution.py:1051
  29.0 0.1 collective-permute-start.8
  29.1 1.3 %collective-permute-start.9 = (f32[3,24,128]{2,1,0:T(8,128)S(1)}, f32[3,24,128]{2,1,0:T(8,128)S(1)}, u32[]{:S(2)}, u32[]{:S(2)}) collective-permute-start(f32[3,24,128]{2,1,0:T(8,128)S(1)} %get-tuple-element.179), channel_id=1, source_target_pairs={{0,4},{4,0},{8,12},{12,8},{16,20},{20,16},{24,28},{28,24},{1,5},{5... | collective-permute-start | bytes 110600 | tf_op jit(solution)/shard_map/ppermute | solution.py:1003
  30.4 0.7 %shard_map.111.pull_in = f32[6,512,256]{2,1,0:T(8,128)S(1)} custom-call(s32[8,128]{1,0:T(8,128)S(1)} %get-tuple-element.123.control_ref, f32[48,128]{1,0:T(8,128)S(1)} %get-tuple-element.140.weight_ref, f32[512,128]{1,0:T(8,128)S(1)} %get-tuple-element.175.pull_message, bf16[2,256,256]{2,1,0:T(8,128)(2,1)S(1)} %get-tuple-element.182.ghost_high, ...), custom_call_target="tpu_custom_call" | custom-call | tf_op jit(solution)/shard_map/pallas_call | solution.py:1051
  31.2 2.2 %collective-permute-done.8.far_in = f32[3,24,128]{2,1,0:T(8,128)S(1)} collective-permute-done((f32[3,24,128]{2,1,0:T(8,128)S(1)}, f32[3,24,128]{2,1,0:T(8,128)S(1)}, u32[]{:S(2)}, u32[]{:S(2)}) %collective-permute-start.8) | collective-permute-done | bytes 36896 | tf_op jit(solution)/shard_map/ppermute | solution.py:1003
  33.3 0.0 collective-permute-done.9.mate_in
  33.4 0.2 collective-permute-start.10
  33.6 2.6 %collective-permute-start.11 = (f32[3,24,128]{2,1,0:T(8,128)S(1)}, f32[3,24,128]{2,1,0:T(8,128)S(1)}, u32[]{:S(2)}, u32[]{:S(2)}) collective-permute-start(f32[3,24,128]{2,1,0:T(8,128)S(1)} %get-tuple-element.190), channel_id=1, source_target_pairs={{0,3},{1,2},{2,1},{3,0},{4,7},{5,6},{6,5},{7,4},{8,11},{9,10},{10,... | collective-permute-start | bytes 110600 | tf_op jit(solution)/shard_map/ppermute | solution.py:1003
  36.2 1.1 %shard_map.112.pull_hist_ref = f32[512,256]{1,0:T(8,128)S(1)} custom-call(s32[8,128]{1,0:T(8,128)S(1)} %get-tuple-element.123.control_ref, f32[512,128]{1,0:T(8,128)S(1)} %get-tuple-element.124.col_ref, f32[8,8,128]{2,1,0:T(8,128)S(1)} %get-tuple-element.125.row_ref, bf16[256,640]{1,0:T(8,128)(2,1)S(1)} %get-tuple-element.158.fold_high, ...), custom_call_target="tpu_custom_call" | custom-call | tf_op jit(solution)/shard_map/pallas_call | solution.py:1051
  37.3 0.1 collective-permute-done.10.zmate_in
  37.4 1.9 %collective-permute-done.11.zfar_in = f32[3,24,128]{2,1,0:T(8,128)S(1)} collective-permute-done((f32[3,24,128]{2,1,0:T(8,128)S(1)}, f32[3,24,128]{2,1,0:T(8,128)S(1)}, u32[]{:S(2)}, u32[]{:S(2)}) %collective-permute-start.11) | collective-permute-done | bytes 36896 | tf_op jit(solution)/shard_map/ppermute | solution.py:1003
  39.3 1.4 %shard_map.113 = (f32[8,128]{1,0:T(8,128)S(1)}, f32[512,256]{1,0:T(8,128)S(1)}, f32[512,128]{1,0:T(8,128)S(1)}) custom-call(s32[8,128]{1,0:T(8,128)S(1)} %get-tuple-element.123.control_ref, bf16[512,128]{1,0:T(8,128)(2,1)S(1)} %get-tuple-element.173.chosen_ref, f32[512,256]{1,0:T(8,128)S(1)} %shard_map.112.pull_hist_ref, ...), custom_call_target="tpu_custom_call" | custom-call | tf_op jit(solution)/shard_map/pallas_call | solution.py:1051
  40.8 0.1 collective-permute-start.12
  40.9 0.9 %collective-permute-start.13 = (f32[8,128]{1,0:T(8,128)S(1)}, f32[8,128]{1,0:T(8,128)S(1)}, u32[]{:S(2)}, u32[]{:S(2)}) collective-permute-start(f32[8,128]{1,0:T(8,128)S(1)} %get-tuple-element.198), channel_id=1, source_target_pairs={{0,4},{4,0},{8,12},{12,8},{16,20},{20,16},{24,28},{28,24},{1,5},{5... | collective-permute-start | bytes 12296 | tf_op jit(solution)/shard_map/ppermute | solution.py:1003
  41.7 0.8 %shard_map.114 = (f32[6,512,256]{2,1,0:T(8,128)S(1)}, f32[1,512]{1,0:T(1,128)}) custom-call(s32[8,128]{1,0:T(8,128)S(1)} %get-tuple-element.123.control_ref, f32[48,128]{1,0:T(8,128)S(1)} %get-tuple-element.140.weight_ref, f32[512,128]{1,0:T(8,128)S(1)} %get-tuple-element.175.pull_message, f32[512,128]{1,0:T(8,128)S(1)} %get-tuple-element.201.share_ref, ...), custom_call_target="tpu_custom_call" | custom-call | tf_op jit(solution)/shard_map/pallas_call | solution.py:1051
  42.5 2.3 %collective-permute-done.12.far_in = f32[8,128]{1,0:T(8,128)S(1)} collective-permute-done((f32[8,128]{1,0:T(8,128)S(1)}, f32[8,128]{1,0:T(8,128)S(1)}, u32[]{:S(2)}, u32[]{:S(2)}) %collective-permute-start.12) | collective-permute-done | bytes 4128 | tf_op jit(solution)/shard_map/ppermute | solution.py:1003
  44.8 0.0 collective-permute-done.13.mate_in
  44.8 0.1 collective-permute-start.14
  44.9 2.6 %collective-permute-start.15 = (f32[3,8,128]{2,1,0:T(8,128)S(1)}, f32[3,8,128]{2,1,0:T(8,128)S(1)}, u32[]{:S(2)}, u32[]{:S(2)}) collective-permute-start(f32[3,8,128]{2,1,0:T(8,128)S(1)} %pad_maximum_fusion.5), channel_id=1, source_target_pairs={{0,3},{1,2},{2,1},{3,0},{4,7},{5,6},{6,5},{7,4},{8,11},{9,10},{10,... | collective-permute-start | bytes 36872 | tf_op jit(solution)/shard_map/ppermute | solution.py:1003
  47.5 0.2 shard_map.115
  47.7 0.7 %collective-permute-done.14.zmate_in = f32[3,8,128]{2,1,0:T(8,128)S(1)} collective-permute-done((f32[3,8,128]{2,1,0:T(8,128)S(1)}, f32[3,8,128]{2,1,0:T(8,128)S(1)}, u32[]{:S(2)}, u32[]{:S(2)}) %collective-permute-start.14) | collective-permute-done | bytes 12320 | tf_op jit(solution)/shard_map/ppermute | solution.py:1003
  48.5 1.9 %collective-permute-done.15.zfar_in = f32[3,8,128]{2,1,0:T(8,128)S(1)} collective-permute-done((f32[3,8,128]{2,1,0:T(8,128)S(1)}, f32[3,8,128]{2,1,0:T(8,128)S(1)}, u32[]{:S(2)}, u32[]{:S(2)}) %collective-permute-start.15) | collective-permute-done | bytes 12320 | tf_op jit(solution)/shard_map/ppermute | solution.py:1003
  50.4 0.9 %shard_map.116 = f32[3,512]{1,0:T(4,128)} custom-call(s32[8,128]{1,0:T(8,128)S(1)} %get-tuple-element.123.control_ref, bf16[128,512]{1,0:T(8,128)(2,1)S(1)} %get-tuple-element.208.turned_ref, f32[8,512]{1,0:T(8,128)S(1)} %get-tuple-element.209.own_ref, f32[8,128]{1,0:T(8,128)S(1)} %collective-permute-done.13.mate_in, ...), custom_call_target="tpu_custom_call" | custom-call | tf_op jit(solution)/shard_map/pallas_call | solution.py:1051
  (9 shorter events, 0.0 us)
Async XLA Ops:
  1.6 5.3 %collective-permute-start = (f32[8,128]{1,0:T(8,128)S(1)}, f32[8,128]{1,0:T(8,128)S(1)}, u32[]{:S(2)}, u32[]{:S(2)}) collective-permute-start(f32[8,128]{1,0:T(8,128)S(1)} %get-tuple-element.111), channel_id=1, source_target_pairs={{0,28},{4,8},{8,4},{12,16},{16,12},{20,24},{24,20},{28,0},{1,29},{... | collective-permute-start | bytes 12296 | tf_op jit(solution)/shard_map/ppermute | solution.py:1003
  5.0 2.0 %collective-permute-start.1 = (f32[8,128]{1,0:T(8,128)S(1)}, f32[8,128]{1,0:T(8,128)S(1)}, u32[]{:S(2)}, u32[]{:S(2)}) collective-permute-start(f32[8,128]{1,0:T(8,128)S(1)} %get-tuple-element.111), channel_id=1, source_target_pairs={{0,4},{4,0},{8,12},{12,8},{16,20},{20,16},{24,28},{28,24},{1,5},{5... | collective-permute-start | bytes 12296 | tf_op jit(solution)/shard_map/ppermute | solution.py:1003
  7.0 4.3 %collective-permute-start.2 = (f32[3,8,128]{2,1,0:T(8,128)S(1)}, f32[3,8,128]{2,1,0:T(8,128)S(1)}, u32[]{:S(2)}, u32[]{:S(2)}) collective-permute-start(f32[3,8,128]{2,1,0:T(8,128)S(1)} %pad_maximum_fusion.4), channel_id=1, source_target_pairs={{0,1},{1,0},{2,3},{3,2},{4,5},{5,4},{6,7},{7,6},{8,9},{9,8},{10,11... | collective-permute-start | bytes 36872 | tf_op jit(solution)/shard_map/ppermute | solution.py:1003
  8.7 5.5 %collective-permute-start.3 = (f32[3,8,128]{2,1,0:T(8,128)S(1)}, f32[3,8,128]{2,1,0:T(8,128)S(1)}, u32[]{:S(2)}, u32[]{:S(2)}) collective-permute-start(f32[3,8,128]{2,1,0:T(8,128)S(1)} %pad_maximum_fusion.4), channel_id=1, source_target_pairs={{0,3},{1,2},{2,1},{3,0},{4,7},{5,6},{6,5},{7,4},{8,11},{9,10},{10,... | collective-permute-start | bytes 36872 | tf_op jit(solution)/shard_map/ppermute | solution.py:1003
  15.5 4.3 %collective-permute-start.4 = (f32[3,24,128]{2,1,0:T(8,128)S(1)}, f32[3,24,128]{2,1,0:T(8,128)S(1)}, u32[]{:S(2)}, u32[]{:S(2)}) collective-permute-start(f32[3,24,128]{2,1,0:T(8,128)S(1)} %get-tuple-element.135), channel_id=1, source_target_pairs={{0,28},{4,8},{8,4},{12,16},{16,12},{20,24},{24,20},{28,0},{1,29},{... | collective-permute-start | bytes 110600 | tf_op jit(solution)/shard_map/ppermute | solution.py:1003
  16.0 3.9 %collective-permute-start.5 = (f32[3,24,128]{2,1,0:T(8,128)S(1)}, f32[3,24,128]{2,1,0:T(8,128)S(1)}, u32[]{:S(2)}, u32[]{:S(2)}) collective-permute-start(f32[3,24,128]{2,1,0:T(8,128)S(1)} %get-tuple-element.136), channel_id=1, source_target_pairs={{0,4},{4,0},{8,12},{12,8},{16,20},{20,16},{24,28},{28,24},{1,5},{5... | collective-permute-start | bytes 110600 | tf_op jit(solution)/shard_map/ppermute | solution.py:1003
  19.9 4.4 %collective-permute-start.6 = (f32[3,24,128]{2,1,0:T(8,128)S(1)}, f32[3,24,128]{2,1,0:T(8,128)S(1)}, u32[]{:S(2)}, u32[]{:S(2)}) collective-permute-start(f32[3,24,128]{2,1,0:T(8,128)S(1)} %get-tuple-element.153), channel_id=1, source_target_pairs={{0,1},{1,0},{2,3},{3,2},{4,5},{5,4},{6,7},{7,6},{8,9},{9,8},{10,11... | collective-permute-start | bytes 110600 | tf_op jit(solution)/shard_map/ppermute | solution.py:1003
  20.0 5.8 %collective-permute-start.7 = (f32[3,24,128]{2,1,0:T(8,128)S(1)}, f32[3,24,128]{2,1,0:T(8,128)S(1)}, u32[]{:S(2)}, u32[]{:S(2)}) collective-permute-start(f32[3,24,128]{2,1,0:T(8,128)S(1)} %get-tuple-element.154), channel_id=1, source_target_pairs={{0,3},{1,2},{2,1},{3,0},{4,7},{5,6},{6,5},{7,4},{8,11},{9,10},{10,... | collective-permute-start | bytes 110600 | tf_op jit(solution)/shard_map/ppermute | solution.py:1003
  29.0 4.3 %collective-permute-start.8 = (f32[3,24,128]{2,1,0:T(8,128)S(1)}, f32[3,24,128]{2,1,0:T(8,128)S(1)}, u32[]{:S(2)}, u32[]{:S(2)}) collective-permute-start(f32[3,24,128]{2,1,0:T(8,128)S(1)} %get-tuple-element.178), channel_id=1, source_target_pairs={{0,28},{4,8},{8,4},{12,16},{16,12},{20,24},{24,20},{28,0},{1,29},{... | collective-permute-start | bytes 110600 | tf_op jit(solution)/shard_map/ppermute | solution.py:1003
  29.1 4.3 %collective-permute-start.9 = (f32[3,24,128]{2,1,0:T(8,128)S(1)}, f32[3,24,128]{2,1,0:T(8,128)S(1)}, u32[]{:S(2)}, u32[]{:S(2)}) collective-permute-start(f32[3,24,128]{2,1,0:T(8,128)S(1)} %get-tuple-element.179), channel_id=1, source_target_pairs={{0,4},{4,0},{8,12},{12,8},{16,20},{20,16},{24,28},{28,24},{1,5},{5... | collective-permute-start | bytes 110600 | tf_op jit(solution)/shard_map/ppermute | solution.py:1003
  33.4 4.0 %collective-permute-start.10 = (f32[3,24,128]{2,1,0:T(8,128)S(1)}, f32[3,24,128]{2,1,0:T(8,128)S(1)}, u32[]{:S(2)}, u32[]{:S(2)}) collective-permute-start(f32[3,24,128]{2,1,0:T(8,128)S(1)} %get-tuple-element.189), channel_id=1, source_target_pairs={{0,1},{1,0},{2,3},{3,2},{4,5},{5,4},{6,7},{7,6},{8,9},{9,8},{10,11... | collective-permute-start | bytes 110600 | tf_op jit(solution)/shard_map/ppermute | solution.py:1003
  33.6 5.8 %collective-permute-start.11 = (f32[3,24,128]{2,1,0:T(8,128)S(1)}, f32[3,24,128]{2,1,0:T(8,128)S(1)}, u32[]{:S(2)}, u32[]{:S(2)}) collective-permute-start(f32[3,24,128]{2,1,0:T(8,128)S(1)} %get-tuple-element.190), channel_id=1, source_target_pairs={{0,3},{1,2},{2,1},{3,0},{4,7},{5,6},{6,5},{7,4},{8,11},{9,10},{10,... | collective-permute-start | bytes 110600 | tf_op jit(solution)/shard_map/ppermute | solution.py:1003
  40.8 4.0 %collective-permute-start.12 = (f32[8,128]{1,0:T(8,128)S(1)}, f32[8,128]{1,0:T(8,128)S(1)}, u32[]{:S(2)}, u32[]{:S(2)}) collective-permute-start(f32[8,128]{1,0:T(8,128)S(1)} %get-tuple-element.198), channel_id=1, source_target_pairs={{0,28},{4,8},{8,4},{12,16},{16,12},{20,24},{24,20},{28,0},{1,29},{... | collective-permute-start | bytes 12296 | tf_op jit(solution)/shard_map/ppermute | solution.py:1003
  40.9 3.9 %collective-permute-start.13 = (f32[8,128]{1,0:T(8,128)S(1)}, f32[8,128]{1,0:T(8,128)S(1)}, u32[]{:S(2)}, u32[]{:S(2)}) collective-permute-start(f32[8,128]{1,0:T(8,128)S(1)} %get-tuple-element.198), channel_id=1, source_target_pairs={{0,4},{4,0},{8,12},{12,8},{16,20},{20,16},{24,28},{28,24},{1,5},{5... | collective-permute-start | bytes 12296 | tf_op jit(solution)/shard_map/ppermute | solution.py:1003
  44.8 3.7 %collective-permute-start.14 = (f32[3,8,128]{2,1,0:T(8,128)S(1)}, f32[3,8,128]{2,1,0:T(8,128)S(1)}, u32[]{:S(2)}, u32[]{:S(2)}) collective-permute-start(f32[3,8,128]{2,1,0:T(8,128)S(1)} %pad_maximum_fusion.5), channel_id=1, source_target_pairs={{0,1},{1,0},{2,3},{3,2},{4,5},{5,4},{6,7},{7,6},{8,9},{9,8},{10,11... | collective-permute-start | bytes 36872 | tf_op jit(solution)/shard_map/ppermute | solution.py:1003
  44.9 5.5 %collective-permute-start.15 = (f32[3,8,128]{2,1,0:T(8,128)S(1)}, f32[3,8,128]{2,1,0:T(8,128)S(1)}, u32[]{:S(2)}, u32[]{:S(2)}) collective-permute-start(f32[3,8,128]{2,1,0:T(8,128)S(1)} %pad_maximum_fusion.5), channel_id=1, source_target_pairs={{0,3},{1,2},{2,1},{3,0},{4,7},{5,6},{6,5},{7,4},{8,11},{9,10},{10,... | collective-permute-start | bytes 36872 | tf_op jit(solution)/shard_map/ppermute | solution.py:1003

commit v5 on v4

--- a/solution.py
+++ b/solution.py
@@ -580,17 +580,21 @@
         ref[part] = pack(gather_ref[place * GHOSTS : place * GHOSTS + GHOSTS, :])
 
 
-def make_features(block, col_ref, kinds, weight_ref, pre_ref, feat_high, feat_low, scalar_ref):
+def make_features(block, col_ref, kinds, weight_ref, pre_ref, feat_high, feat_low, scalar_ref, gate_ref):
     rows = block_rows(block)
     kind = col_ref[rows, 3:4].astype(jnp.int32)
     scalar = jnp.zeros((BLOCK, 128), F32)
     for species in range(kinds):
         scalar = jnp.where(kind == species, weight_ref[species : species + 1, :], scalar)
     pre = pre_ref[rows, 0:128]
-    scalar = scalar + pre * sigmoid(pre)
+    own_gate = sigmoid(pre)
+    scalar = scalar + pre * own_gate
     if scalar_ref is not None:
         scalar_ref[rows, :] = scalar
     gate = sigmoid(pre_ref[rows, 128:256])
+    if gate_ref is not None:
+        gate_ref[rows, 0:128] = own_gate
+        gate_ref[rows, 128:256] = gate
     parts = [scalar] + [pre_ref[rows, (a + 2) * 128 : (a + 3) * 128] * gate for a in range(3)]
     empty = jnp.zeros((BLOCK, 128), BF16)
     for order, part in enumerate(parts):
@@ -655,7 +659,9 @@
     pre_ref[...] = mm3(split(hist_ref[...]), (fold_high[...], fold_low[...]))
 
     def features(block, carried):
-        make_features(block, col_ref, kinds, weight_ref, pre_ref, feat_high, feat_low, scalar_ref)
+        make_features(
+            block, col_ref, kinds, weight_ref, pre_ref, feat_high, feat_low, scalar_ref, None
+        )
         return carried
 
     lax.fori_loop(0, blocks, features, 0)
@@ -735,11 +741,13 @@
     return hidden * hidden_gate * readout, pull_final, pull_message
 
 
-def pull_features(grad_feat, pre_ref):
+def pull_features(grad_feat, pre_ref, gate_ref=None):
     by_scalar = grad_feat[:, 0:128]
     pre = pre_ref[:, 0:128]
-    own_gate = sigmoid(pre)
-    gate = sigmoid(pre_ref[:, 128:256])
+    if gate_ref is None:
+        own_gate, gate = sigmoid(pre), sigmoid(pre_ref[:, 128:256])
+    else:
+        own_gate, gate = gate_ref[:, 0:128], gate_ref[:, 128:256]
     by_gate = jnp.zeros_like(gate)
     by_vector = []
     for a in range(3):
@@ -780,13 +788,16 @@
     message_ref,
     pre_ref,
     grad_feat,
+    gate_ref,
 ):
     even_x, even_y = parities(control_ref)
     fold = (fold_high[...], fold_low[...])
     ghost_hist = pick_all((even_x, even_y, mate_in, far_in, zmate_in, zfar_in))
     pre_ref[...] = mm3(split(ghost_hist), fold)
     for block in range(2):
-        make_features(block, ghost_col, kinds, weight_ref, pre_ref, feat_high, feat_low, None)
+        make_features(
+            block, ghost_col, kinds, weight_ref, pre_ref, feat_high, feat_low, None, gate_ref
+        )
     message_ref[...] = message_in[...]
 
     ghost_tiles(
@@ -809,7 +820,7 @@
         ),
     )
 
-    ghost_pull = mm3(split(pull_features(grad_feat, pre_ref)), fold, ROWROW)
+    ghost_pull = mm3(split(pull_features(grad_feat, pre_ref, gate_ref)), fold, ROWROW)
     put_packets(
         even_x,
         lambda slot: ghost_pull[slot * GHOSTS : slot * GHOSTS + GHOSTS],
@@ -1144,6 +1155,7 @@
             pltpu.VMEM((atoms, 128), F32),
             pltpu.VMEM((8 * GHOSTS, 640), F32),
             pltpu.VMEM((8 * GHOSTS, 512), F32),
+            pltpu.VMEM((8 * GHOSTS, 256), F32),
         ],
     )(
         control, *arrived, ghost_col, *fold, *mix, weights, scalar, message,

time: 51.7 us -> 52.3 us (1.012)
  waiting for transfers between devices: 15.7 us -> 19 us
  starting transfers between devices: 19.4 us -> 17 us
    ppermute x16, waiting for transfers between devices: 15.7 us -> 19 us  [swap(): return lax.ppermute(value, axis, partners(axis, far))]
    ppermute x16, starting transfers between devices: 19.4 us -> 17 us  [swap(): return lax.ppermute(value, axis, partners(axis, far))]
where the time goes in v5:
time: 52.3 us; the launch traced here: 52.2 us
  waiting for transfers between devices  19 us (36%)
  starting transfers between devices  17 us (33%)
  Pallas kernels  14.6 us (28%)
  between operations  1.47 us (3%)
    ppermute x16, waiting for transfers between devices, swap(): return lax.ppermute(value, axis, partners(axis, far))  19 us
    ppermute x16, starting transfers between devices, swap(): return lax.ppermute(value, axis, partners(axis, far))  17 us
    pallas_call x13, Pallas kernels, run(): return made(*placed)  14.6 us
  transfers between devices with their start and end apart: 16, of which 10 were waited for; matrix products, arithmetic and copies ran while one was open for 0% of the time, Pallas kernels for 13%

profile of v5, /device:TPU:0, one launch (start us, length us, event | category | flops | bytes accessed | tf_op | source)
XLA Modules:
  0.0 52.2 jit_solution(6780353097482263780)
XLA Ops:
  0.6 1.0 %shard_map.104 = (f32[8,512]{1,0:T(8,128)S(1)}, f32[8,128]{1,0:T(8,128)S(1)}, s32[8,16]{1,0:T(8,128)S(1)}, s32[8,128]{1,0:T(8,128)S(1)}) custom-call(f32[3,512]{1,0:T(4,128)} %frac_in.1, s32[1,512]{1,0:T(1,128)} %bitcast.21, s32[8,16]{1,0:T(8,128)} %send_in.1, s32[2,6]{1,0:T(2,128)} %tile_in.1), custom_call_target="tpu_custom_call" | custom-call | tf_op jit(solution)/shard_map/pallas_call | solution.py:1062
  1.6 3.4 %collective-permute-start = (f32[8,128]{1,0:T(8,128)S(1)}, f32[8,128]{1,0:T(8,128)S(1)}, u32[]{:S(2)}, u32[]{:S(2)}) collective-permute-start(f32[8,128]{1,0:T(8,128)S(1)} %get-tuple-element.111), channel_id=1, source_target_pairs={{0,28},{4,8},{8,4},{12,16},{16,12},{20,24},{24,20},{28,0},{1,29},{... | collective-permute-start | bytes 12296 | tf_op jit(solution)/shard_map/ppermute | solution.py:1014
  5.0 0.0 collective-permute-start.1
  5.7 0.1 add_bitcast_fusion.words_ref
  5.8 1.2 %shard_map.105 = (s32[8,128]{1,0:T(8,128)S(1)}, f32[512,128]{1,0:T(8,128)S(1)}, f32[8,8,128]{2,1,0:T(8,128)S(1)}, bf16[512,128]{1,0:T(8,128)(2,1)S(1)}, f32[48,1...) custom-call(s32[1,3]{1,0:T(1,128)S(1)} %add_bitcast_fusion.words_ref, s32[8,128]{1,0:T(8,128)S(1)} %get-tuple-element.114.tiles_ref, ...), custom_call_target="tpu_custom_call" | custom-call | tf_op jit(solution)/shard_map/pallas_call | solution.py:1062
  7.0 0.0 collective-permute-done.far_in
  7.0 0.0 collective-permute-done.1.mate_in
  7.0 1.7 %collective-permute-start.2 = (f32[3,8,128]{2,1,0:T(8,128)S(1)}, f32[3,8,128]{2,1,0:T(8,128)S(1)}, u32[]{:S(2)}, u32[]{:S(2)}) collective-permute-start(f32[3,8,128]{2,1,0:T(8,128)S(1)} %pad_maximum_fusion.4), channel_id=1, source_target_pairs={{0,1},{1,0},{2,3},{3,2},{4,5},{5,4},{6,7},{7,6},{8,9},{9,8},{10,11... | collective-permute-start | bytes 36872 | tf_op jit(solution)/shard_map/ppermute | solution.py:1014
  8.7 2.5 %collective-permute-start.3 = (f32[3,8,128]{2,1,0:T(8,128)S(1)}, f32[3,8,128]{2,1,0:T(8,128)S(1)}, u32[]{:S(2)}, u32[]{:S(2)}) collective-permute-start(f32[3,8,128]{2,1,0:T(8,128)S(1)} %pad_maximum_fusion.4), channel_id=1, source_target_pairs={{0,3},{1,2},{2,1},{3,0},{4,7},{5,6},{6,5},{7,4},{8,11},{9,10},{10,... | collective-permute-start | bytes 36872 | tf_op jit(solution)/shard_map/ppermute | solution.py:1014
  11.2 0.1 shard_map.106
  11.3 0.0 collective-permute-done.2.zmate_in
  11.3 2.9 %collective-permute-done.3.zfar_in = f32[3,8,128]{2,1,0:T(8,128)S(1)} collective-permute-done((f32[3,8,128]{2,1,0:T(8,128)S(1)}, f32[3,8,128]{2,1,0:T(8,128)S(1)}, u32[]{:S(2)}, u32[]{:S(2)}) %collective-permute-start.3) | collective-permute-done | bytes 12320 | tf_op jit(solution)/shard_map/ppermute | solution.py:1014
  14.2 1.3 %shard_map.107 = (f32[512,256]{1,0:T(8,128)S(1)}, f32[3,24,128]{2,1,0:T(8,128)S(1)}, f32[3,24,128]{2,1,0:T(8,128)S(1)}, f32[2,24,128]{2,1,0:T(8,128)S(1)}, f32[1...) custom-call(s32[8,128]{1,0:T(8,128)S(1)} %get-tuple-element.123.cont, ...), custom_call_target="tpu_custom_call" | custom-call | tf_op jit(solution)/shard_map/pallas_call | solution.py:1062
  15.5 0.5 collective-permute-start.4
  16.0 0.9 %collective-permute-start.5 = (f32[3,24,128]{2,1,0:T(8,128)S(1)}, f32[3,24,128]{2,1,0:T(8,128)S(1)}, u32[]{:S(2)}, u32[]{:S(2)}) collective-permute-start(f32[3,24,128]{2,1,0:T(8,128)S(1)} %get-tuple-element.136), channel_id=1, source_target_pairs={{0,4},{4,0},{8,12},{12,8},{16,20},{20,16},{24,28},{28,24},{1,5},{5... | collective-permute-start | bytes 110600 | tf_op jit(solution)/shard_map/ppermute | solution.py:1014
  16.9 2.0 %shard_map.108 = (f32[512,640]{1,0:T(8,128)S(1)}, bf16[8,256,256]{2,1,0:T(8,128)(2,1)S(1)}, bf16[8,256,256]{2,1,0:T(8,128)(2,1)S(1)}, f32[512,128]{1,0:T(8,128)S...) custom-call(f32[512,256]{1,0:T(8,128)S(1)} %get-tuple-element.139.hi, ...), custom_call_target="tpu_custom_call" | custom-call | tf_op jit(solution)/shard_map/pallas_call | solution.py:1062
  18.9 0.9 %collective-permute-done.4.far_in = f32[3,24,128]{2,1,0:T(8,128)S(1)} collective-permute-done((f32[3,24,128]{2,1,0:T(8,128)S(1)}, f32[3,24,128]{2,1,0:T(8,128)S(1)}, u32[]{:S(2)}, u32[]{:S(2)}) %collective-permute-start.4) | collective-permute-done | bytes 36896 | tf_op jit(solution)/shard_map/ppermute | solution.py:1014
  19.9 0.0 collective-permute-done.5.mate_in
  19.9 0.1 collective-permute-start.6
  20.0 2.5 %collective-permute-start.7 = (f32[3,24,128]{2,1,0:T(8,128)S(1)}, f32[3,24,128]{2,1,0:T(8,128)S(1)}, u32[]{:S(2)}, u32[]{:S(2)}) collective-permute-start(f32[3,24,128]{2,1,0:T(8,128)S(1)} %get-tuple-element.154), channel_id=1, source_target_pairs={{0,3},{1,2},{2,1},{3,0},{4,7},{5,6},{6,5},{7,4},{8,11},{9,10},{10,... | collective-permute-start | bytes 110600 | tf_op jit(solution)/shard_map/ppermute | solution.py:1014
  22.5 0.5 shard_map.109
  23.0 1.3 %collective-permute-done.6.zmate_in = f32[3,24,128]{2,1,0:T(8,128)S(1)} collective-permute-done((f32[3,24,128]{2,1,0:T(8,128)S(1)}, f32[3,24,128]{2,1,0:T(8,128)S(1)}, u32[]{:S(2)}, u32[]{:S(2)}) %collective-permute-start.6) | collective-permute-done | bytes 36896 | tf_op jit(solution)/shard_map/ppermute | solution.py:1014
  24.3 1.5 %collective-permute-done.7.zfar_in = f32[3,24,128]{2,1,0:T(8,128)S(1)} collective-permute-done((f32[3,24,128]{2,1,0:T(8,128)S(1)}, f32[3,24,128]{2,1,0:T(8,128)S(1)}, u32[]{:S(2)}, u32[]{:S(2)}) %collective-permute-start.7) | collective-permute-done | bytes 36896 | tf_op jit(solution)/shard_map/ppermute | solution.py:1014
  25.8 3.2 %shard_map.110 = (f32[3,24,128]{2,1,0:T(8,128)S(1)}, f32[3,24,128]{2,1,0:T(8,128)S(1)}, f32[2,24,128]{2,1,0:T(8,128)S(1)}, bf16[2,256,256]{2,1,0:T(8,128)(2,1)S(...) custom-call(s32[8,128]{1,0:T(8,128)S(1)} %get-tuple-element.123.cont, ...), custom_call_target="tpu_custom_call" | custom-call | tf_op jit(solution)/shard_map/pallas_call | solution.py:1062
  29.0 0.1 collective-permute-start.8
  29.1 1.0 %collective-permute-start.9 = (f32[3,24,128]{2,1,0:T(8,128)S(1)}, f32[3,24,128]{2,1,0:T(8,128)S(1)}, u32[]{:S(2)}, u32[]{:S(2)}) collective-permute-start(f32[3,24,128]{2,1,0:T(8,128)S(1)} %get-tuple-element.179), channel_id=1, source_target_pairs={{0,4},{4,0},{8,12},{12,8},{16,20},{20,16},{24,28},{28,24},{1,5},{5... | collective-permute-start | bytes 110600 | tf_op jit(solution)/shard_map/ppermute | solution.py:1014
  30.1 0.7 %shard_map.111.pull_in = f32[6,512,256]{2,1,0:T(8,128)S(1)} custom-call(s32[8,128]{1,0:T(8,128)S(1)} %get-tuple-element.123.control_ref, f32[48,128]{1,0:T(8,128)S(1)} %get-tuple-element.140.weight_ref, f32[512,128]{1,0:T(8,128)S(1)} %get-tuple-element.175.pull_message, bf16[2,256,256]{2,1,0:T(8,128)(2,1)S(1)} %get-tuple-element.182.ghost_high, ...), custom_call_target="tpu_custom_call" | custom-call | tf_op jit(solution)/shard_map/pallas_call | solution.py:1062
  30.8 2.6 %collective-permute-done.8.far_in = f32[3,24,128]{2,1,0:T(8,128)S(1)} collective-permute-done((f32[3,24,128]{2,1,0:T(8,128)S(1)}, f32[3,24,128]{2,1,0:T(8,128)S(1)}, u32[]{:S(2)}, u32[]{:S(2)}) %collective-permute-start.8) | collective-permute-done | bytes 36896 | tf_op jit(solution)/shard_map/ppermute | solution.py:1014
  33.3 0.0 collective-permute-done.9.mate_in
  33.4 1.1 %collective-permute-start.10 = (f32[3,24,128]{2,1,0:T(8,128)S(1)}, f32[3,24,128]{2,1,0:T(8,128)S(1)}, u32[]{:S(2)}, u32[]{:S(2)}) collective-permute-start(f32[3,24,128]{2,1,0:T(8,128)S(1)} %get-tuple-element.189), channel_id=1, source_target_pairs={{0,1},{1,0},{2,3},{3,2},{4,5},{5,4},{6,7},{7,6},{8,9},{9,8},{10,11... | collective-permute-start | bytes 110600 | tf_op jit(solution)/shard_map/ppermute | solution.py:1014
  34.5 1.5 %collective-permute-start.11 = (f32[3,24,128]{2,1,0:T(8,128)S(1)}, f32[3,24,128]{2,1,0:T(8,128)S(1)}, u32[]{:S(2)}, u32[]{:S(2)}) collective-permute-start(f32[3,24,128]{2,1,0:T(8,128)S(1)} %get-tuple-element.190), channel_id=1, source_target_pairs={{0,3},{1,2},{2,1},{3,0},{4,7},{5,6},{6,5},{7,4},{8,11},{9,10},{10,... | collective-permute-start | bytes 110600 | tf_op jit(solution)/shard_map/ppermute | solution.py:1014
  36.1 1.1 %shard_map.112.pull_hist_ref = f32[512,256]{1,0:T(8,128)S(1)} custom-call(s32[8,128]{1,0:T(8,128)S(1)} %get-tuple-element.123.control_ref, f32[512,128]{1,0:T(8,128)S(1)} %get-tuple-element.124.col_ref, f32[8,8,128]{2,1,0:T(8,128)S(1)} %get-tuple-element.125.row_ref, bf16[256,640]{1,0:T(8,128)(2,1)S(1)} %get-tuple-element.158.fold_high, ...), custom_call_target="tpu_custom_call" | custom-call | tf_op jit(solution)/shard_map/pallas_call | solution.py:1062
  37.1 0.3 collective-permute-done.10.zmate_in
  37.4 2.9 %collective-permute-done.11.zfar_in = f32[3,24,128]{2,1,0:T(8,128)S(1)} collective-permute-done((f32[3,24,128]{2,1,0:T(8,128)S(1)}, f32[3,24,128]{2,1,0:T(8,128)S(1)}, u32[]{:S(2)}, u32[]{:S(2)}) %collective-permute-start.11) | collective-permute-done | bytes 36896 | tf_op jit(solution)/shard_map/ppermute | solution.py:1014
  40.3 1.4 %shard_map.113 = (f32[8,128]{1,0:T(8,128)S(1)}, f32[512,256]{1,0:T(8,128)S(1)}, f32[512,128]{1,0:T(8,128)S(1)}) custom-call(s32[8,128]{1,0:T(8,128)S(1)} %get-tuple-element.123.control_ref, bf16[512,128]{1,0:T(8,128)(2,1)S(1)} %get-tuple-element.173.chosen_ref, f32[512,256]{1,0:T(8,128)S(1)} %shard_map.112.pull_hist_ref, ...), custom_call_target="tpu_custom_call" | custom-call | tf_op jit(solution)/shard_map/pallas_call | solution.py:1062
  41.7 0.1 collective-permute-start.12
  41.8 0.1 collective-permute-start.13
  41.9 0.8 %shard_map.114 = (f32[6,512,256]{2,1,0:T(8,128)S(1)}, f32[1,512]{1,0:T(1,128)}) custom-call(s32[8,128]{1,0:T(8,128)S(1)} %get-tuple-element.123.control_ref, f32[48,128]{1,0:T(8,128)S(1)} %get-tuple-element.140.weight_ref, f32[512,128]{1,0:T(8,128)S(1)} %get-tuple-element.175.pull_message, f32[512,128]{1,0:T(8,128)S(1)} %get-tuple-element.201.share_ref, ...), custom_call_target="tpu_custom_call" | custom-call | tf_op jit(solution)/shard_map/pallas_call | solution.py:1062
  42.6 3.1 %collective-permute-done.12.far_in = f32[8,128]{1,0:T(8,128)S(1)} collective-permute-done((f32[8,128]{1,0:T(8,128)S(1)}, f32[8,128]{1,0:T(8,128)S(1)}, u32[]{:S(2)}, u32[]{:S(2)}) %collective-permute-start.12) | collective-permute-done | bytes 4128 | tf_op jit(solution)/shard_map/ppermute | solution.py:1014
  45.7 0.0 collective-permute-done.13.mate_in
  45.7 0.0 collective-permute-start.14
  45.7 1.6 %collective-permute-start.15 = (f32[3,8,128]{2,1,0:T(8,128)S(1)}, f32[3,8,128]{2,1,0:T(8,128)S(1)}, u32[]{:S(2)}, u32[]{:S(2)}) collective-permute-start(f32[3,8,128]{2,1,0:T(8,128)S(1)} %pad_maximum_fusion.5), channel_id=1, source_target_pairs={{0,3},{1,2},{2,1},{3,0},{4,7},{5,6},{6,5},{7,4},{8,11},{9,10},{10,... | collective-permute-start | bytes 36872 | tf_op jit(solution)/shard_map/ppermute | solution.py:1014
  47.3 0.2 shard_map.115
  47.6 1.8 %collective-permute-done.14.zmate_in = f32[3,8,128]{2,1,0:T(8,128)S(1)} collective-permute-done((f32[3,8,128]{2,1,0:T(8,128)S(1)}, f32[3,8,128]{2,1,0:T(8,128)S(1)}, u32[]{:S(2)}, u32[]{:S(2)}) %collective-permute-start.14) | collective-permute-done | bytes 12320 | tf_op jit(solution)/shard_map/ppermute | solution.py:1014
  49.4 1.9 %collective-permute-done.15.zfar_in = f32[3,8,128]{2,1,0:T(8,128)S(1)} collective-permute-done((f32[3,8,128]{2,1,0:T(8,128)S(1)}, f32[3,8,128]{2,1,0:T(8,128)S(1)}, u32[]{:S(2)}, u32[]{:S(2)}) %collective-permute-start.15) | collective-permute-done | bytes 12320 | tf_op jit(solution)/shard_map/ppermute | solution.py:1014
  51.3 0.9 %shard_map.116 = f32[3,512]{1,0:T(4,128)} custom-call(s32[8,128]{1,0:T(8,128)S(1)} %get-tuple-element.123.control_ref, bf16[128,512]{1,0:T(8,128)(2,1)S(1)} %get-tuple-element.208.turned_ref, f32[8,512]{1,0:T(8,128)S(1)} %get-tuple-element.209.own_ref, f32[8,128]{1,0:T(8,128)S(1)} %collective-permute-done.13.mate_in, ...), custom_call_target="tpu_custom_call" | custom-call | tf_op jit(solution)/shard_map/pallas_call | solution.py:1062
  (9 shorter events, 0.0 us)
Async XLA Ops:
  1.6 5.3 %collective-permute-start = (f32[8,128]{1,0:T(8,128)S(1)}, f32[8,128]{1,0:T(8,128)S(1)}, u32[]{:S(2)}, u32[]{:S(2)}) collective-permute-start(f32[8,128]{1,0:T(8,128)S(1)} %get-tuple-element.111), channel_id=1, source_target_pairs={{0,28},{4,8},{8,4},{12,16},{16,12},{20,24},{24,20},{28,0},{1,29},{... | collective-permute-start | bytes 12296 | tf_op jit(solution)/shard_map/ppermute | solution.py:1014
  5.0 2.0 %collective-permute-start.1 = (f32[8,128]{1,0:T(8,128)S(1)}, f32[8,128]{1,0:T(8,128)S(1)}, u32[]{:S(2)}, u32[]{:S(2)}) collective-permute-start(f32[8,128]{1,0:T(8,128)S(1)} %get-tuple-element.111), channel_id=1, source_target_pairs={{0,4},{4,0},{8,12},{12,8},{16,20},{20,16},{24,28},{28,24},{1,5},{5... | collective-permute-start | bytes 12296 | tf_op jit(solution)/shard_map/ppermute | solution.py:1014
  7.0 4.3 %collective-permute-start.2 = (f32[3,8,128]{2,1,0:T(8,128)S(1)}, f32[3,8,128]{2,1,0:T(8,128)S(1)}, u32[]{:S(2)}, u32[]{:S(2)}) collective-permute-start(f32[3,8,128]{2,1,0:T(8,128)S(1)} %pad_maximum_fusion.4), channel_id=1, source_target_pairs={{0,1},{1,0},{2,3},{3,2},{4,5},{5,4},{6,7},{7,6},{8,9},{9,8},{10,11... | collective-permute-start | bytes 36872 | tf_op jit(solution)/shard_map/ppermute | solution.py:1014
  8.7 5.5 %collective-permute-start.3 = (f32[3,8,128]{2,1,0:T(8,128)S(1)}, f32[3,8,128]{2,1,0:T(8,128)S(1)}, u32[]{:S(2)}, u32[]{:S(2)}) collective-permute-start(f32[3,8,128]{2,1,0:T(8,128)S(1)} %pad_maximum_fusion.4), channel_id=1, source_target_pairs={{0,3},{1,2},{2,1},{3,0},{4,7},{5,6},{6,5},{7,4},{8,11},{9,10},{10,... | collective-permute-start | bytes 36872 | tf_op jit(solution)/shard_map/ppermute | solution.py:1014
  15.5 4.3 %collective-permute-start.4 = (f32[3,24,128]{2,1,0:T(8,128)S(1)}, f32[3,24,128]{2,1,0:T(8,128)S(1)}, u32[]{:S(2)}, u32[]{:S(2)}) collective-permute-start(f32[3,24,128]{2,1,0:T(8,128)S(1)} %get-tuple-element.135), channel_id=1, source_target_pairs={{0,28},{4,8},{8,4},{12,16},{16,12},{20,24},{24,20},{28,0},{1,29},{... | collective-permute-start | bytes 110600 | tf_op jit(solution)/shard_map/ppermute | solution.py:1014
  16.0 3.9 %collective-permute-start.5 = (f32[3,24,128]{2,1,0:T(8,128)S(1)}, f32[3,24,128]{2,1,0:T(8,128)S(1)}, u32[]{:S(2)}, u32[]{:S(2)}) collective-permute-start(f32[3,24,128]{2,1,0:T(8,128)S(1)} %get-tuple-element.136), channel_id=1, source_target_pairs={{0,4},{4,0},{8,12},{12,8},{16,20},{20,16},{24,28},{28,24},{1,5},{5... | collective-permute-start | bytes 110600 | tf_op jit(solution)/shard_map/ppermute | solution.py:1014
  19.9 4.4 %collective-permute-start.6 = (f32[3,24,128]{2,1,0:T(8,128)S(1)}, f32[3,24,128]{2,1,0:T(8,128)S(1)}, u32[]{:S(2)}, u32[]{:S(2)}) collective-permute-start(f32[3,24,128]{2,1,0:T(8,128)S(1)} %get-tuple-element.153), channel_id=1, source_target_pairs={{0,1},{1,0},{2,3},{3,2},{4,5},{5,4},{6,7},{7,6},{8,9},{9,8},{10,11... | collective-permute-start | bytes 110600 | tf_op jit(solution)/shard_map/ppermute | solution.py:1014
  20.0 5.8 %collective-permute-start.7 = (f32[3,24,128]{2,1,0:T(8,128)S(1)}, f32[3,24,128]{2,1,0:T(8,128)S(1)}, u32[]{:S(2)}, u32[]{:S(2)}) collective-permute-start(f32[3,24,128]{2,1,0:T(8,128)S(1)} %get-tuple-element.154), channel_id=1, source_target_pairs={{0,3},{1,2},{2,1},{3,0},{4,7},{5,6},{6,5},{7,4},{8,11},{9,10},{10,... | collective-permute-start | bytes 110600 | tf_op jit(solution)/shard_map/ppermute | solution.py:1014
  29.0 4.3 %collective-permute-start.8 = (f32[3,24,128]{2,1,0:T(8,128)S(1)}, f32[3,24,128]{2,1,0:T(8,128)S(1)}, u32[]{:S(2)}, u32[]{:S(2)}) collective-permute-start(f32[3,24,128]{2,1,0:T(8,128)S(1)} %get-tuple-element.178), channel_id=1, source_target_pairs={{0,28},{4,8},{8,4},{12,16},{16,12},{20,24},{24,20},{28,0},{1,29},{... | collective-permute-start | bytes 110600 | tf_op jit(solution)/shard_map/ppermute | solution.py:1014
  29.1 4.3 %collective-permute-start.9 = (f32[3,24,128]{2,1,0:T(8,128)S(1)}, f32[3,24,128]{2,1,0:T(8,128)S(1)}, u32[]{:S(2)}, u32[]{:S(2)}) collective-permute-start(f32[3,24,128]{2,1,0:T(8,128)S(1)} %get-tuple-element.179), channel_id=1, source_target_pairs={{0,4},{4,0},{8,12},{12,8},{16,20},{20,16},{24,28},{28,24},{1,5},{5... | collective-permute-start | bytes 110600 | tf_op jit(solution)/shard_map/ppermute | solution.py:1014
  33.4 4.0 %collective-permute-start.10 = (f32[3,24,128]{2,1,0:T(8,128)S(1)}, f32[3,24,128]{2,1,0:T(8,128)S(1)}, u32[]{:S(2)}, u32[]{:S(2)}) collective-permute-start(f32[3,24,128]{2,1,0:T(8,128)S(1)} %get-tuple-element.189), channel_id=1, source_target_pairs={{0,1},{1,0},{2,3},{3,2},{4,5},{5,4},{6,7},{7,6},{8,9},{9,8},{10,11... | collective-permute-start | bytes 110600 | tf_op jit(solution)/shard_map/ppermute | solution.py:1014
  34.5 5.8 %collective-permute-start.11 = (f32[3,24,128]{2,1,0:T(8,128)S(1)}, f32[3,24,128]{2,1,0:T(8,128)S(1)}, u32[]{:S(2)}, u32[]{:S(2)}) collective-permute-start(f32[3,24,128]{2,1,0:T(8,128)S(1)} %get-tuple-element.190), channel_id=1, source_target_pairs={{0,3},{1,2},{2,1},{3,0},{4,7},{5,6},{6,5},{7,4},{8,11},{9,10},{10,... | collective-permute-start | bytes 110600 | tf_op jit(solution)/shard_map/ppermute | solution.py:1014
  41.7 4.0 %collective-permute-start.12 = (f32[8,128]{1,0:T(8,128)S(1)}, f32[8,128]{1,0:T(8,128)S(1)}, u32[]{:S(2)}, u32[]{:S(2)}) collective-permute-start(f32[8,128]{1,0:T(8,128)S(1)} %get-tuple-element.198), channel_id=1, source_target_pairs={{0,28},{4,8},{8,4},{12,16},{16,12},{20,24},{24,20},{28,0},{1,29},{... | collective-permute-start | bytes 12296 | tf_op jit(solution)/shard_map/ppermute | solution.py:1014
  41.8 3.9 %collective-permute-start.13 = (f32[8,128]{1,0:T(8,128)S(1)}, f32[8,128]{1,0:T(8,128)S(1)}, u32[]{:S(2)}, u32[]{:S(2)}) collective-permute-start(f32[8,128]{1,0:T(8,128)S(1)} %get-tuple-element.198), channel_id=1, source_target_pairs={{0,4},{4,0},{8,12},{12,8},{16,20},{20,16},{24,28},{28,24},{1,5},{5... | collective-permute-start | bytes 12296 | tf_op jit(solution)/shard_map/ppermute | solution.py:1014
  45.7 3.7 %collective-permute-start.14 = (f32[3,8,128]{2,1,0:T(8,128)S(1)}, f32[3,8,128]{2,1,0:T(8,128)S(1)}, u32[]{:S(2)}, u32[]{:S(2)}) collective-permute-start(f32[3,8,128]{2,1,0:T(8,128)S(1)} %pad_maximum_fusion.5), channel_id=1, source_target_pairs={{0,1},{1,0},{2,3},{3,2},{4,5},{5,4},{6,7},{7,6},{8,9},{9,8},{10,11... | collective-permute-start | bytes 36872 | tf_op jit(solution)/shard_map/ppermute | solution.py:1014
  45.7 5.6 %collective-permute-start.15 = (f32[3,8,128]{2,1,0:T(8,128)S(1)}, f32[3,8,128]{2,1,0:T(8,128)S(1)}, u32[]{:S(2)}, u32[]{:S(2)}) collective-permute-start(f32[3,8,128]{2,1,0:T(8,128)S(1)} %pad_maximum_fusion.5), channel_id=1, source_target_pairs={{0,3},{1,2},{2,1},{3,0},{4,7},{5,6},{6,5},{7,4},{8,11},{9,10},{10,... | collective-permute-start | bytes 36872 | tf_op jit(solution)/shard_map/ppermute | solution.py:1014

commit v6 on v4

--- a/solution.py
+++ b/solution.py
@@ -22,7 +22,7 @@
 STEP = ROOT * 0.6
 MIDDLE = 1.0 + 0.6 * (BASIS - 1) / 2
 REACH = 5.125
-ROWS = 32
+ROWS = 64
 
 VMEM = pl.BlockSpec(memory_space=pltpu.VMEM)
 HBM = pl.BlockSpec(memory_space=pltpu.HBM)

time: 51.7 us -> 51.9 us (level); the launches traced: 51.3 us -> 52 us
  waiting for transfers between devices: 15.7 us -> 12.7 us
  Pallas kernels: 14.5 us -> 17.4 us
  starting transfers between devices: 19.4 us -> 20.3 us
    ppermute x16, waiting for transfers between devices: 15.7 us -> 12.7 us  [swap(): return lax.ppermute(value, axis, partners(axis, far))]
    pallas_call x13, Pallas kernels: 14.5 us -> 17.4 us  [run(): return made(*placed)]
    ppermute x16, starting transfers between devices: 19.4 us -> 20.3 us  [swap(): return lax.ppermute(value, axis, partners(axis, far))]
  transfers between devices with their start and end apart: 16 -> 16, of which waited for: 10 -> 8; matrix products, arithmetic and copies ran while one was open for 0% -> 0% of each run, Pallas kernels for 13% -> 18%
where the time goes in v6:
time: 51.9 us; the launch traced here: 52 us
  starting transfers between devices  20.3 us (39%)
  Pallas kernels  17.4 us (34%)
  waiting for transfers between devices  12.7 us (24%)
  between operations  1.47 us (3%)
    ppermute x16, starting transfers between devices, swap(): return lax.ppermute(value, axis, partners(axis, far))  20.3 us
    pallas_call x13, Pallas kernels, run(): return made(*placed)  17.4 us
    ppermute x16, waiting for transfers between devices, swap(): return lax.ppermute(value, axis, partners(axis, far))  12.7 us
  transfers between devices with their start and end apart: 16, of which 8 were waited for; matrix products, arithmetic and copies ran while one was open for 0% of the time, Pallas kernels for 18%

profile of v6, /device:TPU:0, one launch (start us, length us, event | category | flops | bytes accessed | tf_op | source)
XLA Modules:
  0.0 52.0 jit_solution(2546252296325032494)
XLA Ops:
  0.6 1.0 %shard_map.104 = (f32[8,512]{1,0:T(8,128)S(1)}, f32[8,128]{1,0:T(8,128)S(1)}, s32[8,16]{1,0:T(8,128)S(1)}, s32[8,128]{1,0:T(8,128)S(1)}) custom-call(f32[3,512]{1,0:T(4,128)} %frac_in.1, s32[1,512]{1,0:T(1,128)} %bitcast.21, s32[8,16]{1,0:T(8,128)} %send_in.1, s32[2,6]{1,0:T(2,128)} %tile_in.1), custom_call_target="tpu_custom_call" | custom-call | tf_op jit(solution)/shard_map/pallas_call | solution.py:1051
  1.6 3.4 %collective-permute-start = (f32[8,128]{1,0:T(8,128)S(1)}, f32[8,128]{1,0:T(8,128)S(1)}, u32[]{:S(2)}, u32[]{:S(2)}) collective-permute-start(f32[8,128]{1,0:T(8,128)S(1)} %get-tuple-element.111), channel_id=1, source_target_pairs={{0,28},{4,8},{8,4},{12,16},{16,12},{20,24},{24,20},{28,0},{1,29},{... | collective-permute-start | bytes 12296 | tf_op jit(solution)/shard_map/ppermute | solution.py:1003
  5.0 0.0 collective-permute-start.1
  5.7 0.1 add_bitcast_fusion.words_ref
  5.8 1.2 %shard_map.105 = (s32[8,128]{1,0:T(8,128)S(1)}, f32[512,128]{1,0:T(8,128)S(1)}, f32[8,8,128]{2,1,0:T(8,128)S(1)}, bf16[512,128]{1,0:T(8,128)(2,1)S(1)}, f32[48,1...) custom-call(s32[1,3]{1,0:T(1,128)S(1)} %add_bitcast_fusion.words_ref, s32[8,128]{1,0:T(8,128)S(1)} %get-tuple-element.114.tiles_ref, ...), custom_call_target="tpu_custom_call" | custom-call | tf_op jit(solution)/shard_map/pallas_call | solution.py:1051
  7.0 0.0 collective-permute-done.far_in
  7.0 0.0 collective-permute-done.1.mate_in
  7.0 1.7 %collective-permute-start.2 = (f32[3,8,128]{2,1,0:T(8,128)S(1)}, f32[3,8,128]{2,1,0:T(8,128)S(1)}, u32[]{:S(2)}, u32[]{:S(2)}) collective-permute-start(f32[3,8,128]{2,1,0:T(8,128)S(1)} %pad_maximum_fusion.4), channel_id=1, source_target_pairs={{0,1},{1,0},{2,3},{3,2},{4,5},{5,4},{6,7},{7,6},{8,9},{9,8},{10,11... | collective-permute-start | bytes 36872 | tf_op jit(solution)/shard_map/ppermute | solution.py:1003
  8.7 2.5 %collective-permute-start.3 = (f32[3,8,128]{2,1,0:T(8,128)S(1)}, f32[3,8,128]{2,1,0:T(8,128)S(1)}, u32[]{:S(2)}, u32[]{:S(2)}) collective-permute-start(f32[3,8,128]{2,1,0:T(8,128)S(1)} %pad_maximum_fusion.4), channel_id=1, source_target_pairs={{0,3},{1,2},{2,1},{3,0},{4,7},{5,6},{6,5},{7,4},{8,11},{9,10},{10,... | collective-permute-start | bytes 36872 | tf_op jit(solution)/shard_map/ppermute | solution.py:1003
  11.2 0.7 %shard_map.106 = (f32[512,256]{1,0:T(8,128)S(1)}, bf16[6,512,256]{2,1,0:T(8,128)(2,1)S(1)}, bf16[6,512,256]{2,1,0:T(8,128)(2,1)S(1)}) custom-call(s32[8,128]{1,0:T(8,128)S(1)} %get-tuple-element.123.control_ref, f32[512,128]{1,0:T(8,128)S(1)} %get-tuple-element.124.col_ref, f32[8,8,128]{2,1,0:T(8,128)S(1)} %get-tuple-element.125.row_ref), custom_call_target="tpu_custom_call" | custom-call | tf_op jit(solution)/shard_map/pallas_call | solution.py:1051
  11.9 0.0 collective-permute-done.2.zmate_in
  11.9 2.3 %collective-permute-done.3.zfar_in = f32[3,8,128]{2,1,0:T(8,128)S(1)} collective-permute-done((f32[3,8,128]{2,1,0:T(8,128)S(1)}, f32[3,8,128]{2,1,0:T(8,128)S(1)}, u32[]{:S(2)}, u32[]{:S(2)}) %collective-permute-start.3) | collective-permute-done | bytes 12320 | tf_op jit(solution)/shard_map/ppermute | solution.py:1003
  14.2 1.3 %shard_map.107 = (f32[512,256]{1,0:T(8,128)S(1)}, f32[3,24,128]{2,1,0:T(8,128)S(1)}, f32[3,24,128]{2,1,0:T(8,128)S(1)}, f32[2,24,128]{2,1,0:T(8,128)S(1)}, f32[1...) custom-call(s32[8,128]{1,0:T(8,128)S(1)} %get-tuple-element.123.cont, ...), custom_call_target="tpu_custom_call" | custom-call | tf_op jit(solution)/shard_map/pallas_call | solution.py:1051
  15.5 0.5 collective-permute-start.4
  16.0 0.9 %collective-permute-start.5 = (f32[3,24,128]{2,1,0:T(8,128)S(1)}, f32[3,24,128]{2,1,0:T(8,128)S(1)}, u32[]{:S(2)}, u32[]{:S(2)}) collective-permute-start(f32[3,24,128]{2,1,0:T(8,128)S(1)} %get-tuple-element.136), channel_id=1, source_target_pairs={{0,4},{4,0},{8,12},{12,8},{16,20},{20,16},{24,28},{28,24},{1,5},{5... | collective-permute-start | bytes 110600 | tf_op jit(solution)/shard_map/ppermute | solution.py:1003
  16.9 2.0 %shard_map.108 = (f32[512,640]{1,0:T(8,128)S(1)}, bf16[8,256,256]{2,1,0:T(8,128)(2,1)S(1)}, bf16[8,256,256]{2,1,0:T(8,128)(2,1)S(1)}, f32[512,128]{1,0:T(8,128)S...) custom-call(f32[512,256]{1,0:T(8,128)S(1)} %get-tuple-element.139.hi, ...), custom_call_target="tpu_custom_call" | custom-call | tf_op jit(solution)/shard_map/pallas_call | solution.py:1051
  18.9 0.9 %collective-permute-done.4.far_in = f32[3,24,128]{2,1,0:T(8,128)S(1)} collective-permute-done((f32[3,24,128]{2,1,0:T(8,128)S(1)}, f32[3,24,128]{2,1,0:T(8,128)S(1)}, u32[]{:S(2)}, u32[]{:S(2)}) %collective-permute-start.4) | collective-permute-done | bytes 36896 | tf_op jit(solution)/shard_map/ppermute | solution.py:1003
  19.9 0.0 collective-permute-done.5.mate_in
  19.9 0.1 collective-permute-start.6
  20.0 2.9 %collective-permute-start.7 = (f32[3,24,128]{2,1,0:T(8,128)S(1)}, f32[3,24,128]{2,1,0:T(8,128)S(1)}, u32[]{:S(2)}, u32[]{:S(2)}) collective-permute-start(f32[3,24,128]{2,1,0:T(8,128)S(1)} %get-tuple-element.154), channel_id=1, source_target_pairs={{0,3},{1,2},{2,1},{3,0},{4,7},{5,6},{6,5},{7,4},{8,11},{9,10},{10,... | collective-permute-start | bytes 110600 | tf_op jit(solution)/shard_map/ppermute | solution.py:1003
  22.9 1.0 %shard_map.109 = (f32[512,128]{1,0:T(8,128)S(1)}, bf16[6,256,512]{2,1,0:T(8,128)(2,1)S(1)}, bf16[6,256,512]{2,1,0:T(8,128)(2,1)S(1)}) custom-call(s32[8,128]{1,0:T(8,128)S(1)} %get-tuple-element.123.control_ref, f32[8,8,128]{2,1,0:T(8,128)S(1)} %get-tuple-element.125.row_ref, f32[128,128]{1,0:T(8,128)S(1)} %get-tuple-element.157.ghost_col, ...), custom_call_target="tpu_custom_call" | custom-call | tf_op jit(solution)/shard_map/pallas_call | solution.py:1051
  23.9 0.4 collective-permute-done.6.zmate_in
  24.3 1.5 %collective-permute-done.7.zfar_in = f32[3,24,128]{2,1,0:T(8,128)S(1)} collective-permute-done((f32[3,24,128]{2,1,0:T(8,128)S(1)}, f32[3,24,128]{2,1,0:T(8,128)S(1)}, u32[]{:S(2)}, u32[]{:S(2)}) %collective-permute-start.7) | collective-permute-done | bytes 36896 | tf_op jit(solution)/shard_map/ppermute | solution.py:1003
  25.8 3.2 %shard_map.110 = (f32[3,24,128]{2,1,0:T(8,128)S(1)}, f32[3,24,128]{2,1,0:T(8,128)S(1)}, f32[2,24,128]{2,1,0:T(8,128)S(1)}, bf16[2,256,256]{2,1,0:T(8,128)(2,1)S(...) custom-call(s32[8,128]{1,0:T(8,128)S(1)} %get-tuple-element.123.cont, ...), custom_call_target="tpu_custom_call" | custom-call | tf_op jit(solution)/shard_map/pallas_call | solution.py:1051
  29.0 0.1 collective-permute-start.8
  29.1 1.0 %collective-permute-start.9 = (f32[3,24,128]{2,1,0:T(8,128)S(1)}, f32[3,24,128]{2,1,0:T(8,128)S(1)}, u32[]{:S(2)}, u32[]{:S(2)}) collective-permute-start(f32[3,24,128]{2,1,0:T(8,128)S(1)} %get-tuple-element.179), channel_id=1, source_target_pairs={{0,4},{4,0},{8,12},{12,8},{16,20},{20,16},{24,28},{28,24},{1,5},{5... | collective-permute-start | bytes 110600 | tf_op jit(solution)/shard_map/ppermute | solution.py:1003
  30.1 0.7 %shard_map.111.pull_in = f32[6,512,256]{2,1,0:T(8,128)S(1)} custom-call(s32[8,128]{1,0:T(8,128)S(1)} %get-tuple-element.123.control_ref, f32[48,128]{1,0:T(8,128)S(1)} %get-tuple-element.140.weight_ref, f32[512,128]{1,0:T(8,128)S(1)} %get-tuple-element.175.pull_message, bf16[2,256,256]{2,1,0:T(8,128)(2,1)S(1)} %get-tuple-element.182.ghost_high, ...), custom_call_target="tpu_custom_call" | custom-call | tf_op jit(solution)/shard_map/pallas_call | solution.py:1051
  30.8 2.5 %collective-permute-done.8.far_in = f32[3,24,128]{2,1,0:T(8,128)S(1)} collective-permute-done((f32[3,24,128]{2,1,0:T(8,128)S(1)}, f32[3,24,128]{2,1,0:T(8,128)S(1)}, u32[]{:S(2)}, u32[]{:S(2)}) %collective-permute-start.8) | collective-permute-done | bytes 36896 | tf_op jit(solution)/shard_map/ppermute | solution.py:1003
  33.3 0.0 collective-permute-done.9.mate_in
  33.4 0.2 collective-permute-start.10
  33.6 3.2 %collective-permute-start.11 = (f32[3,24,128]{2,1,0:T(8,128)S(1)}, f32[3,24,128]{2,1,0:T(8,128)S(1)}, u32[]{:S(2)}, u32[]{:S(2)}) collective-permute-start(f32[3,24,128]{2,1,0:T(8,128)S(1)} %get-tuple-element.190), channel_id=1, source_target_pairs={{0,3},{1,2},{2,1},{3,0},{4,7},{5,6},{6,5},{7,4},{8,11},{9,10},{10,... | collective-permute-start | bytes 110600 | tf_op jit(solution)/shard_map/ppermute | solution.py:1003
  36.8 1.7 %shard_map.112.pull_hist_ref = f32[512,256]{1,0:T(8,128)S(1)} custom-call(s32[8,128]{1,0:T(8,128)S(1)} %get-tuple-element.123.control_ref, f32[512,128]{1,0:T(8,128)S(1)} %get-tuple-element.124.col_ref, f32[8,8,128]{2,1,0:T(8,128)S(1)} %get-tuple-element.125.row_ref, bf16[256,640]{1,0:T(8,128)(2,1)S(1)} %get-tuple-element.158.fold_high, ...), custom_call_target="tpu_custom_call" | custom-call | tf_op jit(solution)/shard_map/pallas_call | solution.py:1051
  38.5 0.0 collective-permute-done.10.zmate_in
  38.5 0.9 %collective-permute-done.11.zfar_in = f32[3,24,128]{2,1,0:T(8,128)S(1)} collective-permute-done((f32[3,24,128]{2,1,0:T(8,128)S(1)}, f32[3,24,128]{2,1,0:T(8,128)S(1)}, u32[]{:S(2)}, u32[]{:S(2)}) %collective-permute-start.11) | collective-permute-done | bytes 36896 | tf_op jit(solution)/shard_map/ppermute | solution.py:1003
  39.4 1.4 %shard_map.113 = (f32[8,128]{1,0:T(8,128)S(1)}, f32[512,256]{1,0:T(8,128)S(1)}, f32[512,128]{1,0:T(8,128)S(1)}) custom-call(s32[8,128]{1,0:T(8,128)S(1)} %get-tuple-element.123.control_ref, bf16[512,128]{1,0:T(8,128)(2,1)S(1)} %get-tuple-element.173.chosen_ref, f32[512,256]{1,0:T(8,128)S(1)} %shard_map.112.pull_hist_ref, ...), custom_call_target="tpu_custom_call" | custom-call | tf_op jit(solution)/shard_map/pallas_call | solution.py:1051
  40.9 0.1 collective-permute-start.12
  40.9 0.5 collective-permute-start.13
  41.4 1.3 %shard_map.114 = (f32[6,512,256]{2,1,0:T(8,128)S(1)}, f32[1,512]{1,0:T(1,128)}) custom-call(s32[8,128]{1,0:T(8,128)S(1)} %get-tuple-element.123.control_ref, f32[48,128]{1,0:T(8,128)S(1)} %get-tuple-element.140.weight_ref, f32[512,128]{1,0:T(8,128)S(1)} %get-tuple-element.175.pull_message, f32[512,128]{1,0:T(8,128)S(1)} %get-tuple-element.201.share_ref, ...), custom_call_target="tpu_custom_call" | custom-call | tf_op jit(solution)/shard_map/pallas_call | solution.py:1051
  42.7 2.2 %collective-permute-done.12.far_in = f32[8,128]{1,0:T(8,128)S(1)} collective-permute-done((f32[8,128]{1,0:T(8,128)S(1)}, f32[8,128]{1,0:T(8,128)S(1)}, u32[]{:S(2)}, u32[]{:S(2)}) %collective-permute-start.12) | collective-permute-done | bytes 4128 | tf_op jit(solution)/shard_map/ppermute | solution.py:1003
  44.9 0.0 collective-permute-done.13.mate_in
  44.9 0.8 %collective-permute-start.14 = (f32[3,8,128]{2,1,0:T(8,128)S(1)}, f32[3,8,128]{2,1,0:T(8,128)S(1)}, u32[]{:S(2)}, u32[]{:S(2)}) collective-permute-start(f32[3,8,128]{2,1,0:T(8,128)S(1)} %pad_maximum_fusion.5), channel_id=1, source_target_pairs={{0,1},{1,0},{2,3},{3,2},{4,5},{5,4},{6,7},{7,6},{8,9},{9,8},{10,11... | collective-permute-start | bytes 36872 | tf_op jit(solution)/shard_map/ppermute | solution.py:1003
  45.6 2.6 %collective-permute-start.15 = (f32[3,8,128]{2,1,0:T(8,128)S(1)}, f32[3,8,128]{2,1,0:T(8,128)S(1)}, u32[]{:S(2)}, u32[]{:S(2)}) collective-permute-start(f32[3,8,128]{2,1,0:T(8,128)S(1)} %pad_maximum_fusion.5), channel_id=1, source_target_pairs={{0,3},{1,2},{2,1},{3,0},{4,7},{5,6},{6,5},{7,4},{8,11},{9,10},{10,... | collective-permute-start | bytes 36872 | tf_op jit(solution)/shard_map/ppermute | solution.py:1003
  48.3 0.9 %shard_map.115 = (f32[8,512]{1,0:T(8,128)S(1)}, bf16[128,512]{1,0:T(8,128)(2,1)S(1)}) custom-call(s32[8,128]{1,0:T(8,128)S(1)} %get-tuple-element.123.control_ref, bf16[512,128]{1,0:T(8,128)(2,1)S(1)} %get-tuple-element.173.chosen_ref, f32[512,256]{1,0:T(8,128)S(1)} %get-tuple-element.205.total_ref, f32[512,128]{1,0:T(8,128)S(1)} %get-tuple-element.124.col_ref, ...), custom_call_target="tpu_custom_call" | custom-call | tf_op jit(solution)/shard_map/pallas_call | solution.py:1051
  49.1 0.0 collective-permute-done.14.zmate_in
  49.2 2.0 %collective-permute-done.15.zfar_in = f32[3,8,128]{2,1,0:T(8,128)S(1)} collective-permute-done((f32[3,8,128]{2,1,0:T(8,128)S(1)}, f32[3,8,128]{2,1,0:T(8,128)S(1)}, u32[]{:S(2)}, u32[]{:S(2)}) %collective-permute-start.15) | collective-permute-done | bytes 12320 | tf_op jit(solution)/shard_map/ppermute | solution.py:1003
  51.1 0.9 %shard_map.116 = f32[3,512]{1,0:T(4,128)} custom-call(s32[8,128]{1,0:T(8,128)S(1)} %get-tuple-element.123.control_ref, bf16[128,512]{1,0:T(8,128)(2,1)S(1)} %get-tuple-element.208.turned_ref, f32[8,512]{1,0:T(8,128)S(1)} %get-tuple-element.209.own_ref, f32[8,128]{1,0:T(8,128)S(1)} %collective-permute-done.13.mate_in, ...), custom_call_target="tpu_custom_call" | custom-call | tf_op jit(solution)/shard_map/pallas_call | solution.py:1051
  (9 shorter events, 0.0 us)
Async XLA Ops:
  1.6 5.3 %collective-permute-start = (f32[8,128]{1,0:T(8,128)S(1)}, f32[8,128]{1,0:T(8,128)S(1)}, u32[]{:S(2)}, u32[]{:S(2)}) collective-permute-start(f32[8,128]{1,0:T(8,128)S(1)} %get-tuple-element.111), channel_id=1, source_target_pairs={{0,28},{4,8},{8,4},{12,16},{16,12},{20,24},{24,20},{28,0},{1,29},{... | collective-permute-start | bytes 12296 | tf_op jit(solution)/shard_map/ppermute | solution.py:1003
  5.0 2.0 %collective-permute-start.1 = (f32[8,128]{1,0:T(8,128)S(1)}, f32[8,128]{1,0:T(8,128)S(1)}, u32[]{:S(2)}, u32[]{:S(2)}) collective-permute-start(f32[8,128]{1,0:T(8,128)S(1)} %get-tuple-element.111), channel_id=1, source_target_pairs={{0,4},{4,0},{8,12},{12,8},{16,20},{20,16},{24,28},{28,24},{1,5},{5... | collective-permute-start | bytes 12296 | tf_op jit(solution)/shard_map/ppermute | solution.py:1003
  7.0 4.9 %collective-permute-start.2 = (f32[3,8,128]{2,1,0:T(8,128)S(1)}, f32[3,8,128]{2,1,0:T(8,128)S(1)}, u32[]{:S(2)}, u32[]{:S(2)}) collective-permute-start(f32[3,8,128]{2,1,0:T(8,128)S(1)} %pad_maximum_fusion.4), channel_id=1, source_target_pairs={{0,1},{1,0},{2,3},{3,2},{4,5},{5,4},{6,7},{7,6},{8,9},{9,8},{10,11... | collective-permute-start | bytes 36872 | tf_op jit(solution)/shard_map/ppermute | solution.py:1003
  8.7 5.5 %collective-permute-start.3 = (f32[3,8,128]{2,1,0:T(8,128)S(1)}, f32[3,8,128]{2,1,0:T(8,128)S(1)}, u32[]{:S(2)}, u32[]{:S(2)}) collective-permute-start(f32[3,8,128]{2,1,0:T(8,128)S(1)} %pad_maximum_fusion.4), channel_id=1, source_target_pairs={{0,3},{1,2},{2,1},{3,0},{4,7},{5,6},{6,5},{7,4},{8,11},{9,10},{10,... | collective-permute-start | bytes 36872 | tf_op jit(solution)/shard_map/ppermute | solution.py:1003
  15.5 4.3 %collective-permute-start.4 = (f32[3,24,128]{2,1,0:T(8,128)S(1)}, f32[3,24,128]{2,1,0:T(8,128)S(1)}, u32[]{:S(2)}, u32[]{:S(2)}) collective-permute-start(f32[3,24,128]{2,1,0:T(8,128)S(1)} %get-tuple-element.135), channel_id=1, source_target_pairs={{0,28},{4,8},{8,4},{12,16},{16,12},{20,24},{24,20},{28,0},{1,29},{... | collective-permute-start | bytes 110600 | tf_op jit(solution)/shard_map/ppermute | solution.py:1003
  16.0 3.9 %collective-permute-start.5 = (f32[3,24,128]{2,1,0:T(8,128)S(1)}, f32[3,24,128]{2,1,0:T(8,128)S(1)}, u32[]{:S(2)}, u32[]{:S(2)}) collective-permute-start(f32[3,24,128]{2,1,0:T(8,128)S(1)} %get-tuple-element.136), channel_id=1, source_target_pairs={{0,4},{4,0},{8,12},{12,8},{16,20},{20,16},{24,28},{28,24},{1,5},{5... | collective-permute-start | bytes 110600 | tf_op jit(solution)/shard_map/ppermute | solution.py:1003
  19.9 4.4 %collective-permute-start.6 = (f32[3,24,128]{2,1,0:T(8,128)S(1)}, f32[3,24,128]{2,1,0:T(8,128)S(1)}, u32[]{:S(2)}, u32[]{:S(2)}) collective-permute-start(f32[3,24,128]{2,1,0:T(8,128)S(1)} %get-tuple-element.153), channel_id=1, source_target_pairs={{0,1},{1,0},{2,3},{3,2},{4,5},{5,4},{6,7},{7,6},{8,9},{9,8},{10,11... | collective-permute-start | bytes 110600 | tf_op jit(solution)/shard_map/ppermute | solution.py:1003
  20.0 5.8 %collective-permute-start.7 = (f32[3,24,128]{2,1,0:T(8,128)S(1)}, f32[3,24,128]{2,1,0:T(8,128)S(1)}, u32[]{:S(2)}, u32[]{:S(2)}) collective-permute-start(f32[3,24,128]{2,1,0:T(8,128)S(1)} %get-tuple-element.154), channel_id=1, source_target_pairs={{0,3},{1,2},{2,1},{3,0},{4,7},{5,6},{6,5},{7,4},{8,11},{9,10},{10,... | collective-permute-start | bytes 110600 | tf_op jit(solution)/shard_map/ppermute | solution.py:1003
  29.0 4.3 %collective-permute-start.8 = (f32[3,24,128]{2,1,0:T(8,128)S(1)}, f32[3,24,128]{2,1,0:T(8,128)S(1)}, u32[]{:S(2)}, u32[]{:S(2)}) collective-permute-start(f32[3,24,128]{2,1,0:T(8,128)S(1)} %get-tuple-element.178), channel_id=1, source_target_pairs={{0,28},{4,8},{8,4},{12,16},{16,12},{20,24},{24,20},{28,0},{1,29},{... | collective-permute-start | bytes 110600 | tf_op jit(solution)/shard_map/ppermute | solution.py:1003
  29.1 4.3 %collective-permute-start.9 = (f32[3,24,128]{2,1,0:T(8,128)S(1)}, f32[3,24,128]{2,1,0:T(8,128)S(1)}, u32[]{:S(2)}, u32[]{:S(2)}) collective-permute-start(f32[3,24,128]{2,1,0:T(8,128)S(1)} %get-tuple-element.179), channel_id=1, source_target_pairs={{0,4},{4,0},{8,12},{12,8},{16,20},{20,16},{24,28},{28,24},{1,5},{5... | collective-permute-start | bytes 110600 | tf_op jit(solution)/shard_map/ppermute | solution.py:1003
  33.4 5.2 %collective-permute-start.10 = (f32[3,24,128]{2,1,0:T(8,128)S(1)}, f32[3,24,128]{2,1,0:T(8,128)S(1)}, u32[]{:S(2)}, u32[]{:S(2)}) collective-permute-start(f32[3,24,128]{2,1,0:T(8,128)S(1)} %get-tuple-element.189), channel_id=1, source_target_pairs={{0,1},{1,0},{2,3},{3,2},{4,5},{5,4},{6,7},{7,6},{8,9},{9,8},{10,11... | collective-permute-start | bytes 110600 | tf_op jit(solution)/shard_map/ppermute | solution.py:1003
  33.6 5.9 %collective-permute-start.11 = (f32[3,24,128]{2,1,0:T(8,128)S(1)}, f32[3,24,128]{2,1,0:T(8,128)S(1)}, u32[]{:S(2)}, u32[]{:S(2)}) collective-permute-start(f32[3,24,128]{2,1,0:T(8,128)S(1)} %get-tuple-element.190), channel_id=1, source_target_pairs={{0,3},{1,2},{2,1},{3,0},{4,7},{5,6},{6,5},{7,4},{8,11},{9,10},{10,... | collective-permute-start | bytes 110600 | tf_op jit(solution)/shard_map/ppermute | solution.py:1003
  40.9 4.0 %collective-permute-start.12 = (f32[8,128]{1,0:T(8,128)S(1)}, f32[8,128]{1,0:T(8,128)S(1)}, u32[]{:S(2)}, u32[]{:S(2)}) collective-permute-start(f32[8,128]{1,0:T(8,128)S(1)} %get-tuple-element.198), channel_id=1, source_target_pairs={{0,28},{4,8},{8,4},{12,16},{16,12},{20,24},{24,20},{28,0},{1,29},{... | collective-permute-start | bytes 12296 | tf_op jit(solution)/shard_map/ppermute | solution.py:1003
  40.9 3.9 %collective-permute-start.13 = (f32[8,128]{1,0:T(8,128)S(1)}, f32[8,128]{1,0:T(8,128)S(1)}, u32[]{:S(2)}, u32[]{:S(2)}) collective-permute-start(f32[8,128]{1,0:T(8,128)S(1)} %get-tuple-element.198), channel_id=1, source_target_pairs={{0,4},{4,0},{8,12},{12,8},{16,20},{20,16},{24,28},{28,24},{1,5},{5... | collective-permute-start | bytes 12296 | tf_op jit(solution)/shard_map/ppermute | solution.py:1003
  44.9 4.3 %collective-permute-start.14 = (f32[3,8,128]{2,1,0:T(8,128)S(1)}, f32[3,8,128]{2,1,0:T(8,128)S(1)}, u32[]{:S(2)}, u32[]{:S(2)}) collective-permute-start(f32[3,8,128]{2,1,0:T(8,128)S(1)} %pad_maximum_fusion.5), channel_id=1, source_target_pairs={{0,1},{1,0},{2,3},{3,2},{4,5},{5,4},{6,7},{7,6},{8,9},{9,8},{10,11... | collective-permute-start | bytes 36872 | tf_op jit(solution)/shard_map/ppermute | solution.py:1003
  45.6 5.5 %collective-permute-start.15 = (f32[3,8,128]{2,1,0:T(8,128)S(1)}, f32[3,8,128]{2,1,0:T(8,128)S(1)}, u32[]{:S(2)}, u32[]{:S(2)}) collective-permute-start(f32[3,8,128]{2,1,0:T(8,128)S(1)} %pad_maximum_fusion.5), channel_id=1, source_target_pairs={{0,3},{1,2},{2,1},{3,0},{4,7},{5,6},{6,5},{7,4},{8,11},{9,10},{10,... | collective-permute-start | bytes 36872 | tf_op jit(solution)/shard_map/ppermute | solution.py:1003
